TPU v7x, 32 devices: a whole 2x2x4 slice. The times are simulated.
32 devices in a mesh: dp: 4 (over z), tensor: 8 (over y, x, core).
Axes of the slice: x: 2, y: 2, z: 4, core: 2. Of those that a mesh axis runs over, the one named last changes fastest.
Arguments:
- inputs: bfloat16 [4096, 1024], P('dp'), may hold values from -6 to 6
- conditioning: bfloat16 [4, 1024], P('dp'), may hold values from -6 to 6
- cotangent: bfloat16 [4096, 1024], P('dp'), may hold values from -6 to 6
- w_ada: float32 [1024, 6144], P('dp', 'tensor'), may hold values from -0.1875 to 0.1875
- w_qkv: float32 [1024, 3072], P('dp', 'tensor'), may hold values from -0.1875 to 0.1875
- w_proj: float32 [1024, 1024], P('tensor', 'dp'), may hold values from -1 to 1
- w_fc1: float32 [1024, 4096], P('dp', 'tensor'), may hold values from -0.1875 to 0.1875
- w_fc2: float32 [4096, 1024], P('tensor', 'dp'), may hold values from -0.09375 to 0.09375
- col_bias: float32 [12288], P(('tensor', 'dp')), may hold values from -1.2 to 1.2
- row_bias: float32 [2, 1024], P(None, 'dp'), may hold values from -1.2 to 1.2
- m_ada: float32 [1024, 6144], P('dp', 'tensor'), may hold values from -20 to 20
- v_ada: float32 [1024, 6144], P('dp', 'tensor'), may hold values from 30.72 to 307.2
- m_qkv: float32 [1024, 3072], P('dp', 'tensor'), may hold values from -40 to 40
- v_qkv: float32 [1024, 3072], P('dp', 'tensor'), may hold values from 122.88 to 1228.8
- m_proj: float32 [1024, 1024], P('tensor', 'dp'), may hold values from -4 to 4
- v_proj: float32 [1024, 1024], P('tensor', 'dp'), may hold values from 1.2288 to 12.288
- m_fc1: float32 [1024, 4096], P('dp', 'tensor'), may hold values from -20 to 20
- v_fc1: float32 [1024, 4096], P('dp', 'tensor'), may hold values from 30.72 to 307.2
- m_fc2: float32 [4096, 1024], P('tensor', 'dp'), may hold values from -20 to 20
- v_fc2: float32 [4096, 1024], P('tensor', 'dp'), may hold values from 30.72 to 307.2
- m_col: float32 [12288], P(('tensor', 'dp')), may hold values from -32 to 32
- v_col: float32 [12288], P(('tensor', 'dp')), may hold values from 60.2112 to 602.112
- m_row: float32 [2, 1024], P(None, 'dp'), may hold values from -32 to 32
- v_row: float32 [2, 1024], P(None, 'dp'), may hold values from 60.2112 to 602.112
Outputs:
- block_out: float32 [4096, 1024], P(('dp', 'tensor'))
- input_grad: float32 [4096, 1024], P(('dp', 'tensor'))
- cond_grad: float32 [4, 1024], P('dp', 'tensor')
- ada_grad: float32 [1024, 6144], P('dp', 'tensor')
- ada_second: float32 [1024, 6144], P('dp', 'tensor')
- ada_new: float32 [1024, 6144], P('dp', 'tensor')
- qkv_grad: float32 [1024, 3072], P('dp', 'tensor')
- qkv_second: float32 [1024, 3072], P('dp', 'tensor')
- qkv_new: float32 [1024, 3072], P('dp', 'tensor')
- proj_grad: float32 [1024, 1024], P('tensor', 'dp')
- proj_second: float32 [1024, 1024], P('tensor', 'dp')
- proj_new: float32 [1024, 1024], P('tensor', 'dp')
- fc1_grad: float32 [1024, 4096], P('dp', 'tensor')
- fc1_second: float32 [1024, 4096], P('dp', 'tensor')
- fc1_new: float32 [1024, 4096], P('dp', 'tensor')
- fc2_grad: float32 [4096, 1024], P('tensor', 'dp')
- fc2_second: float32 [4096, 1024], P('tensor', 'dp')
- fc2_new: float32 [4096, 1024], P('tensor', 'dp')
- col_grad: float32 [12288], P(('tensor', 'dp'))
- col_second: float32 [12288], P(('tensor', 'dp'))
- col_new: float32 [12288], P(('tensor', 'dp'))
- row_grad: float32 [2, 1024], P(None, 'dp')
- row_second: float32 [2, 1024], P(None, 'dp')
- row_new: float32 [2, 1024], P(None, 'dp')
All inputs are finite; a program needn't handle non-finite values.
Results may differ from a plain program's by a relative error of at most 0.02.
The roundings to bfloat16 on the way count: a program that leaves them out, or rounds other values in their place, can miss the bound.
Values may be sent and summed in bfloat16 or wider, within the bound.
No kernel may reach another device: no remote copies, remote signals or barrier semaphores. Data moves between devices by JAX's collectives and lax.ppermute only.
A program may use at most 128 MiB of HBM per device.

v0:
```python
import jax
import jax.numpy as jnp
from jax import lax
from jax.sharding import PartitionSpec as P

D = 1024
HD = 64
FF = 4096
STEP = 10


LN_EPS = 1e-06
GELU_C = 0.7978845608028654
GELU_K = 0.044715
BETA_ONE = 0.9
BETA_TWO = 0.95
ADAM_EPS = 1e-08
DECAY = 0.1
LR_SCALE = 2.0
LR_BIAS = 0.2
CONTRACT_ROWS = (((0,), (0,)), ((), ()))
CONTRACT_COLS = (((1,), (1,)), ((), ()))


def normalize(values):
    center = values - jnp.mean(values, -1, keepdims=True)
    inv_std = lax.rsqrt(jnp.mean(center * center, -1, keepdims=True) + LN_EPS)
    return (center * inv_std, inv_std)


def norm_back(grad_n, normed, inv_std):
    return inv_std * (
        grad_n
        - jnp.mean(grad_n, -1, keepdims=True)
        - normed * jnp.mean(grad_n * normed, -1, keepdims=True)
    )


def gelu_pair(values):
    inner = GELU_C * (values + GELU_K * values * values * values)
    tanh_val = jnp.tanh(inner)
    result = 0.5 * values * (1.0 + tanh_val)
    slope = 0.5 * (1.0 + tanh_val) + 0.5 * values * (1.0 - tanh_val * tanh_val) * GELU_C * (
        1.0 + 3.0 * GELU_K * values * values
    )
    return (result, slope)


def product_rows(left, right):
    return lax.dot_general(left, right, CONTRACT_ROWS, preferred_element_type=jnp.float32)


def product_cols(left, right):
    return lax.dot_general(left, right, CONTRACT_COLS, preferred_element_type=jnp.float32)


def row_sum(left, right, transposed):

    def term():
        if transposed:
            return product_cols(left, right)
        return jnp.dot(left, right, preferred_element_type=jnp.float32)

    return lax.psum_scatter(term(), "tensor", scatter_dimension=0, tiled=True)


def attend(block):
    queries, keyset, values = (block[0], block[1], block[2])
    scores = jnp.einsum("qe,ke->qk", queries, keyset, preferred_element_type=jnp.float32) * HD ** (
        -0.5
    )
    highest = jnp.max(scores, -1, keepdims=True)
    expon = jnp.exp(scores - highest)
    totals = jnp.sum(expon, -1, keepdims=True)
    attn_prob = (expon / totals).astype(jnp.bfloat16)
    output = jnp.dot(attn_prob, values, preferred_element_type=jnp.float32).astype(jnp.bfloat16)
    return (output, (highest + jnp.log(totals))[:, 0])


def attend_back(item):
    block, log_total, grad_out = item
    queries, keyset, values = (block[0], block[1], block[2])
    scale = HD ** (-0.5)
    scores = jnp.einsum("qe,ke->qk", queries, keyset, preferred_element_type=jnp.float32) * scale
    attn_prob = jnp.exp(scores - log_total[:, None])
    grad_prob = jnp.einsum("qe,ke->qk", grad_out, values, preferred_element_type=jnp.float32)
    weighted = jnp.sum(attn_prob * grad_prob, -1, keepdims=True)
    grad_score = (attn_prob * (grad_prob - weighted)).astype(jnp.bfloat16)
    grad_query = (
        jnp.einsum("qk,ke->qe", grad_score, keyset, preferred_element_type=jnp.float32) * scale
    )
    grad_key = (
        jnp.einsum("qk,qe->ke", grad_score, queries, preferred_element_type=jnp.float32) * scale
    )
    grad_value = jnp.einsum(
        "qk,qe->ke", attn_prob.astype(jnp.bfloat16), grad_out, preferred_element_type=jnp.float32
    )
    return jnp.stack([grad_query, grad_key, grad_value]).astype(jnp.bfloat16)


def adam_step(weight, first, second, grad, rate, decay):
    first_new = BETA_ONE * first + (1.0 - BETA_ONE) * grad
    second_new = BETA_TWO * second + (1.0 - BETA_TWO) * grad * grad
    fix_one = 1.0 - BETA_ONE**STEP
    fix_two = 1.0 - BETA_TWO**STEP
    step_dir = first_new / fix_one / (jnp.sqrt(second_new / fix_two) + ADAM_EPS)
    return (second_new, weight - rate * (step_dir + decay * weight))


def shards(
    inputs,
    conditioning,
    cotangent,
    w_ada,
    w_qkv,
    w_proj,
    w_fc1,
    w_fc2,
    col_bias,
    row_bias,
    m_ada,
    v_ada,
    m_qkv,
    v_qkv,
    m_proj,
    v_proj,
    m_fc1,
    v_fc1,
    m_fc2,
    v_fc2,
    m_col,
    v_col,
    m_row,
    v_row,
):
    gathered = (
        lax.all_gather(w_ada.astype(jnp.bfloat16), "dp", axis=0, tiled=True),
        lax.all_gather(w_qkv.astype(jnp.bfloat16), "dp", axis=0, tiled=True),
        lax.all_gather(w_proj.astype(jnp.bfloat16), "dp", axis=1, tiled=True),
        lax.all_gather(w_fc1.astype(jnp.bfloat16), "dp", axis=0, tiled=True),
        lax.all_gather(w_fc2.astype(jnp.bfloat16), "dp", axis=1, tiled=True),
        lax.all_gather(col_bias.astype(jnp.bfloat16), "dp", axis=0, tiled=True),
        lax.all_gather(row_bias.astype(jnp.bfloat16), "dp", axis=1, tiled=True),
    )
    ada_low, qkv_low, proj_low, up_low, down_low, column_low, rows_low = gathered
    tokens, width = inputs.shape
    latents = conditioning.shape[0]
    seq_len = tokens // latents
    tensor_count = lax.axis_size("tensor")
    shard_rows = tokens // tensor_count
    tensor_id = lax.axis_index("tensor")
    ada_cols = ada_low.shape[1]
    head_cols = proj_low.shape[0]
    heads_here = head_cols // HD
    bias_cols = column_low.astype(jnp.float32)
    bias_ada = bias_cols[:ada_cols]
    bias_query = bias_cols[ada_cols : ada_cols + head_cols]
    bias_value = bias_cols[ada_cols + head_cols : ada_cols + 2 * head_cols]
    bias_up = bias_cols[ada_cols + 2 * head_cols :]
    bias_proj = rows_low[0].astype(jnp.float32)
    bias_down = rows_low[1].astype(jnp.float32)
    cond_full = conditioning.astype(jnp.float32)
    silu_low = (cond_full * jax.nn.sigmoid(cond_full)).astype(jnp.bfloat16)
    mod_part = jnp.dot(silu_low, ada_low, preferred_element_type=jnp.float32) + bias_ada
    modulation = lax.all_gather(mod_part, "tensor", axis=1, tiled=True).reshape(latents, 6, width)
    latent_here = tensor_id * latents // tensor_count
    mod_here = lax.dynamic_index_in_dim(modulation, latent_here, 0, keepdims=False)
    row_start = tensor_id * shard_rows
    resid_all = inputs.astype(jnp.float32)
    normed1, inv_one = normalize(resid_all)
    mod_in1 = (
        (
            normed1.reshape(latents, seq_len, width) * (1.0 + modulation[:, None, 1])
            + modulation[:, None, 0]
        )
        .reshape(tokens, width)
        .astype(jnp.bfloat16)
    )
    bias_qkv = jnp.stack(
        [
            bias_query.reshape(heads_here, HD),
            jnp.zeros((heads_here, HD), jnp.float32),
            bias_value.reshape(heads_here, HD),
        ],
        axis=1,
    )
    qkv_act = (
        jnp.dot(mod_in1, qkv_low, preferred_element_type=jnp.float32).reshape(
            tokens, heads_here, 3, HD
        )
        + bias_qkv
    ).astype(jnp.bfloat16)
    pairs = (
        qkv_act.reshape(latents, seq_len, heads_here, 3, HD)
        .transpose(0, 2, 3, 1, 4)
        .reshape(latents * heads_here, 3, seq_len, HD)
    )
    attended_pairs, log_totals = lax.map(attend, pairs)
    attended = (
        attended_pairs.reshape(latents, heads_here, seq_len, HD)
        .transpose(0, 2, 1, 3)
        .reshape(tokens, head_cols)
    )
    branch1 = (
        lax.psum_scatter(
            jnp.dot(attended, proj_low, preferred_element_type=jnp.float32),
            "tensor",
            scatter_dimension=0,
            tiled=True,
        )
        + bias_proj
    )
    resid_rows = lax.dynamic_slice_in_dim(resid_all, row_start, shard_rows, 0)
    resid1 = resid_rows + mod_here[2] * branch1
    normed2, inv_two = normalize(resid1)
    mod_in2 = (normed2 * (1.0 + mod_here[4]) + mod_here[3]).astype(jnp.bfloat16)
    mod_in2_all = lax.all_gather(mod_in2, "tensor", axis=0, tiled=True)
    pre_act = jnp.dot(mod_in2_all, up_low, preferred_element_type=jnp.float32) + bias_up
    activ_full, slope = gelu_pair(pre_act)
    activ = activ_full.astype(jnp.bfloat16)
    branch2 = row_sum(activ, down_low, False) + bias_down
    block_out = resid1 + mod_here[5] * branch2
    grad_all = cotangent.astype(jnp.float32)
    grad_branch2 = (
        (grad_all.reshape(latents, seq_len, width) * modulation[:, None, 5])
        .reshape(tokens, width)
        .astype(jnp.bfloat16)
    )
    down_grad = product_rows(activ, grad_branch2)
    down_bias_grad = jnp.sum(grad_branch2, 0, dtype=jnp.float32)
    grad_pre = (product_cols(grad_branch2, down_low) * slope).astype(jnp.bfloat16)
    up_grad = product_rows(mod_in2_all, grad_pre)
    up_bias_grad = jnp.sum(grad_pre, 0, dtype=jnp.float32)
    grad_in2 = row_sum(grad_pre, up_low, True)
    grad_rows = lax.dynamic_slice_in_dim(grad_all, row_start, shard_rows, 0)
    grad_resid1 = grad_rows + norm_back(grad_in2 * (1.0 + mod_here[4]), normed2, inv_two)
    grad_branch1 = (mod_here[2] * grad_resid1).astype(jnp.bfloat16)
    grad_branch_all = lax.all_gather(grad_branch1, "tensor", axis=0, tiled=True)
    proj_grad = product_rows(attended, grad_branch_all)
    proj_bias_grad = jnp.sum(grad_branch_all, 0, dtype=jnp.float32)
    grad_attended = product_cols(grad_branch_all, proj_low).astype(jnp.bfloat16)
    grad_pairs_in = (
        grad_attended.reshape(latents, seq_len, heads_here, HD)
        .transpose(0, 2, 1, 3)
        .reshape(latents * heads_here, seq_len, HD)
    )
    grad_pairs = lax.map(attend_back, (pairs, log_totals, grad_pairs_in))
    grad_qkv_act = (
        grad_pairs.reshape(latents, heads_here, 3, seq_len, HD)
        .transpose(0, 3, 1, 2, 4)
        .reshape(tokens, 3 * head_cols)
    )
    qkv_grad = product_rows(mod_in1, grad_qkv_act)
    qkv_sums = jnp.sum(grad_qkv_act, 0, dtype=jnp.float32).reshape(heads_here, 3, HD)
    grad_in1 = row_sum(grad_qkv_act, qkv_low, True)
    normed1_rows = lax.dynamic_slice_in_dim(normed1, row_start, shard_rows, 0)
    inv_one_rows = lax.dynamic_slice_in_dim(inv_one, row_start, shard_rows, 0)
    input_grad = grad_resid1 + norm_back(grad_in1 * (1.0 + mod_here[1]), normed1_rows, inv_one_rows)
    mod_terms = jnp.concatenate(
        [
            jnp.sum(grad_in1, 0),
            jnp.sum(grad_in1 * normed1_rows, 0),
            jnp.sum(grad_resid1 * branch1, 0),
            jnp.sum(grad_in2, 0),
            jnp.sum(grad_in2 * normed2, 0),
            jnp.sum(grad_rows * branch2, 0),
        ]
    )
    placed = jnp.where(jnp.arange(latents)[:, None] == latent_here, mod_terms[None, :], 0.0)
    grad_mod = lax.psum_scatter(placed, "tensor", scatter_dimension=1, tiled=True).astype(
        jnp.bfloat16
    )
    ada_grad = product_rows(silu_low, grad_mod)
    ada_bias_grad = jnp.sum(grad_mod, 0, dtype=jnp.float32)
    grad_silu = lax.psum_scatter(
        product_cols(grad_mod, ada_low), "tensor", scatter_dimension=1, tiled=True
    )
    cond_cols = width // tensor_count
    cond_here = lax.dynamic_slice_in_dim(cond_full, tensor_id * cond_cols, cond_cols, 1)
    sig_here = jax.nn.sigmoid(cond_here)
    cond_grad = grad_silu * sig_here * (1.0 + cond_here * (1.0 - sig_here))
    col_grad_part = jnp.concatenate(
        [ada_bias_grad, qkv_sums[:, 0].reshape(-1), qkv_sums[:, 2].reshape(-1), up_bias_grad]
    )
    row_grad_part = jnp.stack([proj_bias_grad, down_bias_grad])
    summed = (
        lax.psum_scatter(ada_grad, "dp", scatter_dimension=0, tiled=True),
        lax.psum_scatter(qkv_grad, "dp", scatter_dimension=0, tiled=True),
        lax.psum_scatter(proj_grad, "dp", scatter_dimension=1, tiled=True),
        lax.psum_scatter(up_grad, "dp", scatter_dimension=0, tiled=True),
        lax.psum_scatter(down_grad, "dp", scatter_dimension=1, tiled=True),
        lax.psum_scatter(col_grad_part, "dp", scatter_dimension=0, tiled=True),
        lax.psum_scatter(row_grad_part, "dp", scatter_dimension=1, tiled=True),
    )
    ada_sum, qkv_sum, proj_sum, up_sum, down_sum, col_sum, row_sum_grad = summed
    ada_second, ada_new = adam_step(w_ada, m_ada, v_ada, ada_sum, LR_SCALE * D ** (-0.5), DECAY)
    qkv_second, qkv_new = adam_step(w_qkv, m_qkv, v_qkv, qkv_sum, LR_SCALE * D ** (-0.5), DECAY)
    proj_second, proj_new = adam_step(
        w_proj, m_proj, v_proj, proj_sum, LR_SCALE * (D // 32) ** (-0.5), DECAY
    )
    fc1_second, fc1_new = adam_step(w_fc1, m_fc1, v_fc1, up_sum, LR_SCALE * D ** (-0.5), DECAY)
    fc2_second, fc2_new = adam_step(w_fc2, m_fc2, v_fc2, down_sum, LR_SCALE * FF ** (-0.5), DECAY)
    col_second, col_new = adam_step(col_bias, m_col, v_col, col_sum, LR_BIAS, 0.0)
    row_second, row_new = adam_step(row_bias, m_row, v_row, row_sum_grad, LR_BIAS, 0.0)
    return (
        block_out,
        input_grad,
        cond_grad,
        ada_sum,
        ada_second,
        ada_new,
        qkv_sum,
        qkv_second,
        qkv_new,
        proj_sum,
        proj_second,
        proj_new,
        up_sum,
        fc1_second,
        fc1_new,
        down_sum,
        fc2_second,
        fc2_new,
        col_sum,
        col_second,
        col_new,
        row_sum_grad,
        row_second,
        row_new,
    )


def solution(mesh):
    return jax.shard_map(
        shards,
        mesh=mesh,
        in_specs=(
            P("dp", None),
            P("dp", None),
            P("dp", None),
            P("dp", "tensor"),
            P("dp", "tensor"),
            P("tensor", "dp"),
            P("dp", "tensor"),
            P("tensor", "dp"),
            P(("tensor", "dp")),
            P(None, "dp"),
            P("dp", "tensor"),
            P("dp", "tensor"),
            P("dp", "tensor"),
            P("dp", "tensor"),
            P("tensor", "dp"),
            P("tensor", "dp"),
            P("dp", "tensor"),
            P("dp", "tensor"),
            P("tensor", "dp"),
            P("tensor", "dp"),
            P(("tensor", "dp")),
            P(("tensor", "dp")),
            P(None, "dp"),
            P(None, "dp"),
        ),
        out_specs=(
            P(("dp", "tensor"), None),
            P(("dp", "tensor"), None),
            P("dp", "tensor"),
            P("dp", "tensor"),
            P("dp", "tensor"),
            P("dp", "tensor"),
            P("dp", "tensor"),
            P("dp", "tensor"),
            P("dp", "tensor"),
            P("tensor", "dp"),
            P("tensor", "dp"),
            P("tensor", "dp"),
            P("dp", "tensor"),
            P("dp", "tensor"),
            P("dp", "tensor"),
            P("tensor", "dp"),
            P("tensor", "dp"),
            P("tensor", "dp"),
            P(("tensor", "dp")),
            P(("tensor", "dp")),
            P(("tensor", "dp")),
            P(None, "dp"),
            P(None, "dp"),
            P(None, "dp"),
        ),
        check_vma=False,
    )
```

profile of v0, /device:TPU:0, one launch (start us, length us, event | category | flops | bytes accessed | tf_op | source)
XLA Modules:
  0.0 816.3 jit_solution(1681909372367903557)
XLA Ops:
  9.9 13.5 %all-gather.1 = bf16[4,1,384]{2,1,0:T(2,128)(2,1)S(1)} all-gather(bf16[1,1,384]{2,1,0:T(2,128)(2,1)S(1)} %reshape.380), channel_id=1, replica_groups=mesh['dp'=4,'tensor'=8] {'dp'}, dimensions={0}, use_global_device_ids=true | all-gather | bytes 3840 | tf_op jit(solution)/shard_map/all_gather | solution.py:142
  24.9 29.2 %all_gather.33 = bf16[1024,384]{1,0:T(8,128)(2,1)S(1)} all-gather(bf16[256,384]{1,0:T(8,128)(2,1)S(1)} %convert_element_type.111), channel_id=1, replica_groups=mesh['dp'=4,'tensor'=8] {'dp'}, dimensions={0}, use_global_device_ids=true | all-gather | bytes 983040 | tf_op jit(solution)/shard_map/all_gather | solution.py:138
  54.5 15.6 %all_gather.34 = bf16[128,1024]{1,0:T(8,128)(2,1)S(1)} all-gather(bf16[128,256]{1,0:T(8,128)(2,1)S(1)} %convert_element_type.113), channel_id=1, replica_groups=mesh['dp'=4,'tensor'=8] {'dp'}, dimensions={1}, use_global_device_ids=true | all-gather | bytes 327680 | tf_op jit(solution)/shard_map/all_gather | solution.py:139
  76.2 9.1 %all-gather.2 = f32[8,1,768]{2,1,0:T(1,128)S(1)} all-gather(f32[1,1,768]{2,1,0:T(1,128)S(1)} %reshape.382), channel_id=2, replica_groups=mesh['dp'=4,'tensor'=8] {'tensor'}, dimensions={0}, use_global_device_ids=true | all-gather | bytes 27648 | tf_op jit(solution)/shard_map/all_gather | solution.py:165
  85.4 3.7 fusion.45
  90.8 11.8 %while.22 = (s32[]{:T(128)}, bf16[2,1024,64]{1,2,0:T(8,128)(2,1)S(1)}, f32[2,1024]{1,0:T(2,128)S(1)}, bf16[2,3,1024,64]{3,2,1,0:T(8,128)(2,1)S(1)}, s32[]{:T(128)}, /*index=5*/s32[]{:T(128)}, s32[]{}, s32[]{}) while((s32[]{:T(128)}, bf16[2,1024,64]{1,2,0:T(8,128)(2,1)S(1)}, f32[2,1024]{1,0:T(2,128)S(1)}, ...), condition=%wide.region_5.6_spmd, body=%wide.region_2.5_spmd.sunk | while | flops 277937152 | bytes 30320788 | solution.py:198
  93.6 3.2 fusion.111
  99.5 3.2 fusion.111
  102.7 2.7 fusion.72
  107.2 4.0 convert_element_type.104
  111.3 10.2 %all_gather.35 = bf16[2,1024]{1,0:T(2,128)(2,1)S(1)} all-gather(bf16[2,256]{1,0:T(2,128)(2,1)S(1)} %convert_element_type.114), channel_id=1, replica_groups=mesh['dp'=4,'tensor'=8] {'dp'}, dimensions={1}, use_global_device_ids=true | all-gather | bytes 5120 | tf_op jit(solution)/shard_map/all_gather | solution.py:143
  121.5 34.7 %reduce-scatter.19.cloned.1.call-done = f32[128,1024]{1,0:T(8,128)} async-done(((f32[1024,1024]{1,0:T(8,128)}), f32[128,1024]{1,0:T(8,128)}) %reduce-scatter.19.cloned.1.call-update) | async-done | bytes 524304 | tf_op jit(solution)/shard_map/reduce_scatter | solution.py:205
  158.7 27.6 %all-gather.13.cloned.1.call-done = bf16[1024,512]{1,0:T(8,128)(2,1)} async-done(((bf16[256,512]{1,0:T(8,128)(2,1)}), bf16[1024,512]{1,0:T(8,128)(2,1)}) %all-gather.13.cloned.1.call-update) | async-done | bytes 1048592 | tf_op jit(solution)/shard_map/all_gather | solution.py:140
  186.4 29.9 %all-gather.11.cloned.1.call-done = bf16[1024,1024]{1,0:T(8,128)(2,1)} async-done(((bf16[128,1024]{1,0:T(8,128)(2,1)}), bf16[1024,1024]{1,0:T(8,128)(2,1)}) %all-gather.11.cloned.1.call-update) | async-done | bytes 2097168 | tf_op jit(solution)/shard_map/all_gather | solution.py:217
  216.3 3.2 fusion.73
  220.9 3.0 fusion.48
  223.9 44.0 %reduce-scatter.35.cloned.1.call-done = f32[512,256]{1,0:T(8,128)} async-done(((f32[512,1024]{1,0:T(8,128)}), f32[512,256]{1,0:T(8,128)}) %reduce-scatter.35.cloned.1.call-update) | async-done | bytes 524304 | tf_op jit(solution)/shard_map/reduce_scatter | solution.py:291
  267.9 2.8 multiply_subtract_fusion.1
  271.0 29.4 %all-gather.15.cloned.1.call-done = bf16[512,1024]{1,0:T(8,128)(2,1)} async-done(((bf16[512,256]{1,0:T(8,128)(2,1)}), bf16[512,1024]{1,0:T(8,128)(2,1)}) %all-gather.15.cloned.1.call-update) | async-done | bytes 1048592 | tf_op jit(solution)/shard_map/all_gather | solution.py:141
  300.4 5.1 convert_reduce_fusion.3
  306.5 3.2 fusion.74
  309.8 5.3 fusion.61
  315.2 4.3 convert_element_type.119
  319.5 40.1 %reduce-scatter.23.cloned.1.call-done = f32[128,1024]{1,0:T(8,128)} async-done(((f32[1024,1024]{1,0:T(8,128)}), f32[128,1024]{1,0:T(8,128)}) %reduce-scatter.23.cloned.1.call-update) | async-done | bytes 524304 | tf_op jit(solution)/shard_map/reduce_scatter | solution.py:64
  360.8 53.8 %reduce-scatter.21.cloned.1.call-done = f32[128,1024]{1,0:T(8,128)} async-done(((f32[1024,1024]{1,0:T(8,128)}), f32[128,1024]{1,0:T(8,128)}) %reduce-scatter.21.cloned.1.call-update) | async-done | bytes 524304 | tf_op jit(solution)/shard_map/reduce_scatter | solution.py:64
  414.6 2.6 multiply_reduce_fusion.5
  418.1 28.0 %all-gather.17.cloned.1.call-done = bf16[1024,1024]{1,0:T(8,128)(2,1)} async-done(((bf16[128,1024]{1,0:T(8,128)(2,1)}), bf16[1024,1024]{1,0:T(8,128)(2,1)}) %all-gather.17.cloned.1.call-update) | async-done | bytes 2097168 | tf_op jit(solution)/shard_map/all_gather | solution.py:238
  446.1 3.1 convolution_convert_fusion
  450.4 20.5 %while.23 = (s32[]{:T(128)}, bf16[2,3,1024,64]{2,3,1,0:T(8,128)(2,1)}, bf16[2,3,1024,64]{3,2,1,0:T(8,128)(2,1)S(1)}, f32[2,1024]{1,0:T(2,128)S(1)}, bf16[2,1024,...) while((s32[]{:T(128)}, bf16[2,3,1024,64]{2,3,1,0:T(8,128)(2,1)}, ...), condition=%wide.region_15.16_spmd, body=%wide.region_13.15_spmd.sunk | while | flops 685177856 | bytes 51280556 | solution.py:247
  450.4 2.6 fusion.116
  453.1 3.3 multiply_reduce_fusion.15
  460.7 2.6 fusion.116
  463.4 3.3 multiply_reduce_fusion.15
  471.0 4.4 fusion.75
  475.5 4.0 subtract_multiply_fusion
  479.5 47.4 %reduce-scatter.25.cloned.1.call-done = f32[128,1024]{1,0:T(8,128)} async-done(((f32[1024,1024]{1,0:T(8,128)}), f32[128,1024]{1,0:T(8,128)}) %reduce-scatter.25.cloned.1.call-update) | async-done | bytes 524304 | tf_op jit(solution)/shard_map/reduce_scatter | solution.py:64
  531.9 4.2 fusion.77
  541.5 3.0 fusion.76
  544.5 4.6 fusion.50
  549.5 27.6 %reduce-scatter.37.cloned.1.call-done = f32[768,1]{1,0:T(8,128)} async-done(((f32[6144,1]{1,0:T(8,128)}), f32[768,1]{1,0:T(8,128)}) %reduce-scatter.37.cloned.1.call-update) | async-done | bytes 3088
  583.5 40.1 %reduce-scatter.33.cloned.1.call-done = f32[256,512]{1,0:T(8,128)} async-done(((f32[1024,512]{1,0:T(8,128)}), f32[256,512]{1,0:T(8,128)}) %reduce-scatter.33.cloned.1.call-update) | async-done | bytes 524304 | tf_op jit(solution)/shard_map/reduce_scatter | solution.py:290
  627.6 19.4 %reduce-scatter.41.cloned.1.call-done = f32[256,2]{1,0:T(8,128)} async-done(((f32[1024,2]{1,0:T(8,128)}), f32[256,2]{1,0:T(8,128)}) %reduce-scatter.41.cloned.1.call-update) | async-done | bytes 2064
  648.7 21.7 %reduce-scatter.31.cloned.1.call-done = f32[128,256]{1,0:T(8,128)} async-done(((f32[128,1024]{1,0:T(8,128)}), f32[128,256]{1,0:T(8,128)}) %reduce-scatter.31.cloned.1.call-update) | async-done | bytes 131088 | tf_op jit(solution)/shard_map/reduce_scatter | solution.py:289
  672.1 34.6 %reduce-scatter.29.cloned.1.call-done = f32[256,384]{1,0:T(8,128)} async-done(((f32[1024,384]{1,0:T(8,128)}), f32[256,384]{1,0:T(8,128)}) %reduce-scatter.29.cloned.1.call-update) | async-done | bytes 393232 | tf_op jit(solution)/shard_map/reduce_scatter | solution.py:288
  711.0 9.9 %all-reduce = f32[1536]{0:T(1024)S(1)} all-reduce(f32[1536]{0:T(1024)S(1)} %pad_maximum_fusion), channel_id=14, replica_groups=mesh['dp'=4,'tensor'=8] {'dp'}, use_global_device_ids=true, to_apply=%region_34.35.clone | all-reduce | flops 1536 | bytes 12288
  721.6 22.0 %reduce-scatter.39.cloned.1.call-done = f32[128,1]{1,0:T(8,128)} async-done(((f32[1024,1]{1,0:T(8,128)}), f32[128,1]{1,0:T(8,128)}) %reduce-scatter.39.cloned.1.call-update) | async-done | bytes 528
  745.1 61.6 %reduce-scatter.27.cloned.1.call-done = f32[256,768]{1,0:T(8,128)} async-done(((f32[1024,768]{1,0:T(8,128)}), f32[256,768]{1,0:T(8,128)}) %reduce-scatter.27.cloned.1.call-update) | async-done | bytes 786448 | tf_op jit(solution)/shard_map/reduce_scatter | solution.py:287
  806.7 3.1 multiply_subtract_fusion
  (210 shorter events, 66.9 us)
Async XLA Ops:
  7.2 67.2 %all-gather.9.cloned.1.call-start = ((), (), s32[]{:S(2)}) async-start(), calls=%async_computation.12 | async-start | bytes 1966080 | tf_op jit(solution)/shard_map/all_gather | solution.py:137
  9.2 45.3 %copy-start.13 = (f32[128,256]{1,0:T(8,128)S(1)}, f32[128,256]{1,0:T(8,128)}, u32[]{:S(2)}) copy-start(f32[128,256]{1,0:T(8,128)} %param.33) | copy-start | bytes 393220
  9.2 147.0 %reduce-scatter.19.cloned.1.call-start = ((), (), s32[]{:S(2)}) async-start(), calls=%async_computation.13 | async-start | bytes 4718592 | tf_op jit(solution)/shard_map/reduce_scatter | solution.py:205
  70.1 32.6 %copy-start.5 = (bf16[128,1024]{1,0:T(8,128)(2,1)}, bf16[128,1024]{1,0:T(8,128)(2,1)S(1)}, u32[]{:S(2)}) copy-start(bf16[128,1024]{1,0:T(8,128)(2,1)S(1)} %all_gather.34) | copy-start | bytes 786436
  70.1 4.4 copy-start.21
  91.6 1.9 copy-start.1
  97.5 1.9 copy-start.1
  102.7 2.7 copy-start.10
  105.4 81.0 %all-gather.13.cloned.1.call-start = ((), (), s32[]{:S(2)}) async-start(), calls=%async_computation.15 | async-start | bytes 1310720 | tf_op jit(solution)/shard_map/all_gather | solution.py:140
  107.2 109.1 %all-gather.11.cloned.1.call-start = ((), (), s32[]{:S(2)}) async-start(), calls=%async_computation.14 | async-start | bytes 2359296 | tf_op jit(solution)/shard_map/all_gather | solution.py:217
  107.2 4.0 copy-start.23
  158.7 109.2 %reduce-scatter.35.cloned.1.call-start = ((), (), s32[]{:S(2)}) async-start(), calls=%async_computation.25 | async-start | bytes 2621440 | tf_op jit(solution)/shard_map/reduce_scatter | solution.py:291
  216.3 4.6 copy-start.2
  223.8 44.1 %copy-start.15 = (f32[512,256]{1,0:T(8,128)S(1)}, f32[512,256]{1,0:T(8,128)}, u32[]{:S(2)}) copy-start(f32[512,256]{1,0:T(8,128)} %param.35) | copy-start | bytes 1572868
  223.9 76.5 %all-gather.15.cloned.1.call-start = ((), (), s32[]{:S(2)}) async-start(), calls=%async_computation.16 | async-start | bytes 1310720 | tf_op jit(solution)/shard_map/all_gather | solution.py:141
  270.7 88.8 %reduce-scatter.23.cloned.1.call-start = ((), (), s32[]{:S(2)}) async-start(), calls=%async_computation.18 | async-start | bytes 4718592 | tf_op jit(solution)/shard_map/reduce_scatter | solution.py:64
  300.4 6.1 copy-start.29
  309.7 104.9 %reduce-scatter.21.cloned.1.call-start = ((), (), s32[]{:S(2)}) async-start(), calls=%async_computation.17 | async-start | bytes 4718592 | tf_op jit(solution)/shard_map/reduce_scatter | solution.py:64
  315.1 131.0 %all-gather.17.cloned.1.call-start = ((), (), s32[]{:S(2)}) async-start(), calls=%async_computation.19 | async-start | bytes 2359296 | tf_op jit(solution)/shard_map/all_gather | solution.py:238
  418.0 108.8 %reduce-scatter.25.cloned.1.call-start = ((), (), s32[]{:S(2)}) async-start(), calls=%async_computation.20 | async-start | bytes 4718592 | tf_op jit(solution)/shard_map/reduce_scatter | solution.py:64
  453.1 3.5 copy-start
  463.3 3.5 copy-start
  475.4 101.7 %reduce-scatter.37.cloned.1.call-start = ((), (), s32[]{:S(2)}) async-start(), calls=%async_computation.26 | async-start | bytes 3538944
  530.7 93.0 %reduce-scatter.33.cloned.1.call-start = ((), (), s32[]{:S(2)}) async-start(), calls=%async_computation.24 | async-start | bytes 2621440 | tf_op jit(solution)/shard_map/reduce_scatter | solution.py:290
  536.1 111.0 %reduce-scatter.41.cloned.1.call-start = ((), (), s32[]{:S(2)}) async-start(), calls=%async_computation.28 | async-start | bytes 655360
  538.2 3.3 copy-start.11
  541.4 128.9 %reduce-scatter.31.cloned.1.call-start = ((), (), s32[]{:S(2)}) async-start(), calls=%async_computation.23 | async-start | bytes 655360 | tf_op jit(solution)/shard_map/reduce_scatter | solution.py:289
  544.5 162.2 %reduce-scatter.29.cloned.1.call-start = ((), (), s32[]{:S(2)}) async-start(), calls=%async_computation.22 | async-start | bytes 1966080 | tf_op jit(solution)/shard_map/reduce_scatter | solution.py:288
  549.1 29.1 %copy-start.3 = (bf16[1024,768]{1,0:T(8,128)(2,1)S(1)}, bf16[1024,768]{1,0:T(8,128)(2,1)}, u32[]{:S(2)}) copy-start(bf16[1024,768]{1,0:T(8,128)(2,1)} %all-gather.9.cloned.1.call-done) | copy-start | bytes 4718596
  549.2 194.5 %reduce-scatter.39.cloned.1.call-start = ((), (), s32[]{:S(2)}) async-start(), calls=%async_computation.27 | async-start | bytes 589824
  579.6 227.1 %reduce-scatter.27.cloned.1.call-start = ((), (), s32[]{:S(2)}) async-start(), calls=%async_computation.21 | async-start | bytes 3932160 | tf_op jit(solution)/shard_map/reduce_scatter | solution.py:287
  581.6 42.0 %copy-start.8 = (f32[256,512]{1,0:T(8,128)S(1)}, f32[256,512]{1,0:T(8,128)}, u32[]{:S(2)}) copy-start(f32[256,512]{1,0:T(8,128)} %param.34) | copy-start | bytes 1572868
  581.6 42.0 %copy-start.16 = (f32[256,512]{1,0:T(8,128)S(1)}, f32[256,512]{1,0:T(8,128)}, u32[]{:S(2)}) copy-start(f32[256,512]{1,0:T(8,128)} %param.44) | copy-start | bytes 1572868
  581.6 42.0 %copy-start.17 = (f32[256,512]{1,0:T(8,128)S(1)}, f32[256,512]{1,0:T(8,128)}, u32[]{:S(2)}) copy-start(f32[256,512]{1,0:T(8,128)} %param.45) | copy-start | bytes 1572868
  581.7 66.4 %copy-start.25 = (f32[2,256]{1,0:T(2,128)S(1)}, f32[2,256]{1,0:T(2,128)}, u32[]{:S(2)}) copy-start(f32[2,256]{1,0:T(2,128)} %param.50) | copy-start | bytes 6148
  581.7 66.4 %copy-start.26 = (f32[2,256]{1,0:T(2,128)S(1)}, f32[2,256]{1,0:T(2,128)}, u32[]{:S(2)}) copy-start(f32[2,256]{1,0:T(2,128)} %param.51) | copy-start | bytes 6148
  581.7 88.7 %copy-start.14 = (f32[128,256]{1,0:T(8,128)S(1)}, f32[128,256]{1,0:T(8,128)}, u32[]{:S(2)}) copy-start(f32[128,256]{1,0:T(8,128)} %param.33) | copy-start | bytes 393220
  581.7 88.7 %copy-start.19 = (f32[128,256]{1,0:T(8,128)S(1)}, f32[128,256]{1,0:T(8,128)}, u32[]{:S(2)}) copy-start(f32[128,256]{1,0:T(8,128)} %param.42) | copy-start | bytes 393220
  581.7 88.7 %copy-start.20 = (f32[128,256]{1,0:T(8,128)S(1)}, f32[128,256]{1,0:T(8,128)}, u32[]{:S(2)}) copy-start(f32[128,256]{1,0:T(8,128)} %param.43) | copy-start | bytes 393220
  583.5 123.2 %copy-start.9 = (f32[256,384]{1,0:T(8,128)S(1)}, f32[256,384]{1,0:T(8,128)}, u32[]{:S(2)}) copy-start(f32[256,384]{1,0:T(8,128)} %param.32) | copy-start | bytes 1179652
  583.5 123.2 %copy-start.18 = (f32[256,384]{1,0:T(8,128)S(1)}, f32[256,384]{1,0:T(8,128)}, u32[]{:S(2)}) copy-start(f32[256,384]{1,0:T(8,128)} %param.40) | copy-start | bytes 1179652
  626.1 82.9 %copy-start.6 = (f32[128,1024]{1,0:T(8,128)S(1)}, f32[128,1024]{1,0:T(8,128)}, u32[]{:S(2)}) copy-start(f32[128,1024]{1,0:T(8,128)} %reduce-scatter.25.cloned.1.call-done) | copy-start | bytes 1572868
  648.1 63.0 %copy-start.22 = (f32[2,256]{1,0:T(2,128)}, f32[2,256]{1,0:T(2,128)S(1)}, u32[]{:S(2)}) copy-start(f32[2,256]{1,0:T(2,128)S(1)} %copy.69) | copy-start | bytes 6148
  672.1 48.9 %copy-start.24 = (f32[384]{0:T(512)S(1)}, f32[384]{0:T(512)}, u32[]{:S(2)}) copy-start(f32[384]{0:T(512)} %param.36) | copy-start | bytes 4612
  672.1 48.9 %copy-start.27 = (f32[384]{0:T(512)S(1)}, f32[384]{0:T(512)}, u32[]{:S(2)}) copy-start(f32[384]{0:T(512)} %param.48) | copy-start | bytes 4612
  672.1 48.9 %copy-start.28 = (f32[384]{0:T(512)S(1)}, f32[384]{0:T(512)}, u32[]{:S(2)}) copy-start(f32[384]{0:T(512)} %param.49) | copy-start | bytes 4612
  672.1 134.6 %copy-start.4 = (f32[256,768]{1,0:T(8,128)S(1)}, f32[256,768]{1,0:T(8,128)}, u32[]{:S(2)}) copy-start(f32[256,768]{1,0:T(8,128)} %param.31) | copy-start | bytes 2359300
  672.1 134.6 %copy-start.12 = (f32[256,768]{1,0:T(8,128)S(1)}, f32[256,768]{1,0:T(8,128)}, u32[]{:S(2)}) copy-start(f32[256,768]{1,0:T(8,128)} %param.38) | copy-start | bytes 2359300
  (5 other events, 5.2 us)
Sparse Core Ops, SparseCore 0:
  10.2 55.4 all-gather.8
  105.5 50.6 reduce-scatter.18
  158.4 27.9 all-gather.12
  188.8 27.3 all-gather.10
  224.0 43.8 reduce-scatter.34
  270.8 29.5 all-gather.14
  309.8 49.6 reduce-scatter.22
  363.2 51.3 reduce-scatter.20
  418.2 27.8 all-gather.16
  475.5 51.3 reduce-scatter.24
  530.8 46.2 reduce-scatter.36
  579.8 43.8 reduce-scatter.32
  626.0 20.9 reduce-scatter.40
  650.4 19.8 reduce-scatter.30
  673.2 33.4 reduce-scatter.28
  710.5 33.1 reduce-scatter.38
  746.4 60.2 reduce-scatter.26
where the time goes:
time: 818 us; the launch traced here: 816 us
  waiting for transfers between devices  562 us (69%)
  blocking collectives  87.5 us (11%)
  matrix products  72.8 us (9%)
  other arithmetic  58.9 us (7%)
  local copies, waits for them, and re-layouts  18.5 us (2%)
  between operations  15.1 us (2%)
    reduce_scatter x3, waiting for transfers between devices, row_sum(): return lax.psum_scatter(term(), 'tensor', scatter_dimension=0, tiled=True)  141 us
    unnamed x20, waiting for transfers between devices  69.3 us
    reduce_scatter x1, waiting for transfers between devices, shards(): lax.psum_scatter(ada_grad, 'dp', scatter_dimension=0, tiled=True)  61.6 us
    reduce_scatter x1, waiting for transfers between devices, shards(): lax.psum_scatter(down_grad, 'dp', scatter_dimension=1, tiled=True)  44 us
    reduce_scatter x1, waiting for transfers between devices, shards(): lax.psum_scatter(up_grad, 'dp', scatter_dimension=0, tiled=True)  40.1 us
    reduce_scatter x1, waiting for transfers between devices, shards(): lax.psum_scatter(jnp.dot(attended, proj_low, preferred_element_type=jnp.f...  34.7 us
    reduce_scatter x1, waiting for transfers between devices, shards(): lax.psum_scatter(qkv_grad, 'dp', scatter_dimension=0, tiled=True)  34.6 us
    all_gather x1, waiting for transfers between devices, shards(): mod_in2_all = lax.all_gather(mod_in2, 'tensor', axis=0, tiled=True)  29.9 us
  transfers between devices with their start and end apart: 17, of which 16 were waited for; matrix products, arithmetic and copies ran while one was open for 8% of the time, Pallas kernels for 0%

commit v1 on v0

v1 whole, which is shorter than its diff:
```python
import functools

import jax
import jax.numpy as jnp
from jax import lax
from jax.experimental import pallas as pl
from jax.experimental.pallas import tpu as pltpu
from jax.sharding import PartitionSpec as P

HD = 64
STEP = 10
LN_EPS = 1e-06
GELU_C = 0.7978845608028654
GELU_K = 0.044715
BETA_ONE = 0.9
BETA_TWO = 0.95
ADAM_EPS = 1e-08
DECAY = 0.1
LR_SCALE = 2.0
LR_BIAS = 0.2
BF = jnp.bfloat16
F32 = jnp.float32
VMEM_LIMIT = 48 * 1024 * 1024


def dot(left, right, left_dim=1, right_dim=0):
    return lax.dot_general(
        left, right, (((left_dim,), (right_dim,)), ((), ())), preferred_element_type=F32
    )


def normalize(values):
    center = values - jnp.mean(values, -1, keepdims=True)
    inv_std = lax.rsqrt(jnp.mean(center * center, -1, keepdims=True) + LN_EPS)
    return (center * inv_std, inv_std)


def norm_back(grad_n, normed, inv_std):
    return inv_std * (
        grad_n
        - jnp.mean(grad_n, -1, keepdims=True)
        - normed * jnp.mean(grad_n * normed, -1, keepdims=True)
    )


def gelu_pair(values):
    square = values * values
    inner = GELU_C * (values + GELU_K * square * values)
    tanh_val = jnp.tanh(inner)
    half = 0.5 * (1.0 + tanh_val)
    result = values * half
    slope = half + 0.5 * values * (1.0 - tanh_val * tanh_val) * GELU_C * (
        1.0 + 3.0 * GELU_K * square
    )
    return (result, slope)


def full(shape):
    return pl.BlockSpec(shape, lambda *_: (0,) * len(shape))


def rows_of(count, width):
    return pl.BlockSpec((count, width), lambda i, *_: (i, 0))


def call(body, grid, in_specs, out_specs, out_shape, args, scratch=(), scalar=None, flops=0, nbytes=0):
    params = pltpu.CompilerParams(vmem_limit_bytes=VMEM_LIMIT)
    cost = pl.CostEstimate(flops=flops, bytes_accessed=nbytes, transcendentals=0)
    if scalar is None:
        return pl.pallas_call(
            body, grid=grid, in_specs=in_specs, out_specs=out_specs, out_shape=out_shape,
            scratch_shapes=list(scratch), compiler_params=params, cost_estimate=cost,
        )(*args)
    spec = pltpu.PrefetchScalarGridSpec(
        num_scalar_prefetch=1, grid=grid, in_specs=in_specs, out_specs=out_specs,
        scratch_shapes=list(scratch),
    )
    return pl.pallas_call(
        body, grid_spec=spec, out_shape=out_shape, compiler_params=params, cost_estimate=cost,
    )(scalar, *args)


def shape(dims, dtype):
    return jax.ShapeDtypeStruct(dims, dtype)


def enter_body(x_ref, mod_ref, w_ref, bias_ref, min_ref, qkv_ref):
    normed, _ = normalize(x_ref[...].astype(F32))
    low = (normed * (1.0 + mod_ref[1:2, :]) + mod_ref[0:1, :]).astype(BF)
    min_ref[...] = low
    width = qkv_ref.shape[1]
    qkv_ref[...] = (dot(low, w_ref[:, :width]) + bias_ref[...]).astype(BF)


def attend_body(blk_ref, qkv_ref, out_ref, lse_ref):
    heads = lse_ref.shape[0]
    outs = []
    blk = blk_ref[...]
    allr = qkv_ref[...]
    for h in range(heads):
        base = h * 3 * HD
        query = blk[:, base : base + HD]
        key = allr[:, base + HD : base + 2 * HD]
        value = allr[:, base + 2 * HD : base + 3 * HD]
        scores = dot(key, query, 1, 1) * HD ** (-0.5)
        highest = jnp.max(scores, 0, keepdims=True)
        expon = jnp.exp(scores - highest)
        totals = jnp.sum(expon, 0, keepdims=True)
        prob = (expon * (1.0 / totals)).astype(BF)
        outs.append(dot(value, prob, 0, 0).T.astype(BF))
        lse_ref[h : h + 1, :] = highest + jnp.log(totals)
    out_ref[...] = outs[0] if heads == 1 else jnp.concatenate(outs, axis=1)


def middle_body(count, rows, t_ref, *refs):
    att = refs[:count]
    (proj_ref, x_ref, mod_ref, bias_ref, min_ref, res_ref, nrm_ref, inv_ref, br_ref,
     res_s, nrm_s, inv_s, br_s) = refs[count:]
    block = x_ref.shape[0]
    joined = jnp.concatenate([r[...] for r in att], axis=1)
    branch = dot(joined, proj_ref[...], 1, 1) + bias_ref[...]
    resid = x_ref[...].astype(F32) + mod_ref[2:3, :] * branch
    normed, inv = normalize(resid)
    min_ref[...] = (normed * (1.0 + mod_ref[4:5, :]) + mod_ref[3:4, :]).astype(BF)
    start = t_ref[0] * rows
    step = pl.program_id(0)

    @pl.when(step == start // block)
    def _():
        res_s[...] = resid
        nrm_s[...] = normed
        inv_s[...] = jnp.broadcast_to(inv, inv_s.shape)
        br_s[...] = branch
        own = pl.ds(pl.multiple_of(start % block, rows), rows)
        res_ref[...] = res_s[own, :]
        nrm_ref[...] = nrm_s[own, :]
        inv_ref[...] = inv_s[own, :]
        br_ref[...] = br_s[own, :]


def store_pair(odd, value, rows, keep_ref, send_ref):
    low, high = value[:rows], value[rows:]
    keep_ref[0] = jnp.where(odd, high, low)
    send_ref[0] = jnp.where(odd, low, high)


def mlp_body(rows, t_ref, in_ref, cot_ref, mod_ref, w_ref, bias_ref,
             act_ref, dpre_ref, db_ref, keep_ref, send_ref, upsum_ref, downsum_ref):
    hidden = act_ref.shape[1]
    up = w_ref[:, :hidden]
    down_t = w_ref[:, hidden:]
    pre = dot(in_ref[...], up) + bias_ref[...]
    act, slope = gelu_pair(pre)
    act_ref[...] = act.astype(BF)
    grad_b = (cot_ref[...].astype(F32) * mod_ref[5:6, :]).astype(BF)
    db_ref[...] = grad_b
    dpre = (dot(grad_b, down_t) * slope).astype(BF)
    dpre_ref[...] = dpre
    part = dot(dpre, up, 1, 1).astype(BF)
    store_pair(t_ref[0] % 2 == 1, part, rows, keep_ref, send_ref)

    @pl.when(pl.program_id(0) == 0)
    def _():
        upsum_ref[...] = jnp.zeros_like(upsum_ref)
        downsum_ref[...] = jnp.zeros_like(downsum_ref)

    upsum_ref[...] += jnp.sum(dpre.astype(F32), 0, keepdims=True)
    downsum_ref[...] += jnp.sum(grad_b.astype(F32), 0, keepdims=True)


def down_body(rows, t_ref, act_ref, w_ref, keep_ref, send_ref):
    hidden = act_ref.shape[1]
    part = dot(act_ref[...], w_ref[:, hidden:], 1, 1).astype(BF)
    store_pair(t_ref[0] % 2 == 1, part, rows, keep_ref, send_ref)


def between_body(din_ref, nrm_ref, inv_ref, mod_ref, cot_ref, br_ref, dres_ref, dbr_ref, sums_ref):
    din = din_ref[...]
    normed = nrm_ref[...]
    inv = inv_ref[:, 0:1]
    dres = cot_ref[...].astype(F32) + norm_back(din * (1.0 + mod_ref[4:5, :]), normed, inv)
    dres_ref[...] = dres
    dbr_ref[...] = (mod_ref[2:3, :] * dres).astype(BF)
    sums_ref[0:1, :] = jnp.sum(dres * br_ref[...], 0, keepdims=True)
    sums_ref[1:2, :] = jnp.sum(din, 0, keepdims=True)
    sums_ref[2:3, :] = jnp.sum(din * normed, 0, keepdims=True)


def attend_back_body(count, rows, t_ref, *refs):
    dbr = refs[:count]
    w_ref, qkv_ref, lse_ref, out_ref, colsum_ref, projsum_ref, datt, acc = refs[count:]
    heads = lse_ref.shape[0]
    width = out_ref.shape[1]
    seq = qkv_ref.shape[0]
    block = lse_ref.shape[1]
    step = pl.program_id(0)
    scale = HD ** (-0.5)

    @pl.when(step == 0)
    def _():
        total = jnp.zeros(projsum_ref.shape, F32)
        for r in range(count):
            piece = dbr[r][...]
            at = pl.ds(pl.multiple_of((t_ref[0] ^ r) * rows, rows), rows)
            datt[at, :] = dot(piece, w_ref[:, width:]).astype(BF)
            total += jnp.sum(piece.astype(F32), 0, keepdims=True)
        projsum_ref[...] = total
        acc[...] = jnp.zeros_like(acc)

    here = pl.ds(pl.multiple_of(step * block, block), block)
    blk = qkv_ref[here, :]
    allr = qkv_ref[...]
    grads = datt[here, :]
    for h in range(heads):
        base = h * 3 * HD
        query = blk[:, base : base + HD]
        key = allr[:, base + HD : base + 2 * HD]
        value = allr[:, base + 2 * HD : base + 3 * HD]
        grad = grads[:, h * HD : (h + 1) * HD]
        scores = dot(key, query, 1, 1) * scale
        prob = jnp.exp(scores - lse_ref[h : h + 1, :])
        dprob = dot(value, grad, 1, 1)
        weighted = jnp.sum(prob * dprob, 0, keepdims=True)
        dscore = (prob * (dprob - weighted)).astype(BF)
        acc[3 * h, here, :] = dot(key, dscore, 0, 0).T * scale
        acc[3 * h + 1] += dot(dscore, query)
        acc[3 * h + 2] += dot(prob.astype(BF), grad)

    @pl.when(step == seq // block - 1)
    def _():
        parts = []
        for h in range(heads):
            parts += [acc[3 * h], acc[3 * h + 1] * scale, acc[3 * h + 2]]
        result = jnp.concatenate(parts, axis=1).astype(BF)
        out_ref[...] = result
        colsum_ref[...] = jnp.sum(result.astype(F32), 0, keepdims=True)


def leave_body(rows, t_ref, dqkv_ref, w_ref, x_ref, keep_ref, send_ref, sums_ref):
    width = dqkv_ref.shape[1]
    part = dot(dqkv_ref[...], w_ref[:, :width], 1, 1)
    store_pair(t_ref[0] % 2 == 1, part.astype(BF), rows, keep_ref, send_ref)
    normed, _ = normalize(x_ref[...].astype(F32))

    @pl.when(pl.program_id(0) == 0)
    def _():
        sums_ref[...] = jnp.zeros_like(sums_ref)

    sums_ref[0:1, :] += jnp.sum(part, 0, keepdims=True)
    sums_ref[1:2, :] += jnp.sum(part * normed, 0, keepdims=True)


def last_body(din_ref, x_ref, mod_ref, dres_ref, out_ref):
    normed, inv = normalize(x_ref[...].astype(F32))
    out_ref[...] = dres_ref[...] + norm_back(din_ref[...] * (1.0 + mod_ref[1:2, :]), normed, inv)


def adam_step(weight, first, second, grad, rate, decay):
    first_new = BETA_ONE * first + (1.0 - BETA_ONE) * grad
    second_new = BETA_TWO * second + (1.0 - BETA_TWO) * grad * grad
    fix_one = 1.0 - BETA_ONE**STEP
    fix_two = 1.0 - BETA_TWO**STEP
    step_dir = first_new / fix_one / (jnp.sqrt(second_new / fix_two) + ADAM_EPS)
    return (second_new, weight - rate * (step_dir + decay * weight))


def swap(value, mask, size):
    return lax.ppermute(value, "tensor", [(i, i ^ mask) for i in range(size)])


def spread(block, size):
    if size != 8:
        have = {0: block}
        bit = 1
        while bit < size:
            for r in list(have):
                have[r ^ bit] = swap(have[r], bit, size)
            bit *= 2
        return [have[r] for r in range(size)]
    half = block.shape[0] // 2
    by_x = swap(block, 2, size)
    by_y = swap(block, 4, size)
    core = swap(block, 1, size)
    diag_a = swap(by_x[:half], 4, size)
    diag_b = swap(by_y[half:], 2, size)
    core_x = swap(by_x, 1, size)
    core_y = swap(by_y, 1, size)
    diag = jnp.concatenate([diag_a, diag_b], axis=0)
    core_d = swap(diag, 1, size)
    return [block, core, by_x, core_x, by_y, core_y, diag, core_d]


def fold(keep, send, size):
    total = keep.astype(F32) + swap(send, 1, size).astype(F32)
    width = total.shape[-1]
    half = width // 2
    bits = []
    bit = 1
    while bit < size // 2:
        bits.append(bit)
        bit *= 2
    parts = []
    for cols, order in ((slice(0, half), bits), (slice(half, width), bits[::-1])):
        have = {m: total[m, :, cols] for m in range(size // 2)}
        parts.append((have, order))
    for stage in range(len(bits)):
        for have, order in parts:
            bit = order[stage]
            away = [m for m in sorted(have) if m & bit]
            moved = swap(jnp.stack([have[m] for m in away]).astype(BF), 2 * bit, size)
            for n, m in enumerate(away):
                have[m ^ bit] = have[m ^ bit] + moved[n].astype(F32)
                del have[m]
    return jnp.concatenate([have[0] for have, _ in parts], axis=1)


def shards(
    inputs, conditioning, cotangent, w_ada, w_qkv, w_proj, w_fc1, w_fc2, col_bias, row_bias,
    m_ada, v_ada, m_qkv, v_qkv, m_proj, v_proj, m_fc1, v_fc1, m_fc2, v_fc2, m_col, v_col, m_row, v_row,
):
    T = lax.axis_size("tensor")
    G = lax.axis_size("dp")
    t = lax.axis_index("tensor")
    z = lax.axis_index("dp")
    S, D = inputs.shape
    rows = S // T
    hc = w_proj.shape[0]
    heads = hc // HD
    F = w_fc1.shape[1]
    ada = w_ada.shape[1]
    share = D // G
    tid = t.astype(jnp.int32).reshape(1)

    def around(value, k):
        return lax.ppermute(value, "dp", [(i, (i + k) % G) for i in range(G)])

    first_all = lax.all_gather(
        jnp.concatenate([w_qkv.astype(BF), w_proj.astype(BF).T], axis=1), "dp", axis=0, tiled=True
    )
    mlp_all = lax.all_gather(
        jnp.concatenate([w_fc1.astype(BF), w_fc2.astype(BF).T], axis=1), "dp", axis=0, tiled=True
    )
    w_ada_low = w_ada.astype(BF)

    cond = conditioning.astype(F32)
    silu_low = (cond * jax.nn.sigmoid(cond)).astype(BF)
    small = jnp.concatenate([silu_low.reshape(-1), col_bias.astype(BF), row_bias.astype(BF).reshape(-1)])
    small_rel = jnp.stack([small] + [around(small, k) for k in range(1, G)])
    silu_rel = lax.dynamic_slice_in_dim(small_rel[:, :D], z * share, share, 1)
    bias_rev = small_rel[::-1, D:]
    bias_abs = lax.dynamic_slice_in_dim(
        jnp.concatenate([bias_rev, bias_rev], axis=0), G - 1 - z, G, 0
    ).astype(F32)
    n_col = col_bias.shape[0]
    cols = bias_abs[:, :n_col].reshape(-1)
    bias_rows = bias_abs[:, n_col:].reshape(G, 2, share).transpose(1, 0, 2).reshape(2, D)
    bias_ada = cols[:ada]
    bias_up = cols[ada + 2 * hc :].reshape(1, F)
    bias_qkv = jnp.stack(
        [cols[ada : ada + hc].reshape(heads, HD), jnp.zeros((heads, HD), F32),
         cols[ada + hc : ada + 2 * hc].reshape(heads, HD)], axis=1,
    ).reshape(1, 3 * hc)

    part = dot(silu_rel, w_ada_low)
    mod_part = part[0]
    for k in range(1, G):
        mod_part = mod_part + around(part[k], G - k)
    mod = lax.all_gather(mod_part + bias_ada, "tensor", axis=0, tiled=True).reshape(6, D)

    blk = min(256, S)
    steps = (S // blk,)
    mod_in1, qkv = call(
        enter_body, steps,
        [rows_of(blk, D), full((6, D)), full(first_all.shape), full((1, 3 * hc))],
        [rows_of(blk, D), rows_of(blk, 3 * hc)],
        [shape((S, D), BF), shape((S, 3 * hc), BF)],
        (inputs, mod, first_all, bias_qkv), flops=2 * S * D * 3 * hc, nbytes=6 * S * D,
    )
    attended, lse = call(
        attend_body, steps,
        [rows_of(blk, 3 * hc), full((S, 3 * hc))],
        [rows_of(blk, hc), pl.BlockSpec((heads, blk), lambda i: (0, i))],
        [shape((S, hc), BF), shape((heads, S), F32)],
        (qkv, qkv), flops=16 * S * S * hc, nbytes=4 * S * hc,
    )
    proj_rel = jnp.concatenate(spread(first_all[:, 3 * hc :], T), axis=1)
    att_rel = spread(attended, T)
    mod_in2, resid1, normed2, inv2, branch1 = call(
        functools.partial(middle_body, T, rows), steps,
        [rows_of(blk, hc)] * T + [full((D, D)), rows_of(blk, D), full((6, D)), full((1, D))],
        [rows_of(blk, D), full((rows, D)), full((rows, D)), full((rows, 128)), full((rows, D))],
        [shape((S, D), BF), shape((rows, D), F32), shape((rows, D), F32), shape((rows, 128), F32),
         shape((rows, D), F32)],
        (*att_rel, proj_rel, inputs, mod, bias_rows[0:1]),
        scratch=[pltpu.VMEM((blk, D), F32), pltpu.VMEM((blk, D), F32), pltpu.VMEM((blk, 128), F32),
                 pltpu.VMEM((blk, D), F32)],
        scalar=tid, flops=2 * S * D * D, nbytes=8 * S * D,
    )

    pair = 2 * rows
    pairs = (T // 2,)
    place = pl.BlockSpec((1, rows, D), lambda i, t_ref: (i ^ (t_ref[0] // 2), 0, 0))
    halves = [shape((T // 2, rows, D), BF)] * 2
    activ, dpre, dbranch2, keep, send, up_sum, down_sum = call(
        functools.partial(mlp_body, rows), pairs,
        [rows_of(pair, D), rows_of(pair, D), full((6, D)), full((D, 2 * F)), full((1, F))],
        [rows_of(pair, F), rows_of(pair, F), rows_of(pair, D), place, place, full((1, F)), full((1, D))],
        [shape((S, F), BF), shape((S, F), BF), shape((S, D), BF), *halves, shape((1, F), F32),
         shape((1, D), F32)],
        (mod_in2, cotangent, mod, mlp_all, bias_up), scalar=tid, flops=6 * S * D * F, nbytes=12 * S * D,
    )
    din2 = fold(keep, send, T)
    cot_rows = lax.dynamic_slice_in_dim(cotangent, t * rows, rows, 0)
    x_rows = lax.dynamic_slice_in_dim(inputs, t * rows, rows, 0)
    dres1, dbranch1, sums_mid = call(
        between_body, (1,),
        [full((rows, D)), full((rows, D)), full((rows, 128)), full((6, D)), full((rows, D)), full((rows, D))],
        [full((rows, D)), full((rows, D)), full((3, D))],
        [shape((rows, D), F32), shape((rows, D), BF), shape((3, D), F32)],
        (din2, normed2, inv2, mod, cot_rows, branch1), nbytes=24 * rows * D,
    )
    dbr_rel = spread(dbranch1, T)
    dqkv, qkv_sum, proj_sum = call(
        functools.partial(attend_back_body, T, rows), steps,
        [full((rows, D))] * T + [full(first_all.shape), full((S, 3 * hc)),
                                 pl.BlockSpec((heads, blk), lambda i, *_: (0, i))],
        [full((S, 3 * hc)), full((1, 3 * hc)), full((1, D))],
        [shape((S, 3 * hc), BF), shape((1, 3 * hc), F32), shape((1, D), F32)],
        (*dbr_rel, first_all, qkv, lse),
        scratch=[pltpu.VMEM((S, hc), BF), pltpu.VMEM((3 * heads, S, HD), F32)],
        scalar=tid, flops=40 * S * S * hc, nbytes=6 * S * D,
    )
    keep1, send1, sums_in = call(
        functools.partial(leave_body, rows), pairs,
        [rows_of(pair, 3 * hc), full(first_all.shape), rows_of(pair, D)],
        [place, place, full((2, D))],
        [*halves, shape((2, D), F32)],
        (dqkv, first_all, inputs), scalar=tid, flops=6 * S * D * hc, nbytes=6 * S * D,
    )
    din1 = fold(keep1, send1, T)
    input_grad = call(
        last_body, (1,),
        [full((rows, D)), full((rows, D)), full((6, D)), full((rows, D))],
        full((rows, D)), shape((rows, D), F32),
        (din1, x_rows, mod, dres1), nbytes=14 * rows * D,
    )

    keep2, send2 = call(
        functools.partial(down_body, rows), pairs,
        [rows_of(pair, F), full((D, 2 * F))],
        [place, place], halves, (activ, mlp_all), scalar=tid, flops=2 * S * D * F, nbytes=4 * S * D,
    )
    branch2 = fold(keep2, send2, T) + bias_rows[1:2]
    block_out = resid1 + mod[5:6] * branch2
    sums_out = jnp.sum(cot_rows.astype(F32) * branch2, 0, keepdims=True)

    mlp_grad = jnp.concatenate(
        [dot(mod_in2, dpre, 0, 0).astype(BF), dot(dbranch2, activ, 0, 0).astype(BF)], axis=1
    )
    mlp_grad = lax.psum_scatter(mlp_grad, "dp", scatter_dimension=0, tiled=True).astype(F32)
    att_rows = jnp.concatenate(
        [lax.dynamic_slice_in_dim(attended, (t ^ r) * rows, rows, 0) for r in range(T)], axis=0
    )
    first_grad = jnp.concatenate(
        [dot(mod_in1, dqkv, 0, 0).astype(BF),
         dot(jnp.concatenate(dbr_rel, axis=0), att_rows, 0, 0).astype(BF)], axis=1
    )
    first_grad = lax.psum_scatter(first_grad, "dp", scatter_dimension=0, tiled=True).astype(F32)

    dmod = jnp.concatenate([sums_in, sums_mid, sums_out], axis=0).reshape(T, ada)
    dmod = jnp.sum(lax.all_to_all(dmod, "tensor", 0, 0, tiled=True), 0)
    qkv_sum = qkv_sum.reshape(heads, 3, HD)
    message = jnp.concatenate(
        [dmod.astype(BF).astype(F32), qkv_sum[:, 0].reshape(-1), qkv_sum[:, 2].reshape(-1),
         up_sum.reshape(-1), proj_sum.reshape(-1), down_sum.reshape(-1)]
    )
    message_rel = jnp.stack([message] + [around(message, k) for k in range(1, G)])
    dmod_rel = message_rel[:, :ada].astype(BF)
    bias_sum = jnp.sum(message_rel, 0)
    col_sum = lax.dynamic_slice_in_dim(bias_sum[: G * n_col], z * n_col, n_col, 0)
    row_sum = lax.dynamic_slice_in_dim(bias_sum[G * n_col :].reshape(2, D), z * share, share, 1)
    ada_sum = dot(silu_rel, dmod_rel, 0, 0)
    per = T // G
    grad_silu = dot(dmod_rel, w_ada_low, 1, 1).reshape(T, D // T)
    grad_silu = jnp.sum(lax.all_to_all(grad_silu, "tensor", 0, 0, tiled=True), 0, keepdims=True)
    grad_silu = lax.ppermute(
        grad_silu, ("dp", "tensor"),
        [(a * T + b, ((a - b // per) % G) * T + a * per + b % per) for a in range(G) for b in range(T)],
    )
    cond_here = lax.dynamic_slice_in_dim(cond, t * (D // T), D // T, 1)
    sig_here = jax.nn.sigmoid(cond_here)
    cond_grad = grad_silu * sig_here * (1.0 + cond_here * (1.0 - sig_here))

    qkv_sum = first_grad[:, : 3 * hc]
    proj_sum = first_grad[:, 3 * hc :].T
    fc1_sum = mlp_grad[:, :F]
    fc2_sum = mlp_grad[:, F:].T
    hidden = F * T
    ada_second, ada_new = adam_step(w_ada, m_ada, v_ada, ada_sum, LR_SCALE * D ** (-0.5), DECAY)
    qkv_second, qkv_new = adam_step(w_qkv, m_qkv, v_qkv, qkv_sum, LR_SCALE * D ** (-0.5), DECAY)
    proj_second, proj_new = adam_step(
        w_proj, m_proj, v_proj, proj_sum, LR_SCALE * (D // 32) ** (-0.5), DECAY
    )
    fc1_second, fc1_new = adam_step(w_fc1, m_fc1, v_fc1, fc1_sum, LR_SCALE * D ** (-0.5), DECAY)
    fc2_second, fc2_new = adam_step(w_fc2, m_fc2, v_fc2, fc2_sum, LR_SCALE * hidden ** (-0.5), DECAY)
    col_second, col_new = adam_step(col_bias, m_col, v_col, col_sum, LR_BIAS, 0.0)
    row_second, row_new = adam_step(row_bias, m_row, v_row, row_sum, LR_BIAS, 0.0)
    return (
        block_out, input_grad, cond_grad,
        ada_sum, ada_second, ada_new,
        qkv_sum, qkv_second, qkv_new,
        proj_sum, proj_second, proj_new,
        fc1_sum, fc1_second, fc1_new,
        fc2_sum, fc2_second, fc2_new,
        col_sum, col_second, col_new,
        row_sum, row_second, row_new,
    )


def solution(mesh):
    by_cols = P("dp", "tensor")
    by_rows = P("tensor", "dp")
    column = P(("tensor", "dp"))
    row = P(None, "dp")
    tokens = P("dp", None)
    weights = (by_cols, by_cols, by_rows, by_cols, by_rows, column, row)
    moments = tuple(spec for spec in weights for _ in range(2))
    results = tuple(spec for spec in weights for _ in range(3))
    mine = P(("dp", "tensor"), None)
    return jax.shard_map(
        shards,
        mesh=mesh,
        in_specs=(tokens, tokens, tokens, *weights, *moments),
        out_specs=(mine, mine, by_cols, *results),
        check_vma=False,
    )
```

time: 818 us -> 241 us (0.29)
  waiting for transfers between devices: 562 us -> 33.1 us
  blocking collectives: 87.5 us -> 9.05 us
  matrix products: 72.8 us -> 12.4 us
  starting transfers between devices: 1.11 us -> 50.5 us
  Pallas kernels: 0 us -> 42.4 us
  local copies, waits for them, and re-layouts: 18.5 us -> 41.9 us
  other arithmetic: 58.9 us -> 35.7 us
    reduce_scatter x9 -> x2, waiting for transfers between devices: 378 us -> 0.01 us  [the longest x1 0.01 us: shards(): lax.psum_scatter(mlp_grad, 'dp', scatter_dimension=0, tiled=True)]
    all_gather x5 -> x2, waiting for transfers between devices: 115 us -> 1.25 us  [the longest x1 1.25 us: shards(): lax.all_gather(jnp.concatenate([w_qkv.astype(BF), w_proj.astype(BF).T], a...]
    unnamed x20 -> x4, waiting for transfers between devices: 69.3 us -> 0.07 us
    all_gather x5 -> x1, blocking collectives: 77.6 us -> 9.05 us  [shards(): lax.all_gather(mod_part + bias_ada, 'tensor', axis=0, tiled=True)]
    dot_general x27 -> x7, matrix products: 71.4 us -> 12.4 us  [dot(): lax.dot_general(left, right, (((left_dim,), (right_dim,)), ((), ())), pre...]
    ppermute x0 -> x49, starting transfers between devices: none -> 43.1 us  [the longest x39 28.1 us: swap(): return lax.ppermute(value, 'tensor', [(i, i ^ mask) for i in range(size)])]
    pallas_call x0 -> x9, Pallas kernels: none -> 42.4 us  [the longest x5 30 us: call(): pl.pallas_call(body, grid_spec=spec, out_shape=out_shape, compiler_params...]
    ppermute x0 -> x49, waiting for transfers between devices: none -> 31.7 us  [the longest x39 27.3 us: swap(): return lax.ppermute(value, 'tensor', [(i, i ^ mask) for i in range(size)])]
  transfers between devices with their start and end apart: 17 -> 55, of which waited for: 16 -> 19; matrix products, arithmetic and copies ran while one was open for 8% -> 31% of each run, Pallas kernels for 0% -> 14%
where the time goes in v1:
time: 241 us; the launch traced here: 240 us
  starting transfers between devices  50.5 us (21%)
  Pallas kernels  42.4 us (18%)
  local copies, waits for them, and re-layouts  41.9 us (17%)
  other arithmetic  35.7 us (15%)
  waiting for transfers between devices  33.1 us (14%)
  between operations  14.9 us (6%)
  matrix products  12.4 us (5%)
  blocking collectives  9.05 us (4%)
    unnamed x120, local copies, waits for them, and re-layouts  35.6 us
    pallas_call x5, Pallas kernels, call(): pl.pallas_call(body, grid_spec=spec, out_shape=out_shape, compiler_params...  30 us
    ppermute x39, starting transfers between devices, swap(): return lax.ppermute(value, 'tensor', [(i, i ^ mask) for i in range(size)])  28.1 us
    ppermute x39, waiting for transfers between devices, swap(): return lax.ppermute(value, 'tensor', [(i, i ^ mask) for i in range(size)])  27.3 us
    ppermute x9, starting transfers between devices, around(): return lax.ppermute(value, 'dp', [(i, (i + k) % G) for i in range(G)])  14.4 us
    pallas_call x4, Pallas kernels, call(): pl.pallas_call(body, grid=grid, in_specs=in_specs, out_specs=out_specs, o...  12.4 us
    dot_general x7, matrix products, dot(): lax.dot_general(left, right, (((left_dim,), (right_dim,)), ((), ())), pre...  12.4 us
    all_gather x1, blocking collectives, shards(): lax.all_gather(mod_part + bias_ada, 'tensor', axis=0, tiled=True)  9.05 us
  transfers between devices with their start and end apart: 55, of which 19 were waited for; matrix products, arithmetic and copies ran while one was open for 31% of the time, Pallas kernels for 14%

profile of v1, /device:TPU:0, one launch (start us, length us, event | category | flops | bytes accessed | tf_op | source)
XLA Modules:
  0.0 239.9 jit_solution(16240911355733010768)
XLA Ops:
  12.8 3.1 %collective-permute-start = (bf16[1920]{0:T(1024)(128)(2,1)S(1)}, bf16[1920]{0:T(1024)(128)(2,1)S(1)}, u32[]{:S(2)}, u32[]{:S(2)}) collective-permute-start(bf16[1920]{0:T(1024)(128)(2,1)S(1)} %pad_maximum_fusion.16), channel_id=1, source_target_pairs={{0,8},{8,16},{16,24},{24,0},{1,9},{9,17},{17,25},{25,1},{2,10},{10... | collective-permute-start | bytes 11528 | tf_op jit(solution)/shard_map/ppermute | solution.py:335
  15.9 2.6 %collective-permute-start.1 = (bf16[1920]{0:T(1024)(128)(2,1)S(1)}, bf16[1920]{0:T(1024)(128)(2,1)S(1)}, u32[]{:S(2)}, u32[]{:S(2)}) collective-permute-start(bf16[1920]{0:T(1024)(128)(2,1)S(1)} %pad_maximum_fusion.16), channel_id=1, source_target_pairs={{0,16},{8,24},{16,0},{24,8},{1,17},{9,25},{17,1},{25,9},{2,18},{10... | collective-permute-start | bytes 11528 | tf_op jit(solution)/shard_map/ppermute | solution.py:335
  23.5 2.1 collective-permute-start.3
  27.3 2.9 %collective-permute-done.4 = f32[768]{0:T(1024)S(1)} collective-permute-done((f32[768]{0:T(1024)S(1)}, f32[768]{0:T(1024)S(1)}, u32[]{:S(2)}, u32[]{:S(2)}) %collective-permute-start.4) | collective-permute-done | bytes 3104 | tf_op jit(solution)/shard_map/ppermute | solution.py:335
  31.2 9.0 %all-gather = f32[8,1,768]{2,1,0:T(1,128)S(1)} all-gather(f32[1,1,768]{2,1,0:T(1,128)S(1)} %reshape.157), channel_id=1, replica_groups=mesh['dp'=4,'tensor'=8] {'tensor'}, dimensions={0}, use_global_device_ids=true | all-gather | bytes 27648 | tf_op jit(solution)/shard_map/all_gather | solution.py:368
  42.8 2.9 %shard_map.415 = (bf16[1024,1024]{1,0:T(8,128)(2,1)S(1)}, bf16[1024,384]{1,0:T(8,128)(2,1)S(1)}) custom-call(bf16[1024,1024]{1,0:T(8,128)(2,1)S(1)} %copy-done, f32[6,1024]{1,0:T(8,128)S(1)} %reshape.147.mod_ref.refs_10_, bf16[1024,512]{1,0:T(8,128)(2,1)S(1)} %copy-done.2, f32[1,384]{1,0:T(1,128)S(1)} %reshape.148.bias_ref), custom_call_target="tpu_custom_call" | custom-call | flops 805306368 | bytes 6291456 | tf_op jit(solution)/shard_map/pallas_call | solution.py:70
  45.7 7.9 %shard_map.416 = (bf16[1024,128]{1,0:T(8,128)(2,1)S(1)}, f32[2,1024]{1,0:T(2,128)S(1)}) custom-call(bf16[1024,384]{1,0:T(8,128)(2,1)S(1)} %get-tuple-element.51.blk_ref.qkv_ref.refs_9_, bf16[1024,384]{1,0:T(8,128)(2,1)S(1)} %get-tuple-element.51.blk_ref.qkv_ref.refs_9_), custom_call_target="tpu_custom_call" | custom-call | flops 2147483648 | bytes 524288 | tf_op jit(solution)/shard_map/pallas_call | solution.py:70
  53.7 1.5 collective-permute-start.7
  58.7 2.1 copy.93
  60.8 2.0 copy.89
  62.7 2.0 copy.90
  64.8 2.0 copy.91
  68.8 1.5 collective-permute-start.11
  70.4 1.5 collective-permute-start.12
  74.1 1.7 constant_dynamic-update-slice_fusion.8
  75.8 1.7 constant_dynamic-update-slice_fusion.7
  84.5 6.5 %shard_map.417 = (bf16[1024,1024]{1,0:T(8,128)(2,1)S(1)}, f32[128,1024]{1,0:T(8,128)S(1)}, f32[128,1024]{1,0:T(8,128)S(1)}, f32[128,128]{1,0:T(8,128)S(1)}, f32[128,1024]{1,0:T(8,128)S(1)}) custom-call(s32[1]{0:T(128)} %bitcast.t_ref, bf16[1024,128]{1,0:T(8,128)(2,1)S(1)} %get-tuple-element.52.refs_0_, bf16[1024,128]{1,0:T(8,128)(2,1)S(1)} %collective-permute-done.6.refs_1_, ...), custom_call_target="tpu_custom_call" | custom-call | flops 2147483648 | bytes 8388608 | tf_op jit(solution)/shard_map/pallas_call | solution.py:78
  92.3 8.2 %shard_map.418 = (bf16[1024,512]{1,0:T(8,128)(2,1)S(1)}, bf16[1024,512]{1,0:T(8,128)(2,1)S(1)}, bf16[1024,1024]{1,0:T(8,128)(2,1)}, bf16[4,128,1024]{2,1,0:T(8,1...) custom-call(s32[1]{0:T(128)} %bitcast.t_ref, ...), custom_call_target="tpu_custom_call" | custom-call | flops 3221225472 | bytes 12582912 | tf_op jit(solution)/shard_map/pallas_call | solution.py:78
  101.7 2.1 shard_map.419
  104.4 3.0 %convolution_convert_fusion = bf16[1024,512]{0,1:T(8,128)(2,1)S(1)} fusion(bf16[1024,1024]{1,0:T(8,128)(2,1)} %get-tuple-element.77, bf16[1024,512]{1,0:T(8,128)(2,1)S(1)} %get-tuple-element.55.act_ref), kind=kOutput, calls=%fused_computation.4 | convolution fusion | flops 1074266112 | bytes 4194304 | tf_op jit(solution)/shard_map/dot_general | solution.py:27
  108.8 1.8 fusion.33
  110.6 1.9 fusion.32
  112.6 1.5 collective-permute-start.23
  116.8 1.5 pad_maximum_fusion
  118.4 3.6 %collective-permute-done.23 = bf16[2,128,512]{2,1,0:T(8,128)(2,1)} collective-permute-done((bf16[2,128,512]{2,1,0:T(8,128)(2,1)S(1)}, bf16[2,128,512]{2,1,0:T(8,128)(2,1)}, u32[]{:S(2)}, u32[]{:S(2)}) %collective-permute-start.23) | collective-permute-done | bytes 262176 | tf_op jit(solution)/shard_map/ppermute | solution.py:268
  126.9 2.2 collective-permute-done.30
  133.3 1.9 multiply_reduce_fusion
  141.4 3.1 %collective-permute-done.33.refs_2_ = bf16[128,1024]{1,0:T(8,128)(2,1)S(1)} collective-permute-done((bf16[128,1024]{1,0:T(8,128)(2,1)S(1)}, bf16[128,1024]{1,0:T(8,128)(2,1)S(1)}, u32[]{:S(2)}, u32[]{:S(2)}) %collective-permute-start.33) | collective-permute-done | bytes 262176 | tf_op jit(solution)/shard_map/ppermute | solution.py:268
  145.4 2.8 %collective-permute-done.35.refs_4_ = bf16[128,1024]{1,0:T(8,128)(2,1)S(1)} collective-permute-done((bf16[128,1024]{1,0:T(8,128)(2,1)S(1)}, bf16[128,1024]{1,0:T(8,128)(2,1)S(1)}, u32[]{:S(2)}, u32[]{:S(2)}) %collective-permute-start.35) | collective-permute-done | bytes 262176 | tf_op jit(solution)/shard_map/ppermute | solution.py:268
  148.3 1.6 collective-permute-start.38
  151.5 1.8 collective-permute-done.38
  155.5 10.2 %shard_map.421 = (bf16[1024,384]{1,0:T(8,128)(2,1)S(1)}, f32[1,384]{1,0:T(1,128)S(1)}, f32[1,1024]{1,0:T(1,128)S(1)}) custom-call(s32[1]{0:T(128)} %bitcast.t_ref, bf16[128,1024]{1,0:T(8,128)(2,1)S(1)} %get-tuple-element.63.refs_0_, bf16[128,1024]{1,0:T(8,128)(2,1)S(1)} %collective-permute-done.32.refs_1_, ...), custom_call_target="tpu_custom_call" | custom-call | flops 5368709120 | bytes 6291456 | tf_op jit(solution)/shard_map/pallas_call | solution.py:78
  165.7 3.0 %shard_map.422 = (bf16[4,128,1024]{2,1,0:T(8,128)(2,1)S(1)}, bf16[4,128,1024]{2,1,0:T(8,128)(2,1)S(1)}, f32[2,1024]{1,0:T(2,128)S(1)}) custom-call(s32[1]{0:T(128)} %bitcast.t_ref, bf16[1024,384]{1,0:T(8,128)(2,1)S(1)} %get-tuple-element.65.dqkv_ref, bf16[1024,512]{1,0:T(8,128)(2,1)S(1)} %copy-done.3, bf16[1024,1024]{1,0:T(8,128)(2,1)S(1)} %copy-done.1), custom_call_target="tpu_custom_call" | custom-call | flops 805306368 | bytes 6291456 | tf_op jit(solution)/shard_map/pallas_call | solution.py:78
  170.4 3.3 %all-to-all-start = ((f32[8,1,768]{2,1,0:T(1,128)}), f32[8,1,768]{2,1,0:T(1,128)S(1)}, u32[]{:S(2)}, u32[]{:S(2)}) async-start(f32[8,1,768]{2,1,0:T(1,128)} %all_to_all.16), calls=%async_computation | async-start | bytes 49152 | tf_op jit(solution)/shard_map/all_to_all | solution.py:471
  175.0 2.2 convolution_convert_fusion.3
  177.3 1.9 convolution_convert_fusion.2
  181.8 2.4 collective-permute-start.47
  184.2 2.2 pad_maximum_fusion.1
  187.4 3.9 %all-to-all-start.1 = ((f32[8,1,128]{2,1,0:T(1,128)}), f32[8,1,128]{2,1,0:T(1,128)S(1)}, u32[]{:S(2)}, u32[]{:S(2)}) async-start(f32[8,1,128]{2,1,0:T(1,128)} %bitcast.18), calls=%async_computation.1 | async-start | bytes 8192 | tf_op jit(solution)/shard_map/all_to_all | solution.py:485
  191.3 3.5 %multiply_subtract_fusion = (f32[256,768]{1,0:T(8,128)}, f32[256,768]{1,0:T(8,128)}, f32[256,768]{1,0:T(8,128)}) fusion(f32[256,768]{1,0:T(8,128)S(1)} %copy-done.13, f32[256,768]{1,0:T(8,128)} %param.34, f32[256,768]{1,0:T(8,128)} %param.35, bf16[4,1024]{1,0:T(4,128)(2,1)S(1)} %slice.279, s32[]{:T(128)S(6)} %select_n.37, bf16[1,3584]{1,0:T(2,128)(2,1)S(1)} %stack.80, ...), kind=kOutput, calls=%fused_computation.13 | convolution fusion | flops 4546560 | bytes 4777988 | tf_op jit(solution)/shard_map/dot_general | solution.py:27
  194.9 3.0 %fusion.34 = (bf16[4,128,1024]{2,1,0:T(8,128)(2,1)S(1)}, f32[4,128,1024]{2,1,0:T(8,128)}) fusion(bf16[4,128,1024]{2,1,0:T(8,128)(2,1)} %collective-permute-done.40, bf16[4,128,1024]{2,1,0:T(8,128)(2,1)S(1)} %get-tuple-element.66), kind=kLoop, calls=%fused_computation.149 | loop fusion | flops 2097152 | bytes 5242880 | tf_op jit(solution)/shard_map/convert.13
  198.0 2.1 collective-permute-start.41
  203.5 3.2 %collective-permute-done.41 = bf16[2,128,512]{2,1,0:T(8,128)(2,1)S(1)} collective-permute-done((bf16[2,128,512]{2,1,0:T(8,128)(2,1)S(1)}, bf16[2,128,512]{2,1,0:T(8,128)(2,1)S(1)}, u32[]{:S(2)}, u32[]{:S(2)}) %collective-permute-start.41) | collective-permute-done | bytes 262176 | tf_op jit(solution)/shard_map/ppermute | solution.py:268
  209.2 1.5 collective-permute-start.42
  212.5 1.8 collective-permute-done.42
  220.6 2.1 copy.98
  222.7 2.0 copy.99
  225.8 2.6 %multiply_subtract_fusion.1 = (f32[512,256]{1,0:T(8,128)}, f32[512,256]{1,0:T(8,128)}, f32[512,256]{1,0:T(8,128)}) fusion(f32[512,256]{1,0:T(8,128)S(1)} %copy-done.14, f32[512,256]{1,0:T(8,128)} %param.42, f32[512,256]{1,0:T(8,128)} %param.43, f32[256,1024]{0,1:T(8,128)S(1)} %convert_element_type.232), kind=kLoop, calls=%fused_computation.22 | loop fusion | flops 1966080 | bytes 3670016 | tf_op jit(solution)/shard_map/sub | solution.py:264
  (304 shorter events, 83.8 us)
Async XLA Ops:
  7.2 34.4 %all-gather.4.cloned.1.call-start = ((), (), s32[]{:S(2)}) async-start(), calls=%async_computation.4 | async-start | bytes 1310720 | tf_op jit(solution)/shard_map/all_gather | solution.py:337
  10.0 82.3 %all-gather.6.cloned.1.call-start = ((), (), s32[]{:S(2)}) async-start(), calls=%async_computation.5 | async-start | bytes 2621440 | tf_op jit(solution)/shard_map/all_gather | solution.py:340
  12.8 10.3 %collective-permute-start = (bf16[1920]{0:T(1024)(128)(2,1)S(1)}, bf16[1920]{0:T(1024)(128)(2,1)S(1)}, u32[]{:S(2)}, u32[]{:S(2)}) collective-permute-start(bf16[1920]{0:T(1024)(128)(2,1)S(1)} %pad_maximum_fusion.16), channel_id=1, source_target_pairs={{0,8},{8,16},{16,24},{24,0},{1,9},{9,17},{17,25},{25,1},{2,10},{10... | collective-permute-start | bytes 11528 | tf_op jit(solution)/shard_map/ppermute | solution.py:335
  15.9 7.3 %collective-permute-start.1 = (bf16[1920]{0:T(1024)(128)(2,1)S(1)}, bf16[1920]{0:T(1024)(128)(2,1)S(1)}, u32[]{:S(2)}, u32[]{:S(2)}) collective-permute-start(bf16[1920]{0:T(1024)(128)(2,1)S(1)} %pad_maximum_fusion.16), channel_id=1, source_target_pairs={{0,16},{8,24},{16,0},{24,8},{1,17},{9,25},{17,1},{25,9},{2,18},{10... | collective-permute-start | bytes 11528 | tf_op jit(solution)/shard_map/ppermute | solution.py:335
  18.5 4.7 %collective-permute-start.2 = (bf16[1920]{0:T(1024)(128)(2,1)S(1)}, bf16[1920]{0:T(1024)(128)(2,1)S(1)}, u32[]{:S(2)}, u32[]{:S(2)}) collective-permute-start(bf16[1920]{0:T(1024)(128)(2,1)S(1)} %pad_maximum_fusion.16), channel_id=1, source_target_pairs={{0,24},{8,0},{16,8},{24,16},{1,25},{9,1},{17,9},{25,17},{2,26},{10... | collective-permute-start | bytes 11528 | tf_op jit(solution)/shard_map/ppermute | solution.py:335
  23.0 195.2 %reduce-scatter.5.cloned.1.call-start = ((), (), s32[]{:S(2)}) async-start(), calls=%async_computation.7 | async-start | bytes 2621440 | tf_op jit(solution)/shard_map/reduce_scatter | solution.py:460
  25.6 4.7 %collective-permute-start.4 = (f32[768]{0:T(1024)S(1)}, f32[768]{0:T(1024)S(1)}, u32[]{:S(2)}, u32[]{:S(2)}) collective-permute-start(f32[768]{0:T(1024)S(1)} %get-tuple-element.152), channel_id=1, source_target_pairs={{0,16},{8,24},{16,0},{24,8},{1,17},{9,25},{17,1},{25,9},{2,18},{10... | collective-permute-start | bytes 9224 | tf_op jit(solution)/shard_map/ppermute | solution.py:335
  25.7 5.5 %collective-permute-start.5 = (f32[768]{0:T(1024)S(1)}, f32[768]{0:T(1024)S(1)}, u32[]{:S(2)}, u32[]{:S(2)}) collective-permute-start(f32[768]{0:T(1024)S(1)} %get-tuple-element.151), channel_id=1, source_target_pairs={{0,8},{8,16},{16,24},{24,0},{1,9},{9,17},{17,25},{25,1},{2,10},{10... | collective-permute-start | bytes 9224 | tf_op jit(solution)/shard_map/ppermute | solution.py:335
  53.7 15.0 %collective-permute-start.7 = (bf16[1024,128]{1,0:T(8,128)(2,1)S(1)}, bf16[1024,128]{1,0:T(8,128)(2,1)S(1)}, u32[]{:S(2)}, u32[]{:S(2)}) collective-permute-start(bf16[1024,128]{1,0:T(8,128)(2,1)S(1)} %get-tuple-element.52.refs_0_), channel_id=1, source_target_pairs={{0,2},{1,3},{2,0},{3,1},{4,6},{5,7},{6,4},{7,5},{8,10},{9,11},{10,... | collective-permute-start | bytes 786440 | tf_op jit(solution)/shard_map/ppermute | solution.py:268
  55.2 13.6 %collective-permute-start.9 = (bf16[1024,128]{1,0:T(8,128)(2,1)S(1)}, bf16[1024,128]{1,0:T(8,128)(2,1)S(1)}, u32[]{:S(2)}, u32[]{:S(2)}) collective-permute-start(bf16[1024,128]{1,0:T(8,128)(2,1)S(1)} %get-tuple-element.52.refs_0_), channel_id=1, source_target_pairs={{0,4},{1,5},{2,6},{3,7},{4,0},{5,1},{6,2},{7,3},{8,12},{9,13},{10,... | collective-permute-start | bytes 786440 | tf_op jit(solution)/shard_map/ppermute | solution.py:268
  57.5 15.9 %collective-permute-start.14 = (bf16[1024,128]{1,0:T(8,128)(2,1)}, bf16[1024,128]{1,0:T(8,128)(2,1)}, u32[]{:S(2)}, u32[]{:S(2)}) collective-permute-start(bf16[1024,128]{1,0:T(8,128)(2,1)} %get-tuple-element.200), channel_id=1, source_target_pairs={{0,1},{1,0},{2,3},{3,2},{4,5},{5,4},{6,7},{7,6},{8,9},{9,8},{10,11... | collective-permute-start | bytes 786440 | tf_op jit(solution)/shard_map/ppermute | solution.py:268
  57.5 12.8 %collective-permute-start.15 = (bf16[1024,128]{1,0:T(8,128)(2,1)}, bf16[1024,128]{1,0:T(8,128)(2,1)}, u32[]{:S(2)}, u32[]{:S(2)}) collective-permute-start(bf16[1024,128]{1,0:T(8,128)(2,1)} %get-tuple-element.200), channel_id=1, source_target_pairs={{0,2},{1,3},{2,0},{3,1},{4,6},{5,7},{6,4},{7,5},{8,10},{9,11},{10,... | collective-permute-start | bytes 786440 | tf_op jit(solution)/shard_map/ppermute | solution.py:268
  58.1 14.7 %collective-permute-start.17 = (bf16[1024,128]{1,0:T(8,128)(2,1)}, bf16[1024,128]{1,0:T(8,128)(2,1)S(1)}, u32[]{:S(2)}, u32[]{:S(2)}) collective-permute-start(bf16[1024,128]{1,0:T(8,128)(2,1)} %get-tuple-element.200), channel_id=1, source_target_pairs={{0,4},{1,5},{2,6},{3,7},{4,0},{5,1},{6,2},{7,3},{8,12},{9,13},{10,... | collective-permute-start | bytes 786440 | tf_op jit(solution)/shard_map/ppermute | solution.py:268
  68.7 15.8 %collective-permute-start.6 = (bf16[1024,128]{1,0:T(8,128)(2,1)S(1)}, bf16[1024,128]{1,0:T(8,128)(2,1)S(1)}, u32[]{:S(2)}, u32[]{:S(2)}) collective-permute-start(bf16[1024,128]{1,0:T(8,128)(2,1)S(1)} %get-tuple-element.52.refs_0_), channel_id=1, source_target_pairs={{0,1},{1,0},{2,3},{3,2},{4,5},{5,4},{6,7},{7,6},{8,9},{9,8},{10,11... | collective-permute-start | bytes 786440 | tf_op jit(solution)/shard_map/ppermute | solution.py:268
  68.8 8.7 %collective-permute-start.11 = (bf16[512,128]{1,0:T(8,128)(2,1)S(1)}, bf16[512,128]{1,0:T(8,128)(2,1)S(1)}, u32[]{:S(2)}, u32[]{:S(2)}) collective-permute-start(bf16[512,128]{1,0:T(8,128)(2,1)S(1)} %slice.288), channel_id=1, source_target_pairs={{0,4},{1,5},{2,6},{3,7},{4,0},{5,1},{6,2},{7,3},{8,12},{9,13},{10,... | collective-permute-start | bytes 393224 | tf_op jit(solution)/shard_map/ppermute | solution.py:268
  70.4 8.5 %collective-permute-start.12 = (bf16[512,128]{1,0:T(8,128)(2,1)S(1)}, bf16[512,128]{1,0:T(8,128)(2,1)S(1)}, u32[]{:S(2)}, u32[]{:S(2)}) collective-permute-start(bf16[512,128]{1,0:T(8,128)(2,1)S(1)} %slice.289), channel_id=1, source_target_pairs={{0,2},{1,3},{2,0},{3,1},{4,6},{5,7},{6,4},{7,5},{8,10},{9,11},{10,... | collective-permute-start | bytes 393224 | tf_op jit(solution)/shard_map/ppermute | solution.py:268
  72.8 5.4 %collective-permute-start.19 = (bf16[512,128]{1,0:T(8,128)(2,1)S(1)}, bf16[512,128]{1,0:T(8,128)(2,1)S(1)}, u32[]{:S(2)}, u32[]{:S(2)}) collective-permute-start(bf16[512,128]{1,0:T(8,128)(2,1)S(1)} %slice.291), channel_id=1, source_target_pairs={{0,4},{1,5},{2,6},{3,7},{4,0},{5,1},{6,2},{7,3},{8,12},{9,13},{10,... | collective-permute-start | bytes 393224 | tf_op jit(solution)/shard_map/ppermute | solution.py:268
  73.5 5.4 %collective-permute-start.20 = (bf16[512,128]{1,0:T(8,128)(2,1)S(1)}, bf16[512,128]{1,0:T(8,128)(2,1)S(1)}, u32[]{:S(2)}, u32[]{:S(2)}) collective-permute-start(bf16[512,128]{1,0:T(8,128)(2,1)S(1)} %slice.292), channel_id=1, source_target_pairs={{0,2},{1,3},{2,0},{3,1},{4,6},{5,7},{6,4},{7,5},{8,10},{9,11},{10,... | collective-permute-start | bytes 393224 | tf_op jit(solution)/shard_map/ppermute | solution.py:268
  78.2 6.3 %collective-permute-start.10 = (bf16[1024,128]{1,0:T(8,128)(2,1)S(1)}, bf16[1024,128]{1,0:T(8,128)(2,1)S(1)}, u32[]{:S(2)}, u32[]{:S(2)}) collective-permute-start(bf16[1024,128]{1,0:T(8,128)(2,1)S(1)} %collective-permute-done.9.refs_4_), channel_id=1, source_target_pairs={{0,1},{1,0},{2,3},{3,2},{4,5},{5,4},{6,7},{7,6},{8,9},{9,8},{10,11... | collective-permute-start | bytes 786440 | tf_op jit(solution)/shard_map/ppermute | solution.py:268
  78.9 5.6 %collective-permute-start.8 = (bf16[1024,128]{1,0:T(8,128)(2,1)S(1)}, bf16[1024,128]{1,0:T(8,128)(2,1)S(1)}, u32[]{:S(2)}, u32[]{:S(2)}) collective-permute-start(bf16[1024,128]{1,0:T(8,128)(2,1)S(1)} %collective-permute-done.7.refs_2_), channel_id=1, source_target_pairs={{0,1},{1,0},{2,3},{3,2},{4,5},{5,4},{6,7},{7,6},{8,9},{9,8},{10,11... | collective-permute-start | bytes 786440 | tf_op jit(solution)/shard_map/ppermute | solution.py:268
  79.5 5.0 %collective-permute-start.13 = (bf16[1024,128]{1,0:T(8,128)(2,1)S(1)}, bf16[1024,128]{1,0:T(8,128)(2,1)S(1)}, u32[]{:S(2)}, u32[]{:S(2)}) collective-permute-start(bf16[1024,128]{1,0:T(8,128)(2,1)S(1)} %constant_dynamic-update-slice_fusion.refs_6_), channel_id=1, source_target_pairs={{0,1},{1,0},{2,3},{3,2},{4,5},{5,4},{6,7},{7,6},{8,9},{9,8},{10,11... | collective-permute-start | bytes 786440 | tf_op jit(solution)/shard_map/ppermute | solution.py:268
  100.5 8.3 %collective-permute-start.27 = (bf16[4,128,1024]{2,1,0:T(8,128)(2,1)S(1)}, bf16[4,128,1024]{2,1,0:T(8,128)(2,1)S(1)}, u32[]{:S(2)}, u32[]{:S(2)}) collective-permute-start(bf16[4,128,1024]{2,1,0:T(8,128)(2,1)S(1)} %get-tuple-element.59), channel_id=1, source_target_pairs={{0,1},{1,0},{2,3},{3,2},{4,5},{5,4},{6,7},{7,6},{8,9},{9,8},{10,11... | collective-permute-start | bytes 3145736 | tf_op jit(solution)/shard_map/ppermute | solution.py:268
  103.9 6.8 %collective-permute-start.22 = (bf16[4,128,1024]{2,1,0:T(8,128)(2,1)S(1)}, bf16[4,128,1024]{2,1,0:T(8,128)(2,1)S(1)}, u32[]{:S(2)}, u32[]{:S(2)}) collective-permute-start(bf16[4,128,1024]{2,1,0:T(8,128)(2,1)S(1)} %get-tuple-element.57), channel_id=1, source_target_pairs={{0,1},{1,0},{2,3},{3,2},{4,5},{5,4},{6,7},{7,6},{8,9},{9,8},{10,11... | collective-permute-start | bytes 3145736 | tf_op jit(solution)/shard_map/ppermute | solution.py:268
  112.6 9.3 %collective-permute-start.23 = (bf16[2,128,512]{2,1,0:T(8,128)(2,1)S(1)}, bf16[2,128,512]{2,1,0:T(8,128)(2,1)}, u32[]{:S(2)}, u32[]{:S(2)}) collective-permute-start(bf16[2,128,512]{2,1,0:T(8,128)(2,1)S(1)} %pad_maximum_fusion.7), channel_id=1, source_target_pairs={{0,2},{1,3},{2,0},{3,1},{4,6},{5,7},{6,4},{7,5},{8,10},{9,11},{10,... | collective-permute-start | bytes 786440 | tf_op jit(solution)/shard_map/ppermute | solution.py:268
  114.1 9.3 %collective-permute-start.25 = (bf16[2,128,512]{2,1,0:T(8,128)(2,1)S(1)}, bf16[2,128,512]{2,1,0:T(8,128)(2,1)}, u32[]{:S(2)}, u32[]{:S(2)}) collective-permute-start(bf16[2,128,512]{2,1,0:T(8,128)(2,1)S(1)} %stack.82), channel_id=1, source_target_pairs={{0,4},{1,5},{2,6},{3,7},{4,0},{5,1},{6,2},{7,3},{8,12},{9,13},{10,... | collective-permute-start | bytes 786440 | tf_op jit(solution)/shard_map/ppermute | solution.py:268
  115.4 11.5 %collective-permute-start.28 = (bf16[2,128,512]{2,1,0:T(8,128)(2,1)S(1)}, bf16[2,128,512]{2,1,0:T(8,128)(2,1)S(1)}, u32[]{:S(2)}, u32[]{:S(2)}) collective-permute-start(bf16[2,128,512]{2,1,0:T(8,128)(2,1)S(1)} %pad_maximum_fusion.8), channel_id=1, source_target_pairs={{0,2},{1,3},{2,0},{3,1},{4,6},{5,7},{6,4},{7,5},{8,10},{9,11},{10,... | collective-permute-start | bytes 786440 | tf_op jit(solution)/shard_map/ppermute | solution.py:268
  116.0 13.1 %collective-permute-start.30 = (bf16[2,128,512]{2,1,0:T(8,128)(2,1)S(1)}, bf16[2,128,512]{2,1,0:T(8,128)(2,1)}, u32[]{:S(2)}, u32[]{:S(2)}) collective-permute-start(bf16[2,128,512]{2,1,0:T(8,128)(2,1)S(1)} %stack.83), channel_id=1, source_target_pairs={{0,4},{1,5},{2,6},{3,7},{4,0},{5,1},{6,2},{7,3},{8,12},{9,13},{10,... | collective-permute-start | bytes 786440 | tf_op jit(solution)/shard_map/ppermute | solution.py:268
  124.6 7.4 %collective-permute-start.24 = (bf16[1,128,512]{2,1,0:T(8,128)(2,1)S(1)}, bf16[1,128,512]{2,1,0:T(8,128)(2,1)S(1)}, u32[]{:S(2)}, u32[]{:S(2)}) collective-permute-start(bf16[1,128,512]{2,1,0:T(8,128)(2,1)S(1)} %get-tuple-element.190), channel_id=1, source_target_pairs={{0,4},{1,5},{2,6},{3,7},{4,0},{5,1},{6,2},{7,3},{8,12},{9,13},{10,... | collective-permute-start | bytes 393224 | tf_op jit(solution)/shard_map/ppermute | solution.py:268
  126.0 6.0 %collective-permute-start.26 = (bf16[1,128,512]{2,1,0:T(8,128)(2,1)S(1)}, bf16[1,128,512]{2,1,0:T(8,128)(2,1)S(1)}, u32[]{:S(2)}, u32[]{:S(2)}) collective-permute-start(bf16[1,128,512]{2,1,0:T(8,128)(2,1)S(1)} %get-tuple-element.191), channel_id=1, source_target_pairs={{0,2},{1,3},{2,0},{3,1},{4,6},{5,7},{6,4},{7,5},{8,10},{9,11},{10,... | collective-permute-start | bytes 393224 | tf_op jit(solution)/shard_map/ppermute | solution.py:268
  130.2 5.0 %collective-permute-start.29 = (bf16[1,128,512]{2,1,0:T(8,128)(2,1)S(1)}, bf16[1,128,512]{2,1,0:T(8,128)(2,1)S(1)}, u32[]{:S(2)}, u32[]{:S(2)}) collective-permute-start(bf16[1,128,512]{2,1,0:T(8,128)(2,1)S(1)} %get-tuple-element.184), channel_id=1, source_target_pairs={{0,4},{1,5},{2,6},{3,7},{4,0},{5,1},{6,2},{7,3},{8,12},{9,13},{10,... | collective-permute-start | bytes 393224 | tf_op jit(solution)/shard_map/ppermute | solution.py:268
  131.5 5.0 %collective-permute-start.31 = (bf16[1,128,512]{2,1,0:T(8,128)(2,1)S(1)}, bf16[1,128,512]{2,1,0:T(8,128)(2,1)S(1)}, u32[]{:S(2)}, u32[]{:S(2)}) collective-permute-start(bf16[1,128,512]{2,1,0:T(8,128)(2,1)S(1)} %get-tuple-element.185), channel_id=1, source_target_pairs={{0,2},{1,3},{2,0},{3,1},{4,6},{5,7},{6,4},{7,5},{8,10},{9,11},{10,... | collective-permute-start | bytes 393224 | tf_op jit(solution)/shard_map/ppermute | solution.py:268
  138.0 6.4 %collective-permute-start.33 = (bf16[128,1024]{1,0:T(8,128)(2,1)S(1)}, bf16[128,1024]{1,0:T(8,128)(2,1)S(1)}, u32[]{:S(2)}, u32[]{:S(2)}) collective-permute-start(bf16[128,1024]{1,0:T(8,128)(2,1)S(1)} %get-tuple-element.63.refs_0_), channel_id=1, source_target_pairs={{0,2},{1,3},{2,0},{3,1},{4,6},{5,7},{6,4},{7,5},{8,10},{9,11},{10,... | collective-permute-start | bytes 786440 | tf_op jit(solution)/shard_map/ppermute | solution.py:268
  139.3 10.6 %collective-permute-start.32 = (bf16[128,1024]{1,0:T(8,128)(2,1)S(1)}, bf16[128,1024]{1,0:T(8,128)(2,1)S(1)}, u32[]{:S(2)}, u32[]{:S(2)}) collective-permute-start(bf16[128,1024]{1,0:T(8,128)(2,1)S(1)} %get-tuple-element.63.refs_0_), channel_id=1, source_target_pairs={{0,1},{1,0},{2,3},{3,2},{4,5},{5,4},{6,7},{7,6},{8,9},{9,8},{10,11... | collective-permute-start | bytes 786440 | tf_op jit(solution)/shard_map/ppermute | solution.py:268
  139.3 9.0 %collective-permute-start.35 = (bf16[128,1024]{1,0:T(8,128)(2,1)S(1)}, bf16[128,1024]{1,0:T(8,128)(2,1)S(1)}, u32[]{:S(2)}, u32[]{:S(2)}) collective-permute-start(bf16[128,1024]{1,0:T(8,128)(2,1)S(1)} %get-tuple-element.63.refs_0_), channel_id=1, source_target_pairs={{0,4},{1,5},{2,6},{3,7},{4,0},{5,1},{6,2},{7,3},{8,12},{9,13},{10,... | collective-permute-start | bytes 786440 | tf_op jit(solution)/shard_map/ppermute | solution.py:268
  144.5 5.5 %collective-permute-start.34 = (bf16[128,1024]{1,0:T(8,128)(2,1)S(1)}, bf16[128,1024]{1,0:T(8,128)(2,1)S(1)}, u32[]{:S(2)}, u32[]{:S(2)}) collective-permute-start(bf16[128,1024]{1,0:T(8,128)(2,1)S(1)} %collective-permute-done.33.refs_2_), channel_id=1, source_target_pairs={{0,1},{1,0},{2,3},{3,2},{4,5},{5,4},{6,7},{7,6},{8,9},{9,8},{10,11... | collective-permute-start | bytes 786440 | tf_op jit(solution)/shard_map/ppermute | solution.py:268
  144.5 7.0 %collective-permute-start.37 = (bf16[64,1024]{1,0:T(8,128)(2,1)S(1)}, bf16[64,1024]{1,0:T(8,128)(2,1)S(1)}, u32[]{:S(2)}, u32[]{:S(2)}) collective-permute-start(bf16[64,1024]{1,0:T(8,128)(2,1)S(1)} %slice.318), channel_id=1, source_target_pairs={{0,4},{1,5},{2,6},{3,7},{4,0},{5,1},{6,2},{7,3},{8,12},{9,13},{10,... | collective-permute-start | bytes 393224 | tf_op jit(solution)/shard_map/ppermute | solution.py:268
  148.3 5.0 %collective-permute-start.38 = (bf16[64,1024]{1,0:T(8,128)(2,1)S(1)}, bf16[64,1024]{1,0:T(8,128)(2,1)S(1)}, u32[]{:S(2)}, u32[]{:S(2)}) collective-permute-start(bf16[64,1024]{1,0:T(8,128)(2,1)S(1)} %slice.319), channel_id=1, source_target_pairs={{0,2},{1,3},{2,0},{3,1},{4,6},{5,7},{6,4},{7,5},{8,10},{9,11},{10,... | collective-permute-start | bytes 393224 | tf_op jit(solution)/shard_map/ppermute | solution.py:268
  170.4 9.0 %all-to-all-start = ((f32[8,1,768]{2,1,0:T(1,128)}), f32[8,1,768]{2,1,0:T(1,128)S(1)}, u32[]{:S(2)}, u32[]{:S(2)}) async-start(f32[8,1,768]{2,1,0:T(1,128)} %all_to_all.16), calls=%async_computation | async-start | bytes 49152 | tf_op jit(solution)/shard_map/all_to_all | solution.py:471
  173.8 54.6 %reduce-scatter.3.cloned.1.call-start = ((), (), s32[]{:S(2)}) async-start(), calls=%async_computation.6 | async-start | bytes 1310720 | tf_op jit(solution)/shard_map/reduce_scatter | solution.py:468
  173.9 20.9 %collective-permute-start.40 = (bf16[4,128,1024]{2,1,0:T(8,128)(2,1)}, bf16[4,128,1024]{2,1,0:T(8,128)(2,1)}, u32[]{:S(2)}, u32[]{:S(2)}) collective-permute-start(bf16[4,128,1024]{2,1,0:T(8,128)(2,1)} %copy-done.7), channel_id=1, source_target_pairs={{0,1},{1,0},{2,3},{3,2},{4,5},{5,4},{6,7},{7,6},{8,9},{9,8},{10,11... | collective-permute-start | bytes 3145736 | tf_op jit(solution)/shard_map/ppermute | solution.py:268
  179.5 6.9 %collective-permute-start.45 = (f32[3584]{0:T(1024)S(1)}, f32[3584]{0:T(1024)S(1)}, u32[]{:S(2)}, u32[]{:S(2)}) collective-permute-start(f32[3584]{0:T(1024)S(1)} %constant_dynamic-update-slice_fusion.33), channel_id=1, source_target_pairs={{0,8},{8,16},{16,24},{24,0},{1,9},{9,17},{17,25},{25,1},{2,10},{10... | collective-permute-start | bytes 43016 | tf_op jit(solution)/shard_map/ppermute | solution.py:335
  180.7 5.7 %collective-permute-start.46 = (f32[3584]{0:T(1024)S(1)}, f32[3584]{0:T(1024)S(1)}, u32[]{:S(2)}, u32[]{:S(2)}) collective-permute-start(f32[3584]{0:T(1024)S(1)} %constant_dynamic-update-slice_fusion.33), channel_id=1, source_target_pairs={{0,16},{8,24},{16,0},{24,8},{1,17},{9,25},{17,1},{25,9},{2,18},{10... | collective-permute-start | bytes 43016 | tf_op jit(solution)/shard_map/ppermute | solution.py:335
  187.4 15.5 %all-to-all-start.1 = ((f32[8,1,128]{2,1,0:T(1,128)}), f32[8,1,128]{2,1,0:T(1,128)S(1)}, u32[]{:S(2)}, u32[]{:S(2)}) async-start(f32[8,1,128]{2,1,0:T(1,128)} %bitcast.18), calls=%async_computation.1 | async-start | bytes 8192 | tf_op jit(solution)/shard_map/all_to_all | solution.py:485
  198.0 8.8 %collective-permute-start.41 = (bf16[2,128,512]{2,1,0:T(8,128)(2,1)S(1)}, bf16[2,128,512]{2,1,0:T(8,128)(2,1)S(1)}, u32[]{:S(2)}, u32[]{:S(2)}) collective-permute-start(bf16[2,128,512]{2,1,0:T(8,128)(2,1)S(1)} %pad_maximum_fusion.9), channel_id=1, source_target_pairs={{0,2},{1,3},{2,0},{3,1},{4,6},{5,7},{6,4},{7,5},{8,10},{9,11},{10,... | collective-permute-start | bytes 786440 | tf_op jit(solution)/shard_map/ppermute | solution.py:268
  200.1 8.1 %collective-permute-start.43 = (bf16[2,128,512]{2,1,0:T(8,128)(2,1)S(1)}, bf16[2,128,512]{2,1,0:T(8,128)(2,1)S(1)}, u32[]{:S(2)}, u32[]{:S(2)}) collective-permute-start(bf16[2,128,512]{2,1,0:T(8,128)(2,1)S(1)} %stack.84), channel_id=1, source_target_pairs={{0,4},{1,5},{2,6},{3,7},{4,0},{5,1},{6,2},{7,3},{8,12},{9,13},{10,... | collective-permute-start | bytes 786440 | tf_op jit(solution)/shard_map/ppermute | solution.py:268
  202.9 8.5 %collective-permute-start.48 = (f32[1,128]{1,0:T(1,128)S(1)}, f32[1,128]{1,0:T(1,128)S(1)}, u32[]{:S(2)}, u32[]{:S(2)}) collective-permute-start(f32[1,128]{1,0:T(1,128)S(1)} %bitcast.66), channel_id=1, source_target_pairs={{0,0},{1,1},{2,24},{3,25},{4,16},{5,17},{6,8},{7,9},{8,10},{9,11},... | collective-permute-start | bytes 1544 | tf_op jit(solution)/shard_map/ppermute | solution.py:486
  209.2 5.0 %collective-permute-start.42 = (bf16[1,128,512]{2,1,0:T(8,128)(2,1)S(1)}, bf16[1,128,512]{2,1,0:T(8,128)(2,1)S(1)}, u32[]{:S(2)}, u32[]{:S(2)}) collective-permute-start(bf16[1,128,512]{2,1,0:T(8,128)(2,1)S(1)} %get-tuple-element.178), channel_id=1, source_target_pairs={{0,4},{1,5},{2,6},{3,7},{4,0},{5,1},{6,2},{7,3},{8,12},{9,13},{10,... | collective-permute-start | bytes 393224 | tf_op jit(solution)/shard_map/ppermute | solution.py:268
  210.8 5.0 %collective-permute-start.44 = (bf16[1,128,512]{2,1,0:T(8,128)(2,1)S(1)}, bf16[1,128,512]{2,1,0:T(8,128)(2,1)S(1)}, u32[]{:S(2)}, u32[]{:S(2)}) collective-permute-start(bf16[1,128,512]{2,1,0:T(8,128)(2,1)S(1)} %get-tuple-element.179), channel_id=1, source_target_pairs={{0,2},{1,3},{2,0},{3,1},{4,6},{5,7},{6,4},{7,5},{8,10},{9,11},{10,... | collective-permute-start | bytes 393224 | tf_op jit(solution)/shard_map/ppermute | solution.py:268
  (44 other events, 243.0 us)
Sparse Core Ops, SparseCore 0:
  10.2 31.3 all-gather.3
  43.7 44.9 all-gather.5
  118.5 42.6 reduce-scatter.4
  186.5 26.4 reduce-scatter.2

commit v2 on v1

v2 whole, which is shorter than its diff:
```python
import functools

import jax
import jax.numpy as jnp
from jax import lax
from jax.experimental import pallas as pl
from jax.experimental.pallas import tpu as pltpu
from jax.sharding import PartitionSpec as P

HD = 64
STEP = 10
LN_EPS = 1e-06
GELU_C = 0.7978845608028654
GELU_K = 0.044715
BETA_ONE = 0.9
BETA_TWO = 0.95
ADAM_EPS = 1e-08
DECAY = 0.1
LR_SCALE = 2.0
LR_BIAS = 0.2
BF = jnp.bfloat16
F32 = jnp.float32
MIB = 1024 * 1024


def dot(left, right, left_dim=1, right_dim=0):
    return lax.dot_general(
        left, right, (((left_dim,), (right_dim,)), ((), ())), preferred_element_type=F32
    )


def normalize(values):
    center = values - jnp.mean(values, -1, keepdims=True)
    inv_std = lax.rsqrt(jnp.mean(center * center, -1, keepdims=True) + LN_EPS)
    return (center * inv_std, inv_std)


def norm_back(grad_n, normed, inv_std):
    return inv_std * (
        grad_n
        - jnp.mean(grad_n, -1, keepdims=True)
        - normed * jnp.mean(grad_n * normed, -1, keepdims=True)
    )


def gelu_pair(values):
    square = values * values
    inner = GELU_C * (values + GELU_K * square * values)
    tanh_val = jnp.tanh(inner)
    half = 0.5 * (1.0 + tanh_val)
    result = values * half
    slope = half + 0.5 * values * (1.0 - tanh_val * tanh_val) * GELU_C * (
        1.0 + 3.0 * GELU_K * square
    )
    return (result, slope)


def full(shape):
    return pl.BlockSpec(shape, lambda *_: (0,) * len(shape))


def rows_of(count, width):
    return pl.BlockSpec((count, width), lambda i, *_: (i, 0))


def call(body, grid, in_specs, out_specs, out_shape, args, scratch=(), scalar=None, flops=0, nbytes=0, near=False):
    params = pltpu.CompilerParams(vmem_limit_bytes=(16 if near else 56) * MIB)
    cost = pl.CostEstimate(flops=flops, bytes_accessed=nbytes, transcendentals=0)
    if near:
        args = [pltpu.with_memory_space_constraint(a, pltpu.VMEM) for a in args]
    if scalar is None:
        return pl.pallas_call(
            body, grid=grid, in_specs=in_specs, out_specs=out_specs, out_shape=out_shape,
            scratch_shapes=list(scratch), compiler_params=params, cost_estimate=cost,
        )(*args)
    spec = pltpu.PrefetchScalarGridSpec(
        num_scalar_prefetch=1, grid=grid, in_specs=in_specs, out_specs=out_specs,
        scratch_shapes=list(scratch),
    )
    return pl.pallas_call(
        body, grid_spec=spec, out_shape=out_shape, compiler_params=params, cost_estimate=cost,
    )(scalar, *args)


def far_shape(dims, dtype):
    return pltpu.HBM(dims, dtype)


def shape(dims, dtype):
    return jax.ShapeDtypeStruct(dims, dtype)


def mod_body(count, s_ref, *refs):
    small = refs[:count]
    w_ref, part_ref, silu_ref, low_ref = refs[count:]
    share = w_ref.shape[0]
    at = pl.ds(pl.multiple_of(s_ref[1] * share, share), share)
    low = w_ref[...].astype(BF)
    silu = jnp.concatenate([r[:, at] for r in small], axis=0).astype(BF)
    low_ref[...] = low
    silu_ref[...] = silu
    part_ref[...] = dot(silu, low)


def pack_first_body(qkv_ref, proj_ref, out_ref):
    width = qkv_ref.shape[1]
    out_ref[:, :width] = qkv_ref[...].astype(BF)
    out_ref[:, width:] = proj_ref[...].T.astype(BF)


def pack_body(up_ref, down_ref, out_ref):
    share, hidden = up_ref.shape
    for n in range(hidden // share):
        out_ref[n * share : (n + 1) * share, :] = up_ref[:, n * share : (n + 1) * share].astype(BF)
    out_ref[hidden:, :] = down_ref[...].astype(BF)


def unpack_first_body(first_ref, w_ref, proj_ref):
    width = w_ref.shape[1]
    w_ref[...] = first_ref[:, :width]
    proj_ref[...] = first_ref[:, width:].T


def enter_body(x_ref, mod_ref, bias_ref, w_ref, min_ref, qkv_ref):
    normed, _ = normalize(x_ref[...].astype(F32))
    low = (normed * (1.0 + mod_ref[1:2, :]) + mod_ref[0:1, :]).astype(BF)
    min_ref[...] = low
    qkv_ref[...] = (dot(low, w_ref[...]) + bias_ref[...]).astype(BF)


def attend_body(blk_ref, qkv_ref, out_ref, lse_ref):
    heads = lse_ref.shape[0]
    outs = []
    blk = blk_ref[...]
    allr = qkv_ref[...]
    for h in range(heads):
        base = h * 3 * HD
        query = blk[:, base : base + HD] * BF(HD ** (-0.5))
        key = allr[:, base + HD : base + 2 * HD]
        value = allr[:, base + 2 * HD : base + 3 * HD]
        scores = dot(key, query, 1, 1)
        highest = jnp.max(scores, 0, keepdims=True)
        expon = jnp.exp(scores - highest)
        totals = jnp.sum(expon, 0, keepdims=True)
        out = dot(value, expon.astype(BF), 0, 0) * (1.0 / totals)
        outs.append(out.T.astype(BF))
        lse_ref[h : h + 1, :] = highest + jnp.log(totals)
    out_ref[...] = outs[0] if heads == 1 else jnp.concatenate(outs, axis=1)


def middle_body(count, rows, s_ref, *refs):
    att = refs[:count]
    proj = refs[count : 2 * count]
    x_ref, mod_ref, bias_ref, min_ref, br_ref, proj_s, br_s = refs[2 * count :]
    block = x_ref.shape[0]
    step = pl.program_id(0)

    @pl.when(step == 0)
    def _():
        at = 0
        for ref in proj:
            proj_s[at : at + ref.shape[0], :] = ref[...]
            at += ref.shape[0]

    joined = jnp.concatenate([ref[...] for ref in att], axis=1)
    branch = dot(joined, proj_s[...]) + bias_ref[...]
    resid = x_ref[...].astype(F32) + mod_ref[2:3, :] * branch
    normed, _ = normalize(resid)
    min_ref[...] = (normed * (1.0 + mod_ref[4:5, :]) + mod_ref[3:4, :]).astype(BF)
    start = s_ref[0] * rows

    @pl.when(step == start // block)
    def _():
        br_s[...] = branch
        br_ref[...] = br_s[pl.ds(pl.multiple_of(start % block, rows), rows), :]


def store_pair(odd, value, rows, keep_ref, send_ref):
    low, high = value[:rows], value[rows:]
    keep_ref[0] = jnp.where(odd, high, low)
    send_ref[0] = jnp.where(odd, low, high)


def mlp_body(rows, s_ref, in_ref, cot_ref, mod_ref, bias_ref, pack_ref,
             act_ref, dpre_ref, keep_ref, send_ref, keep2_ref, send2_ref, upsum_ref, downsum_ref, outsum_ref,
             down_s, up_s):
    planes, _, share = pack_ref.shape
    hidden = act_ref.shape[1]

    @pl.when(pl.program_id(0) == 0)
    def _():
        for plane in range(planes):
            at = slice(plane * share, (plane + 1) * share)
            for n in range(hidden // share):
                up_s[at, n * share : (n + 1) * share] = pack_ref[plane, n * share : (n + 1) * share, :]
            down_s[:, at] = pack_ref[plane, hidden:, :]
        upsum_ref[...] = jnp.zeros_like(upsum_ref)
        downsum_ref[...] = jnp.zeros_like(downsum_ref)
        outsum_ref[...] = jnp.zeros_like(outsum_ref)

    up = up_s[...]
    down = down_s[...]
    odd = s_ref[0] % 2 == 1
    cot = cot_ref[...].astype(F32)
    pre = dot(in_ref[...], up) + bias_ref[...]
    act, slope = gelu_pair(pre)
    act = act.astype(BF)
    act_ref[...] = act
    grad_b = (cot * mod_ref[5:6, :]).astype(BF)
    dpre = (dot(grad_b, down, 1, 1) * slope).astype(BF)
    dpre_ref[...] = dpre
    store_pair(odd, dot(dpre, up, 1, 1).astype(BF), rows, keep_ref, send_ref)
    part = dot(act, down)
    store_pair(odd, part.astype(BF), rows, keep2_ref, send2_ref)
    outsum_ref[...] += jnp.sum(cot * part, 0, keepdims=True)
    upsum_ref[...] += jnp.sum(dpre.astype(F32), 0, keepdims=True)
    downsum_ref[...] += jnp.sum(grad_b.astype(F32), 0, keepdims=True)


def mlp_grad_body(in_ref, dpre_ref, act_ref, cot_ref, mod_ref, out_ref):
    hidden = act_ref.shape[1]
    share = in_ref.shape[1]
    up = dot(in_ref[...], dpre_ref[...], 0, 0).astype(BF)
    for n in range(hidden // share):
        out_ref[0, n * share : (n + 1) * share, :] = up[:, n * share : (n + 1) * share]
    grad_b = (cot_ref[...].astype(F32) * mod_ref[5:6, :]).astype(BF)
    out_ref[0, hidden:, :] = dot(act_ref[...], grad_b, 0, 0).astype(BF)


def first_grad_body(s_ref, in_ref, dqkv_ref, proj_ref, out_ref):
    width = dqkv_ref.shape[1]
    out_ref[0, :, :width] = dot(in_ref[...], dqkv_ref[...], 0, 0).astype(BF)
    out_ref[0, :, width:] = proj_ref[...]


def split_left(total, keep_ref, send_ref):
    for n in range(keep_ref.shape[0]):
        keep_ref[n] = total[2 * n]
        send_ref[n] = total[2 * n + 1].astype(BF)


def split_right(total, keep_ref, send_ref):
    count = keep_ref.shape[0]
    for n in range(count):
        keep_ref[n] = total[n]
        send_ref[n] = total[count + n].astype(BF)


def fold_first_body(keep_ref, got_ref, lk_ref, ls_ref, rk_ref, rs_ref):
    half = lk_ref.shape[2]
    total = keep_ref[...].astype(F32) + got_ref[...].astype(F32)
    split_left(total[:, :, :half], lk_ref, ls_ref)
    split_right(total[:, :, half:], rk_ref, rs_ref)


def fold_next_body(left_ref, lgot_ref, right_ref, rgot_ref, lk_ref, ls_ref, rk_ref, rs_ref):
    split_left(left_ref[...] + lgot_ref[...].astype(F32), lk_ref, ls_ref)
    split_right(right_ref[...] + rgot_ref[...].astype(F32), rk_ref, rs_ref)


def fold_last(refs):
    left, lgot, right, rgot = refs
    return jnp.concatenate(
        [left[0] + lgot[0].astype(F32), right[0] + rgot[0].astype(F32)], axis=1
    )


def between_body(*refs):
    x_ref, mod_ref, cot_ref, br_ref, dres_ref, dbr_ref, res_ref, sums_ref = refs[4:]
    din = fold_last(refs[:4])
    resid = x_ref[...].astype(F32) + mod_ref[2:3, :] * br_ref[...]
    res_ref[...] = resid
    normed, inv = normalize(resid)
    dres = cot_ref[...].astype(F32) + norm_back(din * (1.0 + mod_ref[4:5, :]), normed, inv)
    dres_ref[...] = dres
    dbr_ref[...] = (mod_ref[2:3, :] * dres).astype(BF)
    sums_ref[0:1, :] = jnp.sum(dres * br_ref[...], 0, keepdims=True)
    sums_ref[1:2, :] = jnp.sum(din, 0, keepdims=True)
    sums_ref[2:3, :] = jnp.sum(din * normed, 0, keepdims=True)


def output_body(*refs):
    bias_ref, res_ref, mod_ref, out_ref = refs[4:]
    branch = fold_last(refs[:4]) + bias_ref[...]
    out_ref[...] = res_ref[...] + mod_ref[5:6, :] * branch


def attend_back_body(count, rows, s_ref, *refs):
    dbr = refs[:count]
    (proj_ref, qkv_ref, lse_ref, att_ref, out_ref, colsum_ref, projsum_ref, projgrad_ref,
     datt, acc) = refs[count:]
    heads = lse_ref.shape[0]
    seq = qkv_ref.shape[0]
    block = lse_ref.shape[1]
    step = pl.program_id(0)

    @pl.when(step == 0)
    def _():
        total = jnp.zeros(projsum_ref.shape, F32)
        grad = jnp.zeros(projgrad_ref.shape, F32)
        for r in range(count):
            block_in = dbr[r][...]
            at = pl.ds(pl.multiple_of((s_ref[0] ^ r) * rows, rows), rows)
            datt[at, :] = dot(block_in, proj_ref[...], 1, 1).astype(BF)
            total += jnp.sum(block_in.astype(F32), 0, keepdims=True)
            grad += dot(block_in, att_ref[at, :], 0, 0)
        projgrad_ref[...] = grad.astype(BF)
        projsum_ref[...] = total
        acc[...] = jnp.zeros_like(acc)

    here = pl.ds(pl.multiple_of(step * block, block), block)
    blk = qkv_ref[here, :]
    allr = qkv_ref[...]
    grads = datt[here, :]
    for h in range(heads):
        base = h * 3 * HD
        query = blk[:, base : base + HD] * BF(HD ** (-0.5))
        key = allr[:, base + HD : base + 2 * HD]
        value = allr[:, base + 2 * HD : base + 3 * HD]
        grad = grads[:, h * HD : (h + 1) * HD]
        prob = jnp.exp(dot(key, query, 1, 1) - lse_ref[h : h + 1, :])
        dprob = dot(value, grad, 1, 1)
        weighted = jnp.sum(prob * dprob, 0, keepdims=True)
        dscore = (prob * (dprob - weighted)).astype(BF)
        acc[3 * h, here, :] = dot(key, dscore, 0, 0).T * HD ** (-0.5)
        acc[3 * h + 1] += dot(dscore, query)
        acc[3 * h + 2] += dot(prob.astype(BF), grad)

    @pl.when(step == seq // block - 1)
    def _():
        result = jnp.concatenate([acc[n] for n in range(3 * heads)], axis=1).astype(BF)
        out_ref[...] = result
        colsum_ref[...] = jnp.sum(result.astype(F32), 0, keepdims=True)


def leave_body(rows, s_ref, dqkv_ref, w_ref, x_ref, keep_ref, send_ref, sums_ref):
    part = dot(dqkv_ref[...], w_ref[...], 1, 1)
    store_pair(s_ref[0] % 2 == 1, part.astype(BF), rows, keep_ref, send_ref)
    normed, _ = normalize(x_ref[...].astype(F32))

    @pl.when(pl.program_id(0) == 0)
    def _():
        sums_ref[...] = jnp.zeros_like(sums_ref)

    sums_ref[0:1, :] += jnp.sum(part, 0, keepdims=True)
    sums_ref[1:2, :] += jnp.sum(part * normed, 0, keepdims=True)


def last_body(*refs):
    x_ref, mod_ref, dres_ref, out_ref = refs[4:]
    normed, inv = normalize(x_ref[...].astype(F32))
    din = fold_last(refs[:4])
    out_ref[...] = dres_ref[...] + norm_back(din * (1.0 + mod_ref[1:2, :]), normed, inv)


def adam_step(weight, first, second, grad, rate, decay):
    first_new = BETA_ONE * first + (1.0 - BETA_ONE) * grad
    second_new = BETA_TWO * second + (1.0 - BETA_TWO) * grad * grad
    fix_one = 1.0 - BETA_ONE**STEP
    fix_two = 1.0 - BETA_TWO**STEP
    step_dir = first_new / fix_one / (jnp.sqrt(second_new / fix_two) + ADAM_EPS)
    return (second_new, weight - rate * (step_dir + decay * weight))


def adam_store(grad, w_ref, m_ref, v_ref, grad_ref, second_ref, new_ref, rate):
    grad_ref[...] = grad
    second, new = adam_step(w_ref[...], m_ref[...], v_ref[...], grad, rate, DECAY)
    second_ref[...] = second
    new_ref[...] = new


def adam_first_body(count, rate_qkv, rate_proj, *refs):
    width = refs[count].shape[1]
    grad = refs[0][...].astype(F32)
    for k in range(1, count):
        grad += refs[k][...].astype(F32)
    args, outs = refs[count : count + 6], refs[count + 6 :]
    adam_store(grad[:, :width], *args[:3], *outs[:3], rate_qkv)
    adam_store(grad[:, width:].T, *args[3:], *outs[3:], rate_proj)


def adam_ada_body(rate, silu_ref, dmod_ref, *refs):
    adam_store(dot(silu_ref[...], dmod_ref[...], 0, 0), *refs, rate)


def adam_mlp_body(rate_up, rate_down, gup_ref, gdown_ref, *refs):
    adam_store(gup_ref[...].astype(F32), *refs[0:3], *refs[6:9], rate_up)
    adam_store(gdown_ref[...].astype(F32), *refs[3:6], *refs[9:12], rate_down)


def swap(value, mask, size):
    return lax.ppermute(value, "tensor", [(i, i ^ mask) for i in range(size)])


def spread_first(block, size):
    return swap(block, 2, size), swap(block, 4, size), swap(block, 1, size)


def spread_second(near, size):
    by_x, by_y, _ = near
    return swap(by_x, 4, size), swap(by_x, 1, size), swap(by_y, 1, size)


def spread_third(block, near, more, size):
    by_x, by_y, core = near
    diag, core_x, core_y = more
    return [block, core, by_x, core_x, by_y, core_y, diag, swap(diag, 1, size)]


def spread(block, size):
    if size == 8:
        near = spread_first(block, size)
        return spread_third(block, near, spread_second(near, size), size)
    have = {0: block}
    bit = 1
    while bit < size:
        for r in list(have):
            have[r ^ bit] = swap(have[r], bit, size)
        bit *= 2
    return [have[r] for r in range(size)]


def fold(keep, send, size, beside=None):
    got = swap(send, 1, size)
    count, rows, width = keep.shape
    half = width // 2
    left = right = None
    stage = 0
    while count > 1:
        count //= 2
        dims = (count, rows, half)
        outs = [shape(dims, F32), shape(dims, BF)] * 2
        specs = [full(dims)] * 4
        if left is None:
            args, body = (keep, got), fold_first_body
        else:
            args, body = (left, lgot, right, rgot), fold_next_body
        left, lsend, right, rsend = call(
            body, (1,), [full(a.shape) for a in args], specs, outs, args,
            nbytes=20 * count * rows * width, near=True,
        )
        lgot = swap(lsend, 2 << stage, size)
        rgot = swap(rsend, (size // 2) >> stage, size)
        if beside is not None and stage == 0:
            done = beside(left)
            left, lgot, right, rgot, done = lax.optimization_barrier((left, lgot, right, rgot, done))
        stage += 1
    if beside is not None:
        return (left, lgot, right, rgot), done
    return left, lgot, right, rgot


def shards(
    inputs, conditioning, cotangent, w_ada, w_qkv, w_proj, w_fc1, w_fc2, col_bias, row_bias,
    m_ada, v_ada, m_qkv, v_qkv, m_proj, v_proj, m_fc1, v_fc1, m_fc2, v_fc2, m_col, v_col, m_row, v_row,
):
    T = lax.axis_size("tensor")
    G = lax.axis_size("dp")
    t = lax.axis_index("tensor")
    z = lax.axis_index("dp")
    S, D = inputs.shape
    rows = S // T
    hc = w_proj.shape[0]
    heads = hc // HD
    F = w_fc1.shape[1]
    ada = w_ada.shape[1]
    share = D // G
    scalar = jnp.stack([t, z]).astype(jnp.int32)
    n_col = col_bias.shape[0]

    def around(value, k):
        return lax.ppermute(value, "dp", [(i, (i + k) % G) for i in range(G)])

    def from_planes(value):
        return [value] + [around(value, k) for k in range(1, G)]

    first = call(
        pack_first_body, (1,), [full((share, 3 * hc)), full((hc, share))], full((share, 4 * hc)),
        shape((share, 4 * hc), BF), (w_qkv, w_proj), nbytes=24 * hc * share,
    )
    pack = call(
        pack_body, (1,), [full((share, F)), full((F, share))], full((2 * F, share)),
        shape((2 * F, share), BF), (w_fc1, w_fc2), nbytes=12 * F * share,
    )
    first_all = lax.all_gather(first, "dp", axis=0, tiled=True)
    pack_all = lax.all_gather(pack, "dp", axis=0, tiled=False)

    cond = conditioning.astype(F32)
    silu = (cond * jax.nn.sigmoid(cond)).astype(BF).astype(F32)
    small = jnp.concatenate(
        [silu, col_bias.astype(BF).astype(F32).reshape(1, -1), row_bias.astype(BF).astype(F32).reshape(1, -1)],
        axis=1,
    )
    small_rel = from_planes(small)
    part, silu_own, ada_low = call(
        functools.partial(mod_body, G), (1,),
        [full(small.shape)] * G + [full((share, ada))],
        [full((G, ada)), full((G, share)), full((share, ada))],
        [shape((G, ada), F32), shape((G, share), BF), shape((share, ada), BF)],
        (*small_rel, w_ada), scalar=scalar, nbytes=8 * share * ada, near=True,
    )
    bias_rev = jnp.concatenate(small_rel[::-1] * 2, axis=0)[:, D:]
    bias_abs = lax.dynamic_slice_in_dim(bias_rev, G - 1 - z, G, 0)
    cols = bias_abs[:, :n_col].reshape(-1)
    bias_rows = bias_abs[:, n_col:].reshape(G, 2, share).transpose(1, 0, 2).reshape(2, D)
    bias_up = cols[ada + 2 * hc :].reshape(1, F)
    bias_qkv = jnp.stack(
        [cols[ada : ada + hc].reshape(heads, HD), jnp.zeros((heads, HD), F32),
         cols[ada + hc : ada + 2 * hc].reshape(heads, HD)], axis=1,
    ).reshape(1, 3 * hc)
    mod_part = part[0:1] + cols[:ada].reshape(1, ada)
    for k in range(1, G):
        mod_part = mod_part + around(part[k : k + 1], G - k)
    mod = lax.all_gather(mod_part, "tensor", axis=1, tiled=True).reshape(6, D)

    first_all, mod = lax.optimization_barrier((first_all, mod))
    w_qkv_all, proj_own = call(
        unpack_first_body, (1,), [full((D, 4 * hc))],
        [full((D, 3 * hc)), full((hc, D))], [shape((D, 3 * hc), BF), shape((hc, D), BF)],
        (first_all,), nbytes=20 * hc * D,
    )

    blk = min(256, S)
    steps = (S // blk,)
    mod_in1, qkv = call(
        enter_body, steps,
        [rows_of(blk, D), full((6, D)), full((1, 3 * hc)), full((D, 3 * hc))],
        [rows_of(blk, D), rows_of(blk, 3 * hc)],
        [far_shape((S, D), BF), shape((S, 3 * hc), BF)],
        (inputs, mod, bias_qkv, w_qkv_all), flops=2 * S * D * 3 * hc, nbytes=6 * S * D,
    )
    attended, lse = call(
        attend_body, steps,
        [rows_of(blk, 3 * hc), full((S, 3 * hc))],
        [rows_of(blk, hc), pl.BlockSpec((heads, blk), lambda i: (0, i))],
        [shape((S, hc), BF), shape((heads, S), F32)],
        (qkv, qkv), flops=16 * S * S * hc, nbytes=4 * S * hc,
    )
    if T == 8:
        proj_near, _ = lax.optimization_barrier((spread_first(proj_own, T), qkv))
        proj_more, attended = lax.optimization_barrier((spread_second(proj_near, T), attended))
        proj_all = spread_third(proj_own, proj_near, proj_more, T)
    else:
        proj_all = spread(proj_own, T)
    att_rel = spread(attended, T)
    mod_in2, branch1 = call(
        functools.partial(middle_body, T, rows), steps,
        [rows_of(blk, hc)] * T + [full((hc, D))] * T + [rows_of(blk, D), full((6, D)), full((1, D))],
        [rows_of(blk, D), full((rows, D))],
        [far_shape((S, D), BF), shape((rows, D), F32)],
        (*att_rel, *proj_all, inputs, mod, bias_rows[0:1]),
        scratch=[pltpu.VMEM((T * hc, D), BF), pltpu.VMEM((blk, D), F32)],
        scalar=scalar, flops=2 * S * D * D, nbytes=8 * S * D,
    )

    pair = 2 * rows
    pairs = (T // 2,)
    place_pair = pl.BlockSpec((1, rows, D), lambda i, s_ref: (i ^ (s_ref[0] // 2), 0, 0))
    halves = [shape((T // 2, rows, D), BF)] * 2
    activ, dpre, keep, send, keep2, send2, up_sum, down_sum, out_sum = call(
        functools.partial(mlp_body, rows), pairs,
        [rows_of(pair, D), rows_of(pair, D), full((6, D)), full((1, F))]
        + [full((G, 2 * F, share))],
        [rows_of(pair, F), rows_of(pair, F)] + [place_pair] * 4 + [full((1, F)), full((1, D)), full((1, D))],
        [far_shape((S, F), BF), far_shape((S, F), BF), *halves, *halves, shape((1, F), F32),
         shape((1, D), F32), shape((1, D), F32)],
        (mod_in2, cotangent, mod, bias_up, pack_all),
        scratch=[pltpu.VMEM((F, D), BF), pltpu.VMEM((D, F), BF)],
        scalar=scalar, flops=8 * S * D * F, nbytes=12 * S * D,
    )
    def mlp_grads(after):
        late, _ = lax.optimization_barrier((dpre, after))
        return call(
            mlp_grad_body, (G,),
            [pl.BlockSpec((S, share), lambda i: (0, i)), full((S, F)), full((S, F)),
             pl.BlockSpec((S, share), lambda i: (0, i)), pl.BlockSpec((6, share), lambda i: (0, i))],
            pl.BlockSpec((1, 2 * F, share), lambda i: (i, 0, 0)), far_shape((G, 2 * F, share), BF),
            (mod_in2, late, activ, cotangent, mod), flops=4 * S * D * F, nbytes=8 * S * D,
        )

    din2, mlp_grad = fold(keep, send, T, mlp_grads)
    mlp_grad = lax.psum_scatter(mlp_grad.reshape(G * 2 * F, share), "dp", scatter_dimension=0, tiled=True)
    cot_rows = lax.dynamic_slice_in_dim(cotangent, t * rows, rows, 0)
    x_rows = lax.dynamic_slice_in_dim(inputs, t * rows, rows, 0)
    half = [full((1, rows, D // 2))] * 4
    own = full((rows, D))
    dres1, dbranch1, resid1, sums_mid = call(
        between_body, (1,), half + [own, full((6, D)), own, own], [own, own, own, full((3, D))],
        [shape((rows, D), F32), shape((rows, D), BF), shape((rows, D), F32), shape((3, D), F32)],
        (*din2, x_rows, mod, cot_rows, branch1), nbytes=24 * rows * D, near=True,
    )
    dbr_rel = spread(dbranch1, T)
    dqkv, qkv_sum, proj_sum, proj_grad = call(
        functools.partial(attend_back_body, T, rows), steps,
        [own] * T + [full((hc, D)), full((S, 3 * hc)), pl.BlockSpec((heads, blk), lambda i, *_: (0, i)),
                                         full((S, hc))],
        [full((S, 3 * hc)), full((1, 3 * hc)), full((1, D)), full((D, hc))],
        [shape((S, 3 * hc), BF), shape((1, 3 * hc), F32), shape((1, D), F32), shape((D, hc), BF)],
        (*dbr_rel, proj_own, qkv, lse, attended),
        scratch=[pltpu.VMEM((S, hc), BF), pltpu.VMEM((3 * heads, S, HD), F32)],
        scalar=scalar, flops=40 * S * S * hc, nbytes=6 * S * D,
    )
    keep1, send1, sums_in = call(
        functools.partial(leave_body, rows), pairs,
        [rows_of(pair, 3 * hc), full((D, 3 * hc)), rows_of(pair, D)],
        [place_pair, place_pair, full((2, D))],
        [*halves, shape((2, D), F32)],
        (dqkv, w_qkv_all, inputs), scalar=scalar, flops=6 * S * D * hc, nbytes=6 * S * D,
    )
    first_grad = call(
        first_grad_body, (G,),
        [pl.BlockSpec((S, share), lambda i, s_ref: (0, (i + s_ref[1]) % G)), full((S, 3 * hc)),
         pl.BlockSpec((share, hc), lambda i, s_ref: ((i + s_ref[1]) % G, 0))],
        pl.BlockSpec((1, share, 4 * hc), lambda i, *_: (i, 0, 0)), shape((G, share, 4 * hc), BF),
        (mod_in1, dqkv, proj_grad), scalar=scalar, flops=6 * S * D * hc, nbytes=4 * S * D,
    )

    sums_out = out_sum + bias_rows[1:2] * jnp.sum(cot_rows.astype(F32), 0, keepdims=True)
    dmod = jnp.concatenate([sums_in, sums_mid, sums_out], axis=0).reshape(T, ada)
    dmod = jnp.sum(lax.all_to_all(dmod, "tensor", 0, 0, tiled=True), 0)
    qkv_sum = qkv_sum.reshape(heads, 3, HD)
    message = jnp.concatenate(
        [dmod.astype(BF).astype(F32), qkv_sum[:, 0].reshape(-1), qkv_sum[:, 2].reshape(-1),
         up_sum.reshape(-1), proj_sum.reshape(-1), down_sum.reshape(-1)]
    ).reshape(1, -1)
    message_rel = jnp.concatenate(from_planes(message), axis=0)
    first_grad, message_rel, mlp_grad, keep1, keep2, send2 = lax.optimization_barrier(
        (first_grad, message_rel, mlp_grad, keep1, keep2, send2)
    )
    first_grads = [first_grad[0]] + [around(first_grad[k], k) for k in range(1, G)]
    din1 = fold(keep1, send1, T)
    input_grad = call(
        last_body, (1,), half + [own, full((6, D)), own], own, shape((rows, D), F32),
        (*din1, x_rows, mod, dres1), nbytes=14 * rows * D, near=True,
    )

    block_out = call(
        output_body, (1,), half + [full((1, D)), own, full((6, D))], own, shape((rows, D), F32),
        (*fold(keep2, send2, T), bias_rows[1:2], resid1, mod), nbytes=14 * rows * D, near=True,
    )
    dmod_rel = message_rel[:, :ada].astype(BF)
    bias_sum = jnp.sum(message_rel, 0)
    col_sum = lax.dynamic_slice_in_dim(bias_sum[: G * n_col], z * n_col, n_col, 0)
    row_sum = lax.dynamic_slice_in_dim(bias_sum[G * n_col :].reshape(2, D), z * share, share, 1)
    per = T // G
    grad_silu = dot(dmod_rel, ada_low, 1, 1).reshape(T, D // T)
    grad_silu = jnp.sum(lax.all_to_all(grad_silu, "tensor", 0, 0, tiled=True), 0, keepdims=True)
    grad_silu = lax.ppermute(
        grad_silu, ("dp", "tensor"),
        [(a * T + b, ((a - b // per) % G) * T + a * per + b % per) for a in range(G) for b in range(T)],
    )
    cond_here = lax.dynamic_slice_in_dim(cond, t * (D // T), D // T, 1)
    sig_here = jax.nn.sigmoid(cond_here)
    cond_grad = grad_silu * sig_here * (1.0 + cond_here * (1.0 - sig_here))

    wide = LR_SCALE * D ** (-0.5)
    chunk = ada // 3
    by_chunk = pl.BlockSpec((share, chunk), lambda i: (0, i))
    ada_out = call(
        functools.partial(adam_ada_body, wide), (3,),
        [full((G, share)), pl.BlockSpec((G, chunk), lambda i: (0, i))] + [by_chunk] * 3,
        [by_chunk] * 3, [far_shape((share, ada), F32)] * 3,
        (silu_own, dmod_rel, w_ada, m_ada, v_ada), nbytes=24 * share * ada,
    )
    wide_block, flat = full((share, 3 * hc)), full((hc, share))
    first_out = call(
        functools.partial(adam_first_body, G, wide, LR_SCALE * (D // 32) ** (-0.5)), (1,),
        [full((share, 4 * hc))] * G + [wide_block] * 3 + [flat] * 3, [wide_block] * 3 + [flat] * 3,
        [far_shape((share, 3 * hc), F32)] * 3 + [far_shape((hc, share), F32)] * 3,
        (*first_grads, w_qkv, m_qkv, v_qkv, w_proj, m_proj, v_proj), nbytes=32 * share * 4 * hc,
    )
    chunks = F // share
    square = (share, share)
    up_block = pl.BlockSpec(square, lambda i: (0, i))
    down_block = pl.BlockSpec(square, lambda i: (i, 0))
    mlp_out = call(
        functools.partial(adam_mlp_body, wide, LR_SCALE * (F * T) ** (-0.5)), (chunks,),
        [down_block, pl.BlockSpec(square, lambda i: (chunks + i, 0))] + [up_block] * 3 + [down_block] * 3,
        [up_block] * 3 + [down_block] * 3,
        [far_shape((share, F), F32)] * 3 + [far_shape((F, share), F32)] * 3,
        (mlp_grad, mlp_grad, w_fc1, m_fc1, v_fc1, w_fc2, m_fc2, v_fc2), nbytes=52 * share * F,
    )
    col_second, col_new = adam_step(col_bias, m_col, v_col, col_sum, LR_BIAS, 0.0)
    row_second, row_new = adam_step(row_bias, m_row, v_row, row_sum, LR_BIAS, 0.0)
    return (
        block_out, input_grad, cond_grad, *ada_out, *first_out, *mlp_out,
        col_sum, col_second, col_new, row_sum, row_second, row_new,
    )


def solution(mesh):
    by_cols = P("dp", "tensor")
    by_rows = P("tensor", "dp")
    column = P(("tensor", "dp"))
    row = P(None, "dp")
    tokens = P("dp", None)
    weights = (by_cols, by_cols, by_rows, by_cols, by_rows, column, row)
    moments = tuple(spec for spec in weights for _ in range(2))
    results = tuple(spec for spec in weights for _ in range(3))
    mine = P(("dp", "tensor"), None)
    return jax.shard_map(
        shards,
        mesh=mesh,
        in_specs=(tokens, tokens, tokens, *weights, *moments),
        out_specs=(mine, mine, by_cols, *results),
        check_vma=False,
    )
```

time: 241 us -> 235 us (0.975)
  Pallas kernels: 42.4 us -> 89.3 us
  other arithmetic: 35.7 us -> 4.64 us
  local copies, waits for them, and re-layouts: 41.9 us -> 16.2 us
  matrix products: 12.4 us -> 1.17 us
  starting transfers between devices: 50.5 us -> 59.7 us
  waiting for transfers between devices: 33.1 us -> 39.2 us
    pallas_call x4 -> x18, Pallas kernels: 12.4 us -> 43.4 us  [call(): pl.pallas_call(body, grid=grid, in_specs=in_specs, out_specs=out_specs, o...]
    unnamed x120 -> x114, local copies, waits for them, and re-layouts: 35.6 us -> 8.09 us
    pallas_call x5 -> x6, Pallas kernels: 30 us -> 45.9 us  [call(): pl.pallas_call(body, grid_spec=spec, out_shape=out_shape, compiler_params...]
    dot_general x7 -> x1, matrix products: 12.4 us -> 1.17 us  [dot(): lax.dot_general(left, right, (((left_dim,), (right_dim,)), ((), ())), pre...]
    convert_element_type x9 -> x2, other arithmetic: 8.34 us -> 0.02 us  [the longest x1 0.02 us: shards(): silu = (cond * jax.nn.sigmoid(cond)).astype(BF).astype(F32)]
    another operation x7 -> x1, other arithmetic: 6.85 us -> 0.07 us  [shards(): scalar = jnp.stack([t, z]).astype(jnp.int32)]
    concatenate x8 -> x2, other arithmetic: 5.41 us -> 0.07 us  [the longest x1 0.06 us: shards(): message_rel = jnp.concatenate(from_planes(message), axis=0)]
    sub x6 -> x2, other arithmetic: 6.28 us -> 1.28 us  [adam_step(): return (second_new, weight - rate * (step_dir + decay * weight))]
  transfers between devices with their start and end apart: 55 -> 54, of which waited for: 19 -> 19; matrix products, arithmetic and copies ran while one was open for 31% -> 6% of each run, Pallas kernels for 14% -> 33%
where the time goes in v2:
time: 235 us; the launch traced here: 234 us
  Pallas kernels  89.3 us (38%)
  starting transfers between devices  59.7 us (25%)
  waiting for transfers between devices  39.2 us (17%)
  local copies, waits for them, and re-layouts  16.2 us (7%)
  between operations  14.6 us (6%)
  blocking collectives  9.05 us (4%)
  other arithmetic  4.64 us (2%)
    pallas_call x6, Pallas kernels, call(): pl.pallas_call(body, grid_spec=spec, out_shape=out_shape, compiler_params...  45.9 us
    pallas_call x18, Pallas kernels, call(): pl.pallas_call(body, grid=grid, in_specs=in_specs, out_specs=out_specs, o...  43.4 us
    ppermute x36, starting transfers between devices, swap(): return lax.ppermute(value, 'tensor', [(i, i ^ mask) for i in range(size)])  32.8 us
    ppermute x36, waiting for transfers between devices, swap(): return lax.ppermute(value, 'tensor', [(i, i ^ mask) for i in range(size)])  29.1 us
    ppermute x12, starting transfers between devices, around(): return lax.ppermute(value, 'dp', [(i, (i + k) % G) for i in range(G)])  19 us
    all_gather x1, blocking collectives, shards(): mod = lax.all_gather(mod_part, 'tensor', axis=1, tiled=True).reshape(6, D)  9.05 us
    unnamed x114, local copies, waits for them, and re-layouts  8.09 us
    ppermute x12, waiting for transfers between devices, around(): return lax.ppermute(value, 'dp', [(i, (i + k) % G) for i in range(G)])  5.44 us
  transfers between devices with their start and end apart: 54, of which 19 were waited for; matrix products, arithmetic and copies ran while one was open for 6% of the time, Pallas kernels for 33%

profile of v2, /device:TPU:0, one launch (start us, length us, event | category | flops | bytes accessed | tf_op | source)
XLA Modules:
  0.0 233.9 jit_solution(8229744910443971368)
XLA Ops:
  7.3 1.9 shard_map.415
  9.3 2.0 shard_map.421
  11.5 3.1 %collective-permute-start = (f32[1,1920]{1,0:T(1,128)S(1)}, f32[1,1920]{1,0:T(1,128)S(1)}, u32[]{:S(2)}, u32[]{:S(2)}) collective-permute-start(f32[1,1920]{1,0:T(1,128)S(1)} %maximum_convert_fusion.refs_0_), channel_id=1, source_target_pairs={{0,8},{8,16},{16,24},{24,0},{1,9},{9,17},{17,25},{25,1},{2,10},{10... | collective-permute-start | bytes 23048 | tf_op jit(solution)/shard_map/ppermute | solution.py:472
  14.6 2.6 %collective-permute-start.1 = (f32[1,1920]{1,0:T(1,128)S(1)}, f32[1,1920]{1,0:T(1,128)S(1)}, u32[]{:S(2)}, u32[]{:S(2)}) collective-permute-start(f32[1,1920]{1,0:T(1,128)S(1)} %maximum_convert_fusion.refs_0_), channel_id=1, source_target_pairs={{0,16},{8,24},{16,0},{24,8},{1,17},{9,25},{17,1},{25,9},{2,18},{10... | collective-permute-start | bytes 23048 | tf_op jit(solution)/shard_map/ppermute | solution.py:472
  17.2 1.3 collective-permute-start.2
  19.2 1.6 collective-permute-done.2.refs_3_
  22.4 3.6 %collective-permute-start.4 = (f32[1,768]{1,0:T(1,128)S(1)}, f32[1,768]{1,0:T(1,128)S(1)}, u32[]{:S(2)}, u32[]{:S(2)}) collective-permute-start(f32[1,768]{1,0:T(1,128)S(1)} %get-tuple-element.224), channel_id=1, source_target_pairs={{0,16},{8,24},{16,0},{24,8},{1,17},{9,25},{17,1},{25,9},{2,18},{10... | collective-permute-start | bytes 9224 | tf_op jit(solution)/shard_map/ppermute | solution.py:472
  26.4 1.4 collective-permute-done.5
  27.8 1.9 collective-permute-done.3
  29.7 9.0 %all_gather.13 = f32[1,6144]{1,0:T(1,128)S(1)} all-gather(f32[1,768]{1,0:T(1,128)S(1)} %add_add_fusion), channel_id=1, replica_groups=mesh['dp'=4,'tensor'=8] {'tensor'}, dimensions={1}, use_global_device_ids=true | all-gather | bytes 27648 | tf_op jit(solution)/shard_map/all_gather | solution.py:514
  41.1 2.3 shard_map.417
  43.4 1.5 collective-permute-start.6
  44.9 1.5 collective-permute-start.7
  47.1 5.4 %shard_map.418 = (bf16[1024,1024]{1,0:T(8,128)(2,1)}, bf16[1024,384]{1,0:T(8,128)(2,1)}) custom-call(bf16[1024,1024]{1,0:T(8,128)(2,1)} %x_ref.3, f32[6,1024]{1,0:T(8,128)} %reshape.131.mod_ref.refs_17_.refs_5_.refs_6_, f32[1,384]{1,0:T(1,128)} %reshape.132.bias_ref, bf16[1024,384]{1,0:T(8,128)(2,1)} %get-tuple-element.118.w_ref), custom_call_target="tpu_custom_call" | custom-call | flops 805306368 | bytes 6291456 | tf_op jit(solution)/shard_map/pallas_call | solution.py:72
  52.9 1.4 collective-permute-start.9
  54.8 8.6 %shard_map.419 = (bf16[1024,128]{1,0:T(8,128)(2,1)}, f32[2,1024]{1,0:T(2,128)}) custom-call(bf16[1024,384]{1,0:T(8,128)(2,1)} %get-tuple-element.121.blk_ref.qkv_ref.refs_9_, bf16[1024,384]{1,0:T(8,128)(2,1)} %get-tuple-element.121.blk_ref.qkv_ref.refs_9_), custom_call_target="tpu_custom_call" | custom-call | flops 2147483648 | bytes 524288 | tf_op jit(solution)/shard_map/pallas_call | solution.py:72
  64.7 7.2 %collective-permute-done.13.refs_2_ = bf16[1024,128]{1,0:T(8,128)(2,1)S(1)} collective-permute-done((bf16[1024,128]{1,0:T(8,128)(2,1)}, bf16[1024,128]{1,0:T(8,128)(2,1)S(1)}, u32[]{:S(2)}, u32[]{:S(2)}) %collective-permute-start.13) | collective-permute-done | bytes 262176 | tf_op jit(solution)/shard_map/ppermute | solution.py:392
  73.6 5.8 %collective-permute-done.17.refs_6_ = bf16[1024,128]{1,0:T(8,128)(2,1)S(1)} collective-permute-done((bf16[1024,128]{1,0:T(8,128)(2,1)S(1)}, bf16[1024,128]{1,0:T(8,128)(2,1)S(1)}, u32[]{:S(2)}, u32[]{:S(2)}) %collective-permute-start.17) | collective-permute-done | bytes 262176 | tf_op jit(solution)/shard_map/ppermute | solution.py:392
  81.7 8.5 %shard_map.420 = (bf16[1024,1024]{1,0:T(8,128)(2,1)}, f32[128,1024]{1,0:T(8,128)}) custom-call(s32[2]{0:T(128)} %copy-done.15, bf16[1024,128]{1,0:T(8,128)(2,1)} %get-tuple-element.125.refs_0_.refs_11_, bf16[1024,128]{1,0:T(8,128)(2,1)} %copy-done.40, bf16[1024,128]{1,0:T(8,128)(2,1)} %copy-done.37, bf16[1024,128]{1,0:T(8,128)(2,1)} %copy-done.44, ...), custom_call_target="tpu_custom_call" | custom-call | flops 2147483648 | bytes 8388608 | tf_op jit(solution)/shard_map/pallas_call | solution.py:80
  90.3 10.2 %shard_map.422 = (bf16[1024,512]{1,0:T(8,128)(2,1)}, bf16[1024,512]{1,0:T(8,128)(2,1)}, bf16[4,128,1024]{2,1,0:T(8,128)(2,1)}, bf16[4,128,1024]{2,1,0:T(8,128)(2...) custom-call(s32[2]{0:T(128)} %copy-done.15, ...), custom_call_target="tpu_custom_call" | custom-call | flops 4294967296 | bytes 12582912 | tf_op jit(solution)/shard_map/pallas_call | solution.py:80
  101.0 2.5 %collective-permute-done.20.got_ref = bf16[4,128,1024]{2,1,0:T(8,128)(2,1)S(1)} collective-permute-done((bf16[4,128,1024]{2,1,0:T(8,128)(2,1)}, bf16[4,128,1024]{2,1,0:T(8,128)(2,1)S(1)}, u32[]{:S(2)}, u32[]{:S(2)}) %collective-permute-start.20) | collective-permute-done | bytes 1048608 | tf_op jit(solution)/shard_map/ppermute | solution.py:392
  106.2 6.6 %shard_map.424 = bf16[4,1024,256]{2,1,0:T(8,128)(2,1)} custom-call(bf16[1024,1024]{1,0:T(8,128)(2,1)} %get-tuple-element.130.in_ref, bf16[1024,512]{1,0:T(8,128)(2,1)} %get-tuple-element.138.dpre_ref, bf16[1024,512]{1,0:T(8,128)(2,1)} %get-tuple-element.139.act_ref, bf16[1024,1024]{1,0:T(8,128)(2,1)} %cot_ref.3, ...), custom_call_target="tpu_custom_call" | custom-call | flops 2147483648 | bytes 8388608 | tf_op jit(solution)/shard_map/pallas_call | solution.py:72
  114.7 1.5 collective-permute-start.24
  121.8 1.5 collective-permute-start.26
  123.3 1.4 collective-permute-start.28
  124.7 3.8 %collective-permute-done.26.refs_2_ = bf16[128,1024]{1,0:T(8,128)(2,1)S(1)} collective-permute-done((bf16[128,1024]{1,0:T(8,128)(2,1)S(1)}, bf16[128,1024]{1,0:T(8,128)(2,1)S(1)}, u32[]{:S(2)}, u32[]{:S(2)}) %collective-permute-start.26) | collective-permute-done | bytes 262176 | tf_op jit(solution)/shard_map/ppermute | solution.py:392
  130.5 4.8 %collective-permute-done.30.refs_6_ = bf16[128,1024]{1,0:T(8,128)(2,1)S(1)} collective-permute-done((bf16[128,1024]{1,0:T(8,128)(2,1)S(1)}, bf16[128,1024]{1,0:T(8,128)(2,1)S(1)}, u32[]{:S(2)}, u32[]{:S(2)}) %collective-permute-start.30) | collective-permute-done | bytes 262176 | tf_op jit(solution)/shard_map/ppermute | solution.py:392
  135.4 1.4 collective-permute-done.31.refs_7_
  137.6 14.5 %shard_map.427 = (bf16[1024,384]{1,0:T(8,128)(2,1)}, f32[1,384]{1,0:T(1,128)}, f32[1,1024]{1,0:T(1,128)}, bf16[1024,128]{1,0:T(8,128)(2,1)}) custom-call(s32[2]{0:T(128)} %copy-done.15, bf16[128,1024]{1,0:T(8,128)(2,1)} %copy-done.17, bf16[128,1024]{1,0:T(8,128)(2,1)} %copy-done.47, bf16[128,1024]{1,0:T(8,128)(2,1)} %copy-done.41, ...), custom_call_target="tpu_custom_call" | custom-call | flops 5368709120 | bytes 6291456 | tf_op jit(solution)/shard_map/pallas_call | solution.py:80
  152.1 6.4 %shard_map.429 = (bf16[4,128,1024]{2,1,0:T(8,128)(2,1)}, bf16[4,128,1024]{2,1,0:T(8,128)(2,1)}, f32[2,1024]{1,0:T(2,128)}) custom-call(s32[2]{0:T(128)} %copy-done.15, bf16[1024,384]{1,0:T(8,128)(2,1)} %get-tuple-element.151.dqkv_ref, bf16[1024,384]{1,0:T(8,128)(2,1)} %get-tuple-element.118.w_ref, bf16[1024,1024]{1,0:T(8,128)(2,1)} %x_ref.3), custom_call_target="tpu_custom_call" | custom-call | flops 805306368 | bytes 6291456 | tf_op jit(solution)/shard_map/pallas_call | solution.py:80
  159.8 3.3 %all-to-all-start = ((f32[8,1,768]{2,1,0:T(1,128)}), f32[8,1,768]{2,1,0:T(1,128)S(1)}, u32[]{:S(2)}, u32[]{:S(2)}) async-start(f32[8,1,768]{2,1,0:T(1,128)} %all_to_all.16), calls=%async_computation | async-start | bytes 49152 | tf_op jit(solution)/shard_map/all_to_all | solution.py:620
  163.9 4.0 %all-to-all-done = f32[8,1,768]{2,1,0:T(1,128)S(1)} async-done(((f32[8,1,768]{2,1,0:T(1,128)}), f32[8,1,768]{2,1,0:T(1,128)S(1)}, u32[]{:S(2)}, u32[]{:S(2)}) %all-to-all-start) | async-done | bytes 24608 | tf_op jit(solution)/shard_map/all_to_all | solution.py:620
  168.1 2.2 collective-permute-start.34
  171.0 1.2 collective-permute-start.32
  172.2 5.6 %shard_map.428 = bf16[4,256,512]{2,1,0:T(8,128)(2,1)} custom-call(s32[2]{0:T(128)} %copy-done.15, bf16[1024,1024]{1,0:T(8,128)(2,1)} %get-tuple-element.119.in_ref, bf16[1024,384]{1,0:T(8,128)(2,1)} %get-tuple-element.151.dqkv_ref, bf16[1024,128]{1,0:T(8,128)(2,1)} %get-tuple-element.152.proj_ref), custom_call_target="tpu_custom_call" | custom-call | flops 805306368 | bytes 4194304 | tf_op jit(solution)/shard_map/pallas_call | solution.py:80
  183.6 3.7 %all-to-all-start.1 = ((f32[8,1,128]{2,1,0:T(1,128)}), f32[8,1,128]{2,1,0:T(1,128)S(1)}, u32[]{:S(2)}, u32[]{:S(2)}) async-start(f32[8,1,128]{2,1,0:T(1,128)} %bitcast.14), calls=%async_computation.2 | async-start | bytes 8192 | tf_op jit(solution)/shard_map/all_to_all | solution.py:647
  187.2 2.2 slice_bitcast_fusion
  189.4 1.6 collective-permute-start.46
  191.0 1.6 collective-permute-start.47
  192.6 1.4 shard_map.430
  194.0 2.1 collective-permute-start.36
  196.1 1.5 collective-permute-start.37
  200.4 4.3 %shard_map.436 = (f32[256,768]{1,0:T(8,128)}, f32[256,768]{1,0:T(8,128)}, f32[256,768]{1,0:T(8,128)}) custom-call(bf16[4,256]{1,0:T(4,128)(2,1)} %copy-done.16, bf16[4,768]{1,0:T(4,128)(2,1)} %slice.126.dmod_ref, f32[256,768]{1,0:T(8,128)} %refs_0_.2, f32[256,768]{1,0:T(8,128)} %refs_1_.2, f32[256,768]{1,0:T(8,128)} %refs_2_.2), custom_call_target="tpu_custom_call" | custom-call | bytes 4718592 | tf_op jit(solution)/shard_map/pallas_call | solution.py:72
  205.5 3.6 %shard_map.438 = (f32[256,512]{1,0:T(8,128)}, f32[256,512]{1,0:T(8,128)}, f32[256,512]{1,0:T(8,128)}, f32[512,256]{1,0:T(8,128)}, f32[512,256]{1,0:T(8,128)}, /*index=5*/f32[512,256]{1,0:T(8,128)}) custom-call(bf16[1024,256]{1,0:T(8,128)(2,1)} %reduce-scatter.2.cloned.1.call-done.gup_ref.gdown_ref, ...), custom_call_target="tpu_custom_call" | custom-call | bytes 6815744 | tf_op jit(solution)/shard_map/pallas_call | solution.py:72
  209.2 4.7 %collective-permute-start.43 = (bf16[1,128,512]{2,1,0:T(8,128)(2,1)S(1)}, bf16[1,128,512]{2,1,0:T(8,128)(2,1)S(1)}, u32[]{:S(2)}, u32[]{:S(2)}) collective-permute-start(bf16[1,128,512]{2,1,0:T(8,128)(2,1)S(1)} %get-tuple-element.182), channel_id=1, source_target_pairs={{0,4},{1,5},{2,6},{3,7},{4,0},{5,1},{6,2},{7,3},{8,12},{9,13},{10,... | collective-permute-start | bytes 393224 | tf_op jit(solution)/shard_map/ppermute | solution.py:392
  214.8 3.8 %collective-permute-start.38 = (bf16[1,128,512]{2,1,0:T(8,128)(2,1)S(1)}, bf16[1,128,512]{2,1,0:T(8,128)(2,1)S(1)}, u32[]{:S(2)}, u32[]{:S(2)}) collective-permute-start(bf16[1,128,512]{2,1,0:T(8,128)(2,1)S(1)} %get-tuple-element.171), channel_id=1, source_target_pairs={{0,4},{1,5},{2,6},{3,7},{4,0},{5,1},{6,2},{7,3},{8,12},{9,13},{10,... | collective-permute-start | bytes 393224 | tf_op jit(solution)/shard_map/ppermute | solution.py:392
  218.7 2.0 collective-permute-start.39
  221.9 3.3 %shard_map.437 = (f32[256,384]{1,0:T(8,128)}, f32[256,384]{1,0:T(8,128)}, f32[256,384]{1,0:T(8,128)}, f32[128,256]{1,0:T(8,128)}, f32[128,256]{1,0:T(8,128)}, /*index=5*/f32[128,256]{1,0:T(8,128)}) custom-call(bf16[256,512]{1,0:T(8,128)(2,1)} %get-tuple-element.219.refs_0_, bf16[256,512]{1,0:T(8,128)(2,1)} %collective-permute-done.46.refs_1_, ...), custom_call_target="tpu_custom_call" | custom-call | bytes 4194304 | tf_op jit(solution)/shard_map/pallas_call | solution.py:72
  (253 shorter events, 41.9 us)
Async XLA Ops:
  7.2 33.9 %all-gather.4.cloned.1.call-start = ((), (), s32[]{:S(2)}) async-start(), calls=%async_computation.3 | async-start | bytes 1310720 | tf_op jit(solution)/shard_map/all_gather | solution.py:485
  9.2 81.1 %all-gather.6.cloned.1.call-start = ((), (), s32[]{:S(2)}) async-start(), calls=%async_computation.5 | async-start | bytes 2621440 | tf_op jit(solution)/shard_map/all_gather | solution.py:486
  11.3 166.6 %reduce-scatter.2.cloned.1.call-start = ((), (), s32[]{:S(2)}) async-start(), calls=%async_computation.4 | async-start | bytes 2621440 | tf_op jit(solution)/shard_map/reduce_scatter | solution.py:582
  11.5 7.2 %collective-permute-start = (f32[1,1920]{1,0:T(1,128)S(1)}, f32[1,1920]{1,0:T(1,128)S(1)}, u32[]{:S(2)}, u32[]{:S(2)}) collective-permute-start(f32[1,1920]{1,0:T(1,128)S(1)} %maximum_convert_fusion.refs_0_), channel_id=1, source_target_pairs={{0,8},{8,16},{16,24},{24,0},{1,9},{9,17},{17,25},{25,1},{2,10},{10... | collective-permute-start | bytes 23048 | tf_op jit(solution)/shard_map/ppermute | solution.py:472
  22.3 5.5 %collective-permute-start.5 = (f32[1,768]{1,0:T(1,128)S(1)}, f32[1,768]{1,0:T(1,128)S(1)}, u32[]{:S(2)}, u32[]{:S(2)}) collective-permute-start(f32[1,768]{1,0:T(1,128)S(1)} %get-tuple-element.223), channel_id=1, source_target_pairs={{0,8},{8,16},{16,24},{24,0},{1,9},{9,17},{17,25},{25,1},{2,10},{10... | collective-permute-start | bytes 9224 | tf_op jit(solution)/shard_map/ppermute | solution.py:472
  22.4 5.4 %collective-permute-start.4 = (f32[1,768]{1,0:T(1,128)S(1)}, f32[1,768]{1,0:T(1,128)S(1)}, u32[]{:S(2)}, u32[]{:S(2)}) collective-permute-start(f32[1,768]{1,0:T(1,128)S(1)} %get-tuple-element.224), channel_id=1, source_target_pairs={{0,16},{8,24},{16,0},{24,8},{1,17},{9,25},{17,1},{25,9},{2,18},{10... | collective-permute-start | bytes 9224 | tf_op jit(solution)/shard_map/ppermute | solution.py:472
  43.4 9.1 %collective-permute-start.6 = (bf16[128,1024]{1,0:T(8,128)(2,1)}, bf16[128,1024]{1,0:T(8,128)(2,1)S(1)}, u32[]{:S(2)}, u32[]{:S(2)}) collective-permute-start(bf16[128,1024]{1,0:T(8,128)(2,1)} %get-tuple-element.120.refs_8_), channel_id=1, source_target_pairs={{0,2},{1,3},{2,0},{3,1},{4,6},{5,7},{6,4},{7,5},{8,10},{9,11},{10,... | collective-permute-start | bytes 786440 | tf_op jit(solution)/shard_map/ppermute | solution.py:392
  44.9 8.0 %collective-permute-start.7 = (bf16[128,1024]{1,0:T(8,128)(2,1)}, bf16[128,1024]{1,0:T(8,128)(2,1)S(1)}, u32[]{:S(2)}, u32[]{:S(2)}) collective-permute-start(bf16[128,1024]{1,0:T(8,128)(2,1)} %get-tuple-element.120.refs_8_), channel_id=1, source_target_pairs={{0,4},{1,5},{2,6},{3,7},{4,0},{5,1},{6,2},{7,3},{8,12},{9,13},{10,... | collective-permute-start | bytes 786440 | tf_op jit(solution)/shard_map/ppermute | solution.py:392
  46.4 6.5 %collective-permute-start.8 = (bf16[128,1024]{1,0:T(8,128)(2,1)}, bf16[128,1024]{1,0:T(8,128)(2,1)S(1)}, u32[]{:S(2)}, u32[]{:S(2)}) collective-permute-start(bf16[128,1024]{1,0:T(8,128)(2,1)} %get-tuple-element.120.refs_8_), channel_id=1, source_target_pairs={{0,1},{1,0},{2,3},{3,2},{4,5},{5,4},{6,7},{7,6},{8,9},{9,8},{10,11... | collective-permute-start | bytes 786440 | tf_op jit(solution)/shard_map/ppermute | solution.py:392
  52.9 10.5 %collective-permute-start.9 = (bf16[128,1024]{1,0:T(8,128)(2,1)S(1)}, bf16[128,1024]{1,0:T(8,128)(2,1)S(1)}, u32[]{:S(2)}, u32[]{:S(2)}) collective-permute-start(bf16[128,1024]{1,0:T(8,128)(2,1)S(1)} %collective-permute-done.6.refs_10_), channel_id=1, source_target_pairs={{0,4},{1,5},{2,6},{3,7},{4,0},{5,1},{6,2},{7,3},{8,12},{9,13},{10,... | collective-permute-start | bytes 786440 | tf_op jit(solution)/shard_map/ppermute | solution.py:392
  54.3 9.1 %collective-permute-start.10 = (bf16[128,1024]{1,0:T(8,128)(2,1)S(1)}, bf16[128,1024]{1,0:T(8,128)(2,1)S(1)}, u32[]{:S(2)}, u32[]{:S(2)}) collective-permute-start(bf16[128,1024]{1,0:T(8,128)(2,1)S(1)} %collective-permute-done.6.refs_10_), channel_id=1, source_target_pairs={{0,1},{1,0},{2,3},{3,2},{4,5},{5,4},{6,7},{7,6},{8,9},{9,8},{10,11... | collective-permute-start | bytes 786440 | tf_op jit(solution)/shard_map/ppermute | solution.py:392
  54.3 9.1 %collective-permute-start.11 = (bf16[128,1024]{1,0:T(8,128)(2,1)S(1)}, bf16[128,1024]{1,0:T(8,128)(2,1)S(1)}, u32[]{:S(2)}, u32[]{:S(2)}) collective-permute-start(bf16[128,1024]{1,0:T(8,128)(2,1)S(1)} %collective-permute-done.7.refs_12_), channel_id=1, source_target_pairs={{0,1},{1,0},{2,3},{3,2},{4,5},{5,4},{6,7},{7,6},{8,9},{9,8},{10,11... | collective-permute-start | bytes 786440 | tf_op jit(solution)/shard_map/ppermute | solution.py:392
  63.4 8.5 %collective-permute-start.13 = (bf16[1024,128]{1,0:T(8,128)(2,1)}, bf16[1024,128]{1,0:T(8,128)(2,1)S(1)}, u32[]{:S(2)}, u32[]{:S(2)}) collective-permute-start(bf16[1024,128]{1,0:T(8,128)(2,1)} %get-tuple-element.125.refs_0_.refs_11_), channel_id=1, source_target_pairs={{0,2},{1,3},{2,0},{3,1},{4,6},{5,7},{6,4},{7,5},{8,10},{9,11},{10,... | collective-permute-start | bytes 786440 | tf_op jit(solution)/shard_map/ppermute | solution.py:392
  64.1 8.9 %collective-permute-start.15 = (bf16[1024,128]{1,0:T(8,128)(2,1)}, bf16[1024,128]{1,0:T(8,128)(2,1)S(1)}, u32[]{:S(2)}, u32[]{:S(2)}) collective-permute-start(bf16[1024,128]{1,0:T(8,128)(2,1)} %get-tuple-element.125.refs_0_.refs_11_), channel_id=1, source_target_pairs={{0,4},{1,5},{2,6},{3,7},{4,0},{5,1},{6,2},{7,3},{8,12},{9,13},{10,... | collective-permute-start | bytes 786440 | tf_op jit(solution)/shard_map/ppermute | solution.py:392
  71.9 7.5 %collective-permute-start.17 = (bf16[1024,128]{1,0:T(8,128)(2,1)S(1)}, bf16[1024,128]{1,0:T(8,128)(2,1)S(1)}, u32[]{:S(2)}, u32[]{:S(2)}) collective-permute-start(bf16[1024,128]{1,0:T(8,128)(2,1)S(1)} %collective-permute-done.13.refs_2_), channel_id=1, source_target_pairs={{0,4},{1,5},{2,6},{3,7},{4,0},{5,1},{6,2},{7,3},{8,12},{9,13},{10,... | collective-permute-start | bytes 786440 | tf_op jit(solution)/shard_map/ppermute | solution.py:392
  72.6 8.1 %collective-permute-start.12 = (bf16[1024,128]{1,0:T(8,128)(2,1)}, bf16[1024,128]{1,0:T(8,128)(2,1)S(1)}, u32[]{:S(2)}, u32[]{:S(2)}) collective-permute-start(bf16[1024,128]{1,0:T(8,128)(2,1)} %get-tuple-element.125.refs_0_.refs_11_), channel_id=1, source_target_pairs={{0,1},{1,0},{2,3},{3,2},{4,5},{5,4},{6,7},{7,6},{8,9},{9,8},{10,11... | collective-permute-start | bytes 786440 | tf_op jit(solution)/shard_map/ppermute | solution.py:392
  72.6 8.1 %collective-permute-start.19 = (bf16[128,1024]{1,0:T(8,128)(2,1)S(1)}, bf16[128,1024]{1,0:T(8,128)(2,1)S(1)}, u32[]{:S(2)}, u32[]{:S(2)}) collective-permute-start(bf16[128,1024]{1,0:T(8,128)(2,1)S(1)} %collective-permute-done.9.refs_14_), channel_id=1, source_target_pairs={{0,1},{1,0},{2,3},{3,2},{4,5},{5,4},{6,7},{7,6},{8,9},{9,8},{10,11... | collective-permute-start | bytes 786440 | tf_op jit(solution)/shard_map/ppermute | solution.py:392
  73.1 7.6 %collective-permute-start.14 = (bf16[1024,128]{1,0:T(8,128)(2,1)S(1)}, bf16[1024,128]{1,0:T(8,128)(2,1)S(1)}, u32[]{:S(2)}, u32[]{:S(2)}) collective-permute-start(bf16[1024,128]{1,0:T(8,128)(2,1)S(1)} %collective-permute-done.13.refs_2_), channel_id=1, source_target_pairs={{0,1},{1,0},{2,3},{3,2},{4,5},{5,4},{6,7},{7,6},{8,9},{9,8},{10,11... | collective-permute-start | bytes 786440 | tf_op jit(solution)/shard_map/ppermute | solution.py:392
  73.1 7.6 %collective-permute-start.16 = (bf16[1024,128]{1,0:T(8,128)(2,1)S(1)}, bf16[1024,128]{1,0:T(8,128)(2,1)S(1)}, u32[]{:S(2)}, u32[]{:S(2)}) collective-permute-start(bf16[1024,128]{1,0:T(8,128)(2,1)S(1)} %collective-permute-done.15.refs_4_), channel_id=1, source_target_pairs={{0,1},{1,0},{2,3},{3,2},{4,5},{5,4},{6,7},{7,6},{8,9},{9,8},{10,11... | collective-permute-start | bytes 786440 | tf_op jit(solution)/shard_map/ppermute | solution.py:392
  105.0 8.7 %collective-permute-start.21 = (bf16[2,128,512]{2,1,0:T(8,128)(2,1)S(1)}, bf16[2,128,512]{2,1,0:T(8,128)(2,1)S(1)}, u32[]{:S(2)}, u32[]{:S(2)}) collective-permute-start(bf16[2,128,512]{2,1,0:T(8,128)(2,1)S(1)} %get-tuple-element.134), channel_id=1, source_target_pairs={{0,2},{1,3},{2,0},{3,1},{4,6},{5,7},{6,4},{7,5},{8,10},{9,11},{10,... | collective-permute-start | bytes 786440 | tf_op jit(solution)/shard_map/ppermute | solution.py:392
  105.6 8.3 %collective-permute-start.22 = (bf16[2,128,512]{2,1,0:T(8,128)(2,1)S(1)}, bf16[2,128,512]{2,1,0:T(8,128)(2,1)S(1)}, u32[]{:S(2)}, u32[]{:S(2)}) collective-permute-start(bf16[2,128,512]{2,1,0:T(8,128)(2,1)S(1)} %get-tuple-element.136), channel_id=1, source_target_pairs={{0,4},{1,5},{2,6},{3,7},{4,0},{5,1},{6,2},{7,3},{8,12},{9,13},{10,... | collective-permute-start | bytes 786440 | tf_op jit(solution)/shard_map/ppermute | solution.py:392
  114.1 5.0 %collective-permute-start.23 = (bf16[1,128,512]{2,1,0:T(8,128)(2,1)S(1)}, bf16[1,128,512]{2,1,0:T(8,128)(2,1)S(1)}, u32[]{:S(2)}, u32[]{:S(2)}) collective-permute-start(bf16[1,128,512]{2,1,0:T(8,128)(2,1)S(1)} %get-tuple-element.145), channel_id=1, source_target_pairs={{0,4},{1,5},{2,6},{3,7},{4,0},{5,1},{6,2},{7,3},{8,12},{9,13},{10,... | collective-permute-start | bytes 393224 | tf_op jit(solution)/shard_map/ppermute | solution.py:392
  114.7 5.0 %collective-permute-start.24 = (bf16[1,128,512]{2,1,0:T(8,128)(2,1)S(1)}, bf16[1,128,512]{2,1,0:T(8,128)(2,1)S(1)}, u32[]{:S(2)}, u32[]{:S(2)}) collective-permute-start(bf16[1,128,512]{2,1,0:T(8,128)(2,1)S(1)} %get-tuple-element.147), channel_id=1, source_target_pairs={{0,2},{1,3},{2,0},{3,1},{4,6},{5,7},{6,4},{7,5},{8,10},{9,11},{10,... | collective-permute-start | bytes 393224 | tf_op jit(solution)/shard_map/ppermute | solution.py:392
  121.8 6.7 %collective-permute-start.26 = (bf16[128,1024]{1,0:T(8,128)(2,1)S(1)}, bf16[128,1024]{1,0:T(8,128)(2,1)S(1)}, u32[]{:S(2)}, u32[]{:S(2)}) collective-permute-start(bf16[128,1024]{1,0:T(8,128)(2,1)S(1)} %get-tuple-element.149.refs_0_), channel_id=1, source_target_pairs={{0,2},{1,3},{2,0},{3,1},{4,6},{5,7},{6,4},{7,5},{8,10},{9,11},{10,... | collective-permute-start | bytes 786440 | tf_op jit(solution)/shard_map/ppermute | solution.py:392
  123.3 7.2 %collective-permute-start.28 = (bf16[128,1024]{1,0:T(8,128)(2,1)S(1)}, bf16[128,1024]{1,0:T(8,128)(2,1)S(1)}, u32[]{:S(2)}, u32[]{:S(2)}) collective-permute-start(bf16[128,1024]{1,0:T(8,128)(2,1)S(1)} %get-tuple-element.149.refs_0_), channel_id=1, source_target_pairs={{0,4},{1,5},{2,6},{3,7},{4,0},{5,1},{6,2},{7,3},{8,12},{9,13},{10,... | collective-permute-start | bytes 786440 | tf_op jit(solution)/shard_map/ppermute | solution.py:392
  128.5 6.8 %collective-permute-start.30 = (bf16[128,1024]{1,0:T(8,128)(2,1)S(1)}, bf16[128,1024]{1,0:T(8,128)(2,1)S(1)}, u32[]{:S(2)}, u32[]{:S(2)}) collective-permute-start(bf16[128,1024]{1,0:T(8,128)(2,1)S(1)} %collective-permute-done.26.refs_2_), channel_id=1, source_target_pairs={{0,4},{1,5},{2,6},{3,7},{4,0},{5,1},{6,2},{7,3},{8,12},{9,13},{10,... | collective-permute-start | bytes 786440 | tf_op jit(solution)/shard_map/ppermute | solution.py:392
  129.6 5.7 %collective-permute-start.25 = (bf16[128,1024]{1,0:T(8,128)(2,1)S(1)}, bf16[128,1024]{1,0:T(8,128)(2,1)S(1)}, u32[]{:S(2)}, u32[]{:S(2)}) collective-permute-start(bf16[128,1024]{1,0:T(8,128)(2,1)S(1)} %get-tuple-element.149.refs_0_), channel_id=1, source_target_pairs={{0,1},{1,0},{2,3},{3,2},{4,5},{5,4},{6,7},{7,6},{8,9},{9,8},{10,11... | collective-permute-start | bytes 786440 | tf_op jit(solution)/shard_map/ppermute | solution.py:392
  129.6 5.7 %collective-permute-start.27 = (bf16[128,1024]{1,0:T(8,128)(2,1)S(1)}, bf16[128,1024]{1,0:T(8,128)(2,1)S(1)}, u32[]{:S(2)}, u32[]{:S(2)}) collective-permute-start(bf16[128,1024]{1,0:T(8,128)(2,1)S(1)} %collective-permute-done.26.refs_2_), channel_id=1, source_target_pairs={{0,1},{1,0},{2,3},{3,2},{4,5},{5,4},{6,7},{7,6},{8,9},{9,8},{10,11... | collective-permute-start | bytes 786440 | tf_op jit(solution)/shard_map/ppermute | solution.py:392
  130.5 4.9 %collective-permute-start.29 = (bf16[128,1024]{1,0:T(8,128)(2,1)S(1)}, bf16[128,1024]{1,0:T(8,128)(2,1)S(1)}, u32[]{:S(2)}, u32[]{:S(2)}) collective-permute-start(bf16[128,1024]{1,0:T(8,128)(2,1)S(1)} %collective-permute-done.28.refs_4_), channel_id=1, source_target_pairs={{0,1},{1,0},{2,3},{3,2},{4,5},{5,4},{6,7},{7,6},{8,9},{9,8},{10,11... | collective-permute-start | bytes 786440 | tf_op jit(solution)/shard_map/ppermute | solution.py:392
  159.8 8.1 %all-to-all-start = ((f32[8,1,768]{2,1,0:T(1,128)}), f32[8,1,768]{2,1,0:T(1,128)S(1)}, u32[]{:S(2)}, u32[]{:S(2)}) async-start(f32[8,1,768]{2,1,0:T(1,128)} %all_to_all.16), calls=%async_computation | async-start | bytes 49152 | tf_op jit(solution)/shard_map/all_to_all | solution.py:620
  163.5 14.6 %collective-permute-start.40 = (bf16[4,128,1024]{2,1,0:T(8,128)(2,1)}, bf16[4,128,1024]{2,1,0:T(8,128)(2,1)S(1)}, u32[]{:S(2)}, u32[]{:S(2)}) collective-permute-start(bf16[4,128,1024]{2,1,0:T(8,128)(2,1)} %get-tuple-element.176), channel_id=1, source_target_pairs={{0,1},{1,0},{2,3},{3,2},{4,5},{5,4},{6,7},{7,6},{8,9},{9,8},{10,11... | collective-permute-start | bytes 3145736 | tf_op jit(solution)/shard_map/ppermute | solution.py:392
  168.1 9.8 %collective-permute-start.34 = (f32[1,3584]{1,0:T(1,128)S(1)}, f32[1,3584]{1,0:T(1,128)S(1)}, u32[]{:S(2)}, u32[]{:S(2)}) collective-permute-start(f32[1,3584]{1,0:T(1,128)S(1)} %reshape.140), channel_id=1, source_target_pairs={{0,24},{8,0},{16,8},{24,16},{1,25},{9,1},{17,9},{25,17},{2,26},{10... | collective-permute-start | bytes 43016 | tf_op jit(solution)/shard_map/ppermute | solution.py:472
  170.3 7.5 %collective-permute-start.33 = (f32[1,3584]{1,0:T(1,128)S(1)}, f32[1,3584]{1,0:T(1,128)S(1)}, u32[]{:S(2)}, u32[]{:S(2)}) collective-permute-start(f32[1,3584]{1,0:T(1,128)S(1)} %reshape.140), channel_id=1, source_target_pairs={{0,16},{8,24},{16,0},{24,8},{1,17},{9,25},{17,1},{25,9},{2,18},{10... | collective-permute-start | bytes 43016 | tf_op jit(solution)/shard_map/ppermute | solution.py:472
  171.0 6.9 %collective-permute-start.32 = (f32[1,3584]{1,0:T(1,128)S(1)}, f32[1,3584]{1,0:T(1,128)S(1)}, u32[]{:S(2)}, u32[]{:S(2)}) collective-permute-start(f32[1,3584]{1,0:T(1,128)S(1)} %reshape.140), channel_id=1, source_target_pairs={{0,8},{8,16},{16,24},{24,0},{1,9},{9,17},{17,25},{25,1},{2,10},{10... | collective-permute-start | bytes 43016 | tf_op jit(solution)/shard_map/ppermute | solution.py:472
  177.9 14.6 %collective-permute-start.35 = (bf16[4,128,1024]{2,1,0:T(8,128)(2,1)}, bf16[4,128,1024]{2,1,0:T(8,128)(2,1)}, u32[]{:S(2)}, u32[]{:S(2)}) collective-permute-start(bf16[4,128,1024]{2,1,0:T(8,128)(2,1)} %get-tuple-element.165), channel_id=1, source_target_pairs={{0,1},{1,0},{2,3},{3,2},{4,5},{5,4},{6,7},{7,6},{8,9},{9,8},{10,11... | collective-permute-start | bytes 3145736 | tf_op jit(solution)/shard_map/ppermute | solution.py:392
  180.5 15.6 %collective-permute-start.41 = (bf16[2,128,512]{2,1,0:T(8,128)(2,1)}, bf16[2,128,512]{2,1,0:T(8,128)(2,1)S(1)}, u32[]{:S(2)}, u32[]{:S(2)}) collective-permute-start(bf16[2,128,512]{2,1,0:T(8,128)(2,1)} %get-tuple-element.178), channel_id=1, source_target_pairs={{0,2},{1,3},{2,0},{3,1},{4,6},{5,7},{6,4},{7,5},{8,10},{9,11},{10,... | collective-permute-start | bytes 786440 | tf_op jit(solution)/shard_map/ppermute | solution.py:392
  181.1 17.2 %collective-permute-start.42 = (bf16[2,128,512]{2,1,0:T(8,128)(2,1)}, bf16[2,128,512]{2,1,0:T(8,128)(2,1)S(1)}, u32[]{:S(2)}, u32[]{:S(2)}) collective-permute-start(bf16[2,128,512]{2,1,0:T(8,128)(2,1)} %get-tuple-element.180), channel_id=1, source_target_pairs={{0,4},{1,5},{2,6},{3,7},{4,0},{5,1},{6,2},{7,3},{8,12},{9,13},{10,... | collective-permute-start | bytes 786440 | tf_op jit(solution)/shard_map/ppermute | solution.py:392
  183.6 21.1 %all-to-all-start.1 = ((f32[8,1,128]{2,1,0:T(1,128)}), f32[8,1,128]{2,1,0:T(1,128)S(1)}, u32[]{:S(2)}, u32[]{:S(2)}) async-start(f32[8,1,128]{2,1,0:T(1,128)} %bitcast.14), calls=%async_computation.2 | async-start | bytes 8192 | tf_op jit(solution)/shard_map/all_to_all | solution.py:647
  189.4 25.4 %collective-permute-start.46 = (bf16[256,512]{1,0:T(8,128)(2,1)}, bf16[256,512]{1,0:T(8,128)(2,1)}, u32[]{:S(2)}, u32[]{:S(2)}) collective-permute-start(bf16[256,512]{1,0:T(8,128)(2,1)} %get-tuple-element.218), channel_id=1, source_target_pairs={{0,8},{8,16},{16,24},{24,0},{1,9},{9,17},{17,25},{25,1},{2,10},{10... | collective-permute-start | bytes 786440 | tf_op jit(solution)/shard_map/ppermute | solution.py:472
  191.0 27.7 %collective-permute-start.47 = (bf16[256,512]{1,0:T(8,128)(2,1)}, bf16[256,512]{1,0:T(8,128)(2,1)}, u32[]{:S(2)}, u32[]{:S(2)}) collective-permute-start(bf16[256,512]{1,0:T(8,128)(2,1)} %get-tuple-element.217), channel_id=1, source_target_pairs={{0,16},{8,24},{16,0},{24,8},{1,17},{9,25},{17,1},{25,9},{2,18},{10... | collective-permute-start | bytes 786440 | tf_op jit(solution)/shard_map/ppermute | solution.py:472
  194.0 10.7 %collective-permute-start.36 = (bf16[2,128,512]{2,1,0:T(8,128)(2,1)S(1)}, bf16[2,128,512]{2,1,0:T(8,128)(2,1)S(1)}, u32[]{:S(2)}, u32[]{:S(2)}) collective-permute-start(bf16[2,128,512]{2,1,0:T(8,128)(2,1)S(1)} %get-tuple-element.167), channel_id=1, source_target_pairs={{0,2},{1,3},{2,0},{3,1},{4,6},{5,7},{6,4},{7,5},{8,10},{9,11},{10,... | collective-permute-start | bytes 786440 | tf_op jit(solution)/shard_map/ppermute | solution.py:392
  196.1 13.1 %collective-permute-start.37 = (bf16[2,128,512]{2,1,0:T(8,128)(2,1)S(1)}, bf16[2,128,512]{2,1,0:T(8,128)(2,1)S(1)}, u32[]{:S(2)}, u32[]{:S(2)}) collective-permute-start(bf16[2,128,512]{2,1,0:T(8,128)(2,1)S(1)} %get-tuple-element.169), channel_id=1, source_target_pairs={{0,4},{1,5},{2,6},{3,7},{4,0},{5,1},{6,2},{7,3},{8,12},{9,13},{10,... | collective-permute-start | bytes 786440 | tf_op jit(solution)/shard_map/ppermute | solution.py:392
  198.3 22.9 %collective-permute-start.48 = (bf16[256,512]{1,0:T(8,128)(2,1)}, bf16[256,512]{1,0:T(8,128)(2,1)S(1)}, u32[]{:S(2)}, u32[]{:S(2)}) collective-permute-start(bf16[256,512]{1,0:T(8,128)(2,1)} %get-tuple-element.216), channel_id=1, source_target_pairs={{0,24},{8,0},{16,8},{24,16},{1,25},{9,1},{17,9},{25,17},{2,26},{10... | collective-permute-start | bytes 786440 | tf_op jit(solution)/shard_map/ppermute | solution.py:472
  204.7 9.3 %collective-permute-start.45 = (f32[1,128]{1,0:T(1,128)S(1)}, f32[1,128]{1,0:T(1,128)S(1)}, u32[]{:S(2)}, u32[]{:S(2)}) collective-permute-start(f32[1,128]{1,0:T(1,128)S(1)} %bitcast.53), channel_id=1, source_target_pairs={{0,0},{1,1},{2,24},{3,25},{4,16},{5,17},{6,8},{7,9},{8,10},{9,11},... | collective-permute-start | bytes 1544 | tf_op jit(solution)/shard_map/ppermute | solution.py:648
  209.2 16.0 %collective-permute-start.43 = (bf16[1,128,512]{2,1,0:T(8,128)(2,1)S(1)}, bf16[1,128,512]{2,1,0:T(8,128)(2,1)S(1)}, u32[]{:S(2)}, u32[]{:S(2)}) collective-permute-start(bf16[1,128,512]{2,1,0:T(8,128)(2,1)S(1)} %get-tuple-element.182), channel_id=1, source_target_pairs={{0,4},{1,5},{2,6},{3,7},{4,0},{5,1},{6,2},{7,3},{8,12},{9,13},{10,... | collective-permute-start | bytes 393224 | tf_op jit(solution)/shard_map/ppermute | solution.py:392
  214.0 11.2 %collective-permute-start.44 = (bf16[1,128,512]{2,1,0:T(8,128)(2,1)S(1)}, bf16[1,128,512]{2,1,0:T(8,128)(2,1)S(1)}, u32[]{:S(2)}, u32[]{:S(2)}) collective-permute-start(bf16[1,128,512]{2,1,0:T(8,128)(2,1)S(1)} %get-tuple-element.184), channel_id=1, source_target_pairs={{0,2},{1,3},{2,0},{3,1},{4,6},{5,7},{6,4},{7,5},{8,10},{9,11},{10,... | collective-permute-start | bytes 393224 | tf_op jit(solution)/shard_map/ppermute | solution.py:392
  214.8 11.6 %collective-permute-start.38 = (bf16[1,128,512]{2,1,0:T(8,128)(2,1)S(1)}, bf16[1,128,512]{2,1,0:T(8,128)(2,1)S(1)}, u32[]{:S(2)}, u32[]{:S(2)}) collective-permute-start(bf16[1,128,512]{2,1,0:T(8,128)(2,1)S(1)} %get-tuple-element.171), channel_id=1, source_target_pairs={{0,4},{1,5},{2,6},{3,7},{4,0},{5,1},{6,2},{7,3},{8,12},{9,13},{10,... | collective-permute-start | bytes 393224 | tf_op jit(solution)/shard_map/ppermute | solution.py:392
  218.7 7.8 %collective-permute-start.39 = (bf16[1,128,512]{2,1,0:T(8,128)(2,1)S(1)}, bf16[1,128,512]{2,1,0:T(8,128)(2,1)S(1)}, u32[]{:S(2)}, u32[]{:S(2)}) collective-permute-start(bf16[1,128,512]{2,1,0:T(8,128)(2,1)S(1)} %get-tuple-element.173), channel_id=1, source_target_pairs={{0,2},{1,3},{2,0},{3,1},{4,6},{5,7},{6,4},{7,5},{8,10},{9,11},{10,... | collective-permute-start | bytes 393224 | tf_op jit(solution)/shard_map/ppermute | solution.py:392
  (58 other events, 439.2 us)
Sparse Core Ops, SparseCore 0:
  10.2 30.8 all-gather.3
  43.3 45.3 all-gather.5
  114.1 42.6 reduce-scatter.1

commit v3 on v2

--- a/solution.py
+++ b/solution.py
@@ -63,11 +63,15 @@
     return pl.BlockSpec((count, width), lambda i, *_: (i, 0))
 
 
-def call(body, grid, in_specs, out_specs, out_shape, args, scratch=(), scalar=None, flops=0, nbytes=0, near=False):
-    params = pltpu.CompilerParams(vmem_limit_bytes=(16 if near else 56) * MIB)
+def call(body, grid, in_specs, out_specs, out_shape, args, scratch=(), scalar=None, flops=0, nbytes=0, near=False, mib=56,
+         far=()):
+    params = pltpu.CompilerParams(vmem_limit_bytes=(16 if near else mib) * MIB)
     cost = pl.CostEstimate(flops=flops, bytes_accessed=nbytes, transcendentals=0)
-    if near:
-        args = [pltpu.with_memory_space_constraint(a, pltpu.VMEM) for a in args]
+    args = [
+        pltpu.with_memory_space_constraint(a, pltpu.HBM) if n in far
+        else pltpu.with_memory_space_constraint(a, pltpu.VMEM) if near else a
+        for n, a in enumerate(args)
+    ]
     if scalar is None:
         return pl.pallas_call(
             body, grid=grid, in_specs=in_specs, out_specs=out_specs, out_shape=out_shape,
@@ -227,30 +231,33 @@
     out_ref[0, hidden:, :] = dot(act_ref[...], grad_b, 0, 0).astype(BF)
 
 
-def first_grad_body(s_ref, in_ref, dqkv_ref, proj_ref, out_ref):
+def first_grad_body(in_ref, dqkv_ref, proj_ref, out_ref):
     width = dqkv_ref.shape[1]
-    out_ref[0, :, :width] = dot(in_ref[...], dqkv_ref[...], 0, 0).astype(BF)
-    out_ref[0, :, width:] = proj_ref[...]
-
-
-def split_left(total, keep_ref, send_ref):
+    out_ref[:, :width] = dot(in_ref[...], dqkv_ref[...], 0, 0).astype(BF)
+    out_ref[:, width:] = proj_ref[...]
+
+
+def split_left(total, keep_ref, send_ref, cols=slice(None)):
     for n in range(keep_ref.shape[0]):
-        keep_ref[n] = total[2 * n]
-        send_ref[n] = total[2 * n + 1].astype(BF)
-
-
-def split_right(total, keep_ref, send_ref):
+        keep_ref[n, :, cols] = total[2 * n]
+        send_ref[n, :, cols] = total[2 * n + 1].astype(BF)
+
+
+def split_right(total, keep_ref, send_ref, cols=slice(None)):
     count = keep_ref.shape[0]
     for n in range(count):
-        keep_ref[n] = total[n]
-        send_ref[n] = total[count + n].astype(BF)
-
-
-def fold_first_body(keep_ref, got_ref, lk_ref, ls_ref, rk_ref, rs_ref):
-    half = lk_ref.shape[2]
-    total = keep_ref[...].astype(F32) + got_ref[...].astype(F32)
-    split_left(total[:, :, :half], lk_ref, ls_ref)
-    split_right(total[:, :, half:], rk_ref, rs_ref)
+        keep_ref[n, :, cols] = total[n]
+        send_ref[n, :, cols] = total[count + n].astype(BF)
+
+
+def fold_first_body(count, *refs):
+    lk_ref, ls_ref, rk_ref, rs_ref = refs[2 * count :]
+    half = refs[0].shape[2] // 2
+    for n in range(count):
+        total = refs[n][...].astype(F32) + refs[count + n][...].astype(F32)
+        cols = slice(n * half, (n + 1) * half)
+        split_left(total[:, :, :half], lk_ref, ls_ref, cols)
+        split_right(total[:, :, half:], rk_ref, rs_ref, cols)
 
 
 def fold_next_body(left_ref, lgot_ref, right_ref, rgot_ref, lk_ref, ls_ref, rk_ref, rs_ref):
@@ -258,10 +265,12 @@
     split_right(right_ref[...] + rgot_ref[...].astype(F32), rk_ref, rs_ref)
 
 
-def fold_last(refs):
+def fold_last(refs, n=0, count=1):
     left, lgot, right, rgot = refs
+    half = left.shape[2] // count
+    cols = slice(n * half, (n + 1) * half)
     return jnp.concatenate(
-        [left[0] + lgot[0].astype(F32), right[0] + rgot[0].astype(F32)], axis=1
+        [left[0, :, cols] + lgot[0, :, cols].astype(F32), right[0, :, cols] + rgot[0, :, cols].astype(F32)], axis=1
     )
 
 
@@ -277,12 +286,6 @@
     sums_ref[0:1, :] = jnp.sum(dres * br_ref[...], 0, keepdims=True)
     sums_ref[1:2, :] = jnp.sum(din, 0, keepdims=True)
     sums_ref[2:3, :] = jnp.sum(din * normed, 0, keepdims=True)
-
-
-def output_body(*refs):
-    bias_ref, res_ref, mod_ref, out_ref = refs[4:]
-    branch = fold_last(refs[:4]) + bias_ref[...]
-    out_ref[...] = res_ref[...] + mod_ref[5:6, :] * branch
 
 
 def attend_back_body(count, rows, s_ref, *refs):
@@ -346,11 +349,12 @@
     sums_ref[1:2, :] += jnp.sum(part * normed, 0, keepdims=True)
 
 
-def last_body(*refs):
-    x_ref, mod_ref, dres_ref, out_ref = refs[4:]
+def finish_body(*refs):
+    x_ref, mod_ref, dres_ref, bias_ref, res_ref, grad_ref, out_ref = refs[4:]
     normed, inv = normalize(x_ref[...].astype(F32))
-    din = fold_last(refs[:4])
-    out_ref[...] = dres_ref[...] + norm_back(din * (1.0 + mod_ref[1:2, :]), normed, inv)
+    din = fold_last(refs[:4], 0, 2)
+    grad_ref[...] = dres_ref[...] + norm_back(din * (1.0 + mod_ref[1:2, :]), normed, inv)
+    out_ref[...] = res_ref[...] + mod_ref[5:6, :] * (fold_last(refs[:4], 1, 2) + bias_ref[...])
 
 
 def adam_step(weight, first, second, grad, rate, decay):
@@ -369,12 +373,10 @@
     new_ref[...] = new
 
 
-def adam_first_body(count, rate_qkv, rate_proj, *refs):
-    width = refs[count].shape[1]
-    grad = refs[0][...].astype(F32)
-    for k in range(1, count):
-        grad += refs[k][...].astype(F32)
-    args, outs = refs[count : count + 6], refs[count + 6 :]
+def adam_first_body(rate_qkv, rate_proj, grad_ref, *refs):
+    args, outs = refs[:6], refs[6:]
+    width = args[0].shape[1]
+    grad = grad_ref[...].astype(F32)
     adam_store(grad[:, :width], *args[:3], *outs[:3], rate_qkv)
     adam_store(grad[:, width:].T, *args[3:], *outs[3:], rate_proj)
 
@@ -420,11 +422,11 @@
     return [have[r] for r in range(size)]
 
 
-def fold(keep, send, size, beside=None):
-    got = swap(send, 1, size)
-    count, rows, width = keep.shape
-    half = width // 2
-    left = right = None
+def fold(keeps, sends, size, beside=None):
+    gots = [swap(send, 1, size) for send in sends]
+    count, rows, width = keeps[0].shape
+    half = width // 2 * len(keeps)
+    left = right = done = None
     stage = 0
     while count > 1:
         count //= 2
@@ -432,12 +434,12 @@
         outs = [shape(dims, F32), shape(dims, BF)] * 2
         specs = [full(dims)] * 4
         if left is None:
-            args, body = (keep, got), fold_first_body
+            args, body, far = (*keeps, *gots), functools.partial(fold_first_body, len(keeps)), range(len(keeps))
         else:
-            args, body = (left, lgot, right, rgot), fold_next_body
+            args, body, far = (left, lgot, right, rgot), fold_next_body, ()
         left, lsend, right, rsend = call(
             body, (1,), [full(a.shape) for a in args], specs, outs, args,
-            nbytes=20 * count * rows * width, near=True,
+            nbytes=40 * count * rows * half, near=True, far=far,
         )
         lgot = swap(lsend, 2 << stage, size)
         rgot = swap(rsend, (size // 2) >> stage, size)
@@ -445,9 +447,7 @@
             done = beside(left)
             left, lgot, right, rgot, done = lax.optimization_barrier((left, lgot, right, rgot, done))
         stage += 1
-    if beside is not None:
-        return (left, lgot, right, rgot), done
-    return left, lgot, right, rgot
+    return (left, lgot, right, rgot), done
 
 
 def shards(
@@ -522,6 +522,8 @@
 
     blk = min(256, S)
     steps = (S // blk,)
+    wide_blk = min(1024, S)
+    wide_steps = (S // wide_blk,)
     mod_in1, qkv = call(
         enter_body, steps,
         [rows_of(blk, D), full((6, D)), full((1, 3 * hc)), full((D, 3 * hc))],
@@ -530,11 +532,11 @@
         (inputs, mod, bias_qkv, w_qkv_all), flops=2 * S * D * 3 * hc, nbytes=6 * S * D,
     )
     attended, lse = call(
-        attend_body, steps,
-        [rows_of(blk, 3 * hc), full((S, 3 * hc))],
-        [rows_of(blk, hc), pl.BlockSpec((heads, blk), lambda i: (0, i))],
+        attend_body, wide_steps,
+        [rows_of(wide_blk, 3 * hc), full((S, 3 * hc))],
+        [rows_of(wide_blk, hc), pl.BlockSpec((heads, wide_blk), lambda i: (0, i))],
         [shape((S, hc), BF), shape((heads, S), F32)],
-        (qkv, qkv), flops=16 * S * S * hc, nbytes=4 * S * hc,
+        (qkv, qkv), flops=16 * S * S * hc, nbytes=4 * S * hc, mib=32,
     )
     if T == 8:
         proj_near, _ = lax.optimization_barrier((spread_first(proj_own, T), qkv))
@@ -578,7 +580,7 @@
             (mod_in2, late, activ, cotangent, mod), flops=4 * S * D * F, nbytes=8 * S * D,
         )
 
-    din2, mlp_grad = fold(keep, send, T, mlp_grads)
+    din2, mlp_grad = fold([keep], [send], T, mlp_grads)
     mlp_grad = lax.psum_scatter(mlp_grad.reshape(G * 2 * F, share), "dp", scatter_dimension=0, tiled=True)
     cot_rows = lax.dynamic_slice_in_dim(cotangent, t * rows, rows, 0)
     x_rows = lax.dynamic_slice_in_dim(inputs, t * rows, rows, 0)
@@ -586,13 +588,13 @@
     own = full((rows, D))
     dres1, dbranch1, resid1, sums_mid = call(
         between_body, (1,), half + [own, full((6, D)), own, own], [own, own, own, full((3, D))],
-        [shape((rows, D), F32), shape((rows, D), BF), shape((rows, D), F32), shape((3, D), F32)],
+        [far_shape((rows, D), F32), shape((rows, D), BF), far_shape((rows, D), F32), shape((3, D), F32)],
         (*din2, x_rows, mod, cot_rows, branch1), nbytes=24 * rows * D, near=True,
     )
     dbr_rel = spread(dbranch1, T)
     dqkv, qkv_sum, proj_sum, proj_grad = call(
-        functools.partial(attend_back_body, T, rows), steps,
-        [own] * T + [full((hc, D)), full((S, 3 * hc)), pl.BlockSpec((heads, blk), lambda i, *_: (0, i)),
+        functools.partial(attend_back_body, T, rows), wide_steps,
+        [own] * T + [full((hc, D)), full((S, 3 * hc)), pl.BlockSpec((heads, wide_blk), lambda i, *_: (0, i)),
                                          full((S, hc))],
         [full((S, 3 * hc)), full((1, 3 * hc)), full((1, D)), full((D, hc))],
         [shape((S, 3 * hc), BF), shape((1, 3 * hc), F32), shape((1, D), F32), shape((D, hc), BF)],
@@ -604,39 +606,33 @@
         functools.partial(leave_body, rows), pairs,
         [rows_of(pair, 3 * hc), full((D, 3 * hc)), rows_of(pair, D)],
         [place_pair, place_pair, full((2, D))],
-        [*halves, shape((2, D), F32)],
-        (dqkv, w_qkv_all, inputs), scalar=scalar, flops=6 * S * D * hc, nbytes=6 * S * D,
-    )
+        [far_shape((T // 2, rows, D), BF)] * 2 + [shape((2, D), F32)],
+        (dqkv, w_qkv_all, inputs), scalar=scalar, flops=6 * S * D * hc, nbytes=6 * S * D, mib=32, far=(2,),
+    )
+    sums_out = out_sum + bias_rows[1:2] * jnp.sum(cot_rows.astype(F32), 0, keepdims=True)
+    dmod = jnp.concatenate([sums_in, sums_mid, sums_out], axis=0).reshape(T, ada)
+    dmod, mlp_grad, keep2, send2 = lax.optimization_barrier((dmod, mlp_grad, keep2, send2))
+    dmod = jnp.sum(lax.all_to_all(dmod, "tensor", 0, 0, tiled=True), 0)
+    dqkv_late, dmod = lax.optimization_barrier((dqkv, dmod))
     first_grad = call(
         first_grad_body, (G,),
-        [pl.BlockSpec((S, share), lambda i, s_ref: (0, (i + s_ref[1]) % G)), full((S, 3 * hc)),
-         pl.BlockSpec((share, hc), lambda i, s_ref: ((i + s_ref[1]) % G, 0))],
-        pl.BlockSpec((1, share, 4 * hc), lambda i, *_: (i, 0, 0)), shape((G, share, 4 * hc), BF),
-        (mod_in1, dqkv, proj_grad), scalar=scalar, flops=6 * S * D * hc, nbytes=4 * S * D,
-    )
-
-    sums_out = out_sum + bias_rows[1:2] * jnp.sum(cot_rows.astype(F32), 0, keepdims=True)
-    dmod = jnp.concatenate([sums_in, sums_mid, sums_out], axis=0).reshape(T, ada)
-    dmod = jnp.sum(lax.all_to_all(dmod, "tensor", 0, 0, tiled=True), 0)
+        [pl.BlockSpec((S, share), lambda i: (0, i)), full((S, 3 * hc)), pl.BlockSpec((share, hc), lambda i: (i, 0))],
+        pl.BlockSpec((share, 4 * hc), lambda i: (i, 0)), far_shape((D, 4 * hc), BF),
+        (mod_in1, dqkv_late, proj_grad), flops=6 * S * D * hc, nbytes=4 * S * D, mib=32, far=(0,),
+    )
+    first_grad = lax.psum_scatter(first_grad, "dp", scatter_dimension=0, tiled=True)
     qkv_sum = qkv_sum.reshape(heads, 3, HD)
     message = jnp.concatenate(
         [dmod.astype(BF).astype(F32), qkv_sum[:, 0].reshape(-1), qkv_sum[:, 2].reshape(-1),
          up_sum.reshape(-1), proj_sum.reshape(-1), down_sum.reshape(-1)]
     ).reshape(1, -1)
     message_rel = jnp.concatenate(from_planes(message), axis=0)
-    first_grad, message_rel, mlp_grad, keep1, keep2, send2 = lax.optimization_barrier(
-        (first_grad, message_rel, mlp_grad, keep1, keep2, send2)
-    )
-    first_grads = [first_grad[0]] + [around(first_grad[k], k) for k in range(1, G)]
-    din1 = fold(keep1, send1, T)
-    input_grad = call(
-        last_body, (1,), half + [own, full((6, D)), own], own, shape((rows, D), F32),
-        (*din1, x_rows, mod, dres1), nbytes=14 * rows * D, near=True,
-    )
-
-    block_out = call(
-        output_body, (1,), half + [full((1, D)), own, full((6, D))], own, shape((rows, D), F32),
-        (*fold(keep2, send2, T), bias_rows[1:2], resid1, mod), nbytes=14 * rows * D, near=True,
+    keep1, message_rel = lax.optimization_barrier((keep1, message_rel))
+    sums, _ = fold([keep1, keep2], [send1, send2], T)
+    input_grad, block_out = call(
+        finish_body, (1,), [full((1, rows, D))] * 4 + [own, full((6, D)), own, full((1, D)), own], [own, own],
+        [far_shape((rows, D), F32)] * 2,
+        (*sums, x_rows, mod, dres1, bias_rows[1:2], resid1), nbytes=28 * rows * D, near=True, far=(6, 8),
     )
     dmod_rel = message_rel[:, :ada].astype(BF)
     bias_sum = jnp.sum(message_rel, 0)
@@ -664,10 +660,10 @@
     )
     wide_block, flat = full((share, 3 * hc)), full((hc, share))
     first_out = call(
-        functools.partial(adam_first_body, G, wide, LR_SCALE * (D // 32) ** (-0.5)), (1,),
-        [full((share, 4 * hc))] * G + [wide_block] * 3 + [flat] * 3, [wide_block] * 3 + [flat] * 3,
+        functools.partial(adam_first_body, wide, LR_SCALE * (D // 32) ** (-0.5)), (1,),
+        [full((share, 4 * hc))] + [wide_block] * 3 + [flat] * 3, [wide_block] * 3 + [flat] * 3,
         [far_shape((share, 3 * hc), F32)] * 3 + [far_shape((hc, share), F32)] * 3,
-        (*first_grads, w_qkv, m_qkv, v_qkv, w_proj, m_proj, v_proj), nbytes=32 * share * 4 * hc,
+        (first_grad, w_qkv, m_qkv, v_qkv, w_proj, m_proj, v_proj), nbytes=32 * share * 4 * hc,
     )
     chunks = F // share
     square = (share, share)

time: 235 us -> 225 us (0.957)
  starting transfers between devices: 59.7 us -> 47.8 us
  waiting for transfers between devices: 39.2 us -> 47.9 us
  Pallas kernels: 89.3 us -> 83.2 us
    pallas_call x6 -> x5, Pallas kernels: 45.9 us -> 36.5 us  [call(): pl.pallas_call(body, grid_spec=spec, out_shape=out_shape, compiler_params...]
    ppermute x36 -> x32, starting transfers between devices: 32.8 us -> 24.1 us  [swap(): return lax.ppermute(value, 'tensor', [(i, i ^ mask) for i in range(size)])]
    all_to_all x1, waiting for transfers between devices: 0.01 us -> 3.93 us  [shards(): lax.all_to_all(grad_silu, 'tensor', 0, 0, tiled=True)]
    ppermute x12 -> x9, starting transfers between devices: 19 us -> 15.6 us  [around(): return lax.ppermute(value, 'dp', [(i, (i + k) % G) for i in range(G)])]
    pallas_call x18 -> x16, Pallas kernels: 43.4 us -> 46.7 us  [call(): pl.pallas_call(body, grid=grid, in_specs=in_specs, out_specs=out_specs, o...]
    ppermute x12 -> x9, waiting for transfers between devices: 5.44 us -> 8.34 us  [around(): return lax.ppermute(value, 'dp', [(i, (i + k) % G) for i in range(G)])]
    unnamed x114 -> x116, local copies, waits for them, and re-layouts: 8.09 us -> 10.9 us
    ppermute x36 -> x32, waiting for transfers between devices: 29.1 us -> 31.2 us  [swap(): return lax.ppermute(value, 'tensor', [(i, i ^ mask) for i in range(size)])]
  transfers between devices with their start and end apart: 54 -> 48, of which waited for: 19 -> 22; matrix products, arithmetic and copies ran while one was open for 6% -> 4% of each run, Pallas kernels for 33% -> 30%
where the time goes in v3:
time: 225 us; the launch traced here: 224 us
  Pallas kernels  83.2 us (37%)
  waiting for transfers between devices  47.9 us (21%)
  starting transfers between devices  47.8 us (21%)
  local copies, waits for them, and re-layouts  16.8 us (7%)
  between operations  14.6 us (6%)
  blocking collectives  9.05 us (4%)
  other arithmetic  3.94 us (2%)
    pallas_call x16, Pallas kernels, call(): pl.pallas_call(body, grid=grid, in_specs=in_specs, out_specs=out_specs, o...  46.7 us
    pallas_call x5, Pallas kernels, call(): pl.pallas_call(body, grid_spec=spec, out_shape=out_shape, compiler_params...  36.5 us
    ppermute x32, waiting for transfers between devices, swap(): return lax.ppermute(value, 'tensor', [(i, i ^ mask) for i in range(size)])  31.2 us
    ppermute x32, starting transfers between devices, swap(): return lax.ppermute(value, 'tensor', [(i, i ^ mask) for i in range(size)])  24.1 us
    ppermute x9, starting transfers between devices, around(): return lax.ppermute(value, 'dp', [(i, (i + k) % G) for i in range(G)])  15.6 us
    unnamed x116, local copies, waits for them, and re-layouts  10.9 us
    all_gather x1, blocking collectives, shards(): mod = lax.all_gather(mod_part, 'tensor', axis=1, tiled=True).reshape(6, D)  9.05 us
    ppermute x9, waiting for transfers between devices, around(): return lax.ppermute(value, 'dp', [(i, (i + k) % G) for i in range(G)])  8.34 us
  transfers between devices with their start and end apart: 48, of which 22 were waited for; matrix products, arithmetic and copies ran while one was open for 4% of the time, Pallas kernels for 30%

profile of v3, /device:TPU:0, one launch (start us, length us, event | category | flops | bytes accessed | tf_op | source)
XLA Modules:
  0.0 223.5 jit_solution(2135298787927531576)
XLA Ops:
  7.3 1.9 shard_map.415
  9.3 2.0 shard_map.421
  11.5 3.1 %collective-permute-start = (f32[1,1920]{1,0:T(1,128)S(1)}, f32[1,1920]{1,0:T(1,128)S(1)}, u32[]{:S(2)}, u32[]{:S(2)}) collective-permute-start(f32[1,1920]{1,0:T(1,128)S(1)} %maximum_convert_fusion.refs_0_), channel_id=1, source_target_pairs={{0,8},{8,16},{16,24},{24,0},{1,9},{9,17},{17,25},{25,1},{2,10},{10... | collective-permute-start | bytes 23048 | tf_op jit(solution)/shard_map/ppermute | solution.py:472
  14.6 2.6 %collective-permute-start.1 = (f32[1,1920]{1,0:T(1,128)S(1)}, f32[1,1920]{1,0:T(1,128)S(1)}, u32[]{:S(2)}, u32[]{:S(2)}) collective-permute-start(f32[1,1920]{1,0:T(1,128)S(1)} %maximum_convert_fusion.refs_0_), channel_id=1, source_target_pairs={{0,16},{8,24},{16,0},{24,8},{1,17},{9,25},{17,1},{25,9},{2,18},{10... | collective-permute-start | bytes 23048 | tf_op jit(solution)/shard_map/ppermute | solution.py:472
  17.2 1.3 collective-permute-start.2
  19.2 1.6 collective-permute-done.2.refs_3_
  23.0 3.2 %collective-permute-start.3 = (f32[1,768]{1,0:T(1,128)S(1)}, f32[1,768]{1,0:T(1,128)S(1)}, u32[]{:S(2)}, u32[]{:S(2)}) collective-permute-start(f32[1,768]{1,0:T(1,128)S(1)} %get-tuple-element.210), channel_id=1, source_target_pairs={{0,24},{8,0},{16,8},{24,16},{1,25},{9,1},{17,9},{25,17},{2,26},{10... | collective-permute-start | bytes 9224 | tf_op jit(solution)/shard_map/ppermute | solution.py:472
  27.5 3.3 %collective-permute-done.4 = f32[1,768]{1,0:T(1,128)S(1)} collective-permute-done((f32[1,768]{1,0:T(1,128)S(1)}, f32[1,768]{1,0:T(1,128)S(1)}, u32[]{:S(2)}, u32[]{:S(2)}) %collective-permute-start.4) | collective-permute-done | bytes 3104 | tf_op jit(solution)/shard_map/ppermute | solution.py:472
  31.7 9.0 %all_gather.13 = f32[1,6144]{1,0:T(1,128)S(1)} all-gather(f32[1,768]{1,0:T(1,128)S(1)} %add_add_fusion), channel_id=1, replica_groups=mesh['dp'=4,'tensor'=8] {'tensor'}, dimensions={1}, use_global_device_ids=true | all-gather | bytes 27648 | tf_op jit(solution)/shard_map/all_gather | solution.py:514
  42.5 2.3 %shard_map.417 = (bf16[1024,384]{1,0:T(8,128)(2,1)}, bf16[128,1024]{1,0:T(8,128)(2,1)}) custom-call(bf16[1024,512]{1,0:T(8,128)(2,1)} %all-gather.4.cloned.1.call-done.first_ref), custom_call_target="tpu_custom_call" | custom-call | bytes 2621440 | tf_op jit(solution)/shard_map/pallas_call | solution.py:76
  44.8 1.5 collective-permute-start.6
  47.6 5.4 %shard_map.418 = (bf16[1024,1024]{1,0:T(8,128)(2,1)}, bf16[1024,384]{1,0:T(8,128)(2,1)}) custom-call(bf16[1024,1024]{1,0:T(8,128)(2,1)} %x_ref.3, f32[6,1024]{1,0:T(8,128)} %reshape.132.mod_ref.refs_17_.refs_5_, f32[1,384]{1,0:T(1,128)} %reshape.133.bias_ref, bf16[1024,384]{1,0:T(8,128)(2,1)} %get-tuple-element.115.w_ref), custom_call_target="tpu_custom_call" | custom-call | flops 805306368 | bytes 6291456 | tf_op jit(solution)/shard_map/pallas_call | solution.py:76
  57.0 3.5 %shard_map.419 = (bf16[1024,128]{1,0:T(8,128)(2,1)S(1)}, f32[2,1024]{1,0:T(2,128)S(1)}) custom-call(bf16[1024,384]{1,0:T(8,128)(2,1)S(1)} %copy-done.18, bf16[1024,384]{1,0:T(8,128)(2,1)S(1)} %copy-done.18), custom_call_target="tpu_custom_call" | custom-call | flops 2147483648 | bytes 524288 | tf_op jit(solution)/shard_map/pallas_call | solution.py:76
  61.2 2.5 %collective-permute-done.9.refs_14_ = bf16[128,1024]{1,0:T(8,128)(2,1)S(1)} collective-permute-done((bf16[128,1024]{1,0:T(8,128)(2,1)S(1)}, bf16[128,1024]{1,0:T(8,128)(2,1)S(1)}, u32[]{:S(2)}, u32[]{:S(2)}) %collective-permute-start.9) | collective-permute-done | bytes 262176 | tf_op jit(solution)/shard_map/ppermute | solution.py:394
  64.2 1.5 collective-permute-start.15
  65.7 5.5 %collective-permute-done.13.refs_2_ = bf16[1024,128]{1,0:T(8,128)(2,1)S(1)} collective-permute-done((bf16[1024,128]{1,0:T(8,128)(2,1)S(1)}, bf16[1024,128]{1,0:T(8,128)(2,1)S(1)}, u32[]{:S(2)}, u32[]{:S(2)}) %collective-permute-start.13) | collective-permute-done | bytes 262176 | tf_op jit(solution)/shard_map/ppermute | solution.py:394
  72.8 5.2 %collective-permute-done.17.refs_6_ = bf16[1024,128]{1,0:T(8,128)(2,1)S(1)} collective-permute-done((bf16[1024,128]{1,0:T(8,128)(2,1)S(1)}, bf16[1024,128]{1,0:T(8,128)(2,1)S(1)}, u32[]{:S(2)}, u32[]{:S(2)}) %collective-permute-start.17) | collective-permute-done | bytes 262176 | tf_op jit(solution)/shard_map/ppermute | solution.py:394
  80.3 8.5 %shard_map.420 = (bf16[1024,1024]{1,0:T(8,128)(2,1)}, f32[128,1024]{1,0:T(8,128)}) custom-call(s32[2]{0:T(128)} %copy-done.14, bf16[1024,128]{1,0:T(8,128)(2,1)} %copy-done.16, bf16[1024,128]{1,0:T(8,128)(2,1)} %copy-done.41, bf16[1024,128]{1,0:T(8,128)(2,1)} %copy-done.38, bf16[1024,128]{1,0:T(8,128)(2,1)} %copy-done.45, bf16[1024,128]{1,0:T(8,128)(2,1)} %copy-done.39, ...), custom_call_target="tpu_custom_call" | custom-call | flops 2147483648 | bytes 8388608 | tf_op jit(solution)/shard_map/pallas_call | solution.py:84
  88.9 10.1 %shard_map.422 = (bf16[1024,512]{1,0:T(8,128)(2,1)}, bf16[1024,512]{1,0:T(8,128)(2,1)}, bf16[4,128,1024]{2,1,0:T(8,128)(2,1)}, bf16[4,128,1024]{2,1,0:T(8,128)(2...) custom-call(s32[2]{0:T(128)} %copy-done.14, ...), custom_call_target="tpu_custom_call" | custom-call | flops 4294967296 | bytes 12582912 | tf_op jit(solution)/shard_map/pallas_call | solution.py:84
  99.6 2.5 %collective-permute-done.20.refs_1_ = bf16[4,128,1024]{2,1,0:T(8,128)(2,1)S(1)} collective-permute-done((bf16[4,128,1024]{2,1,0:T(8,128)(2,1)}, bf16[4,128,1024]{2,1,0:T(8,128)(2,1)S(1)}, u32[]{:S(2)}, u32[]{:S(2)}) %collective-permute-start.20) | collective-permute-done | bytes 1048608 | tf_op jit(solution)/shard_map/ppermute | solution.py:394
  102.1 1.5 shard_map.423
  103.6 1.2 collective-permute-start.21
  104.8 1.5 collective-permute-start.22
  106.3 6.6 %shard_map.424 = bf16[4,1024,256]{2,1,0:T(8,128)(2,1)} custom-call(bf16[1024,1024]{1,0:T(8,128)(2,1)} %get-tuple-element.125.in_ref, bf16[1024,512]{1,0:T(8,128)(2,1)} %get-tuple-element.133.dpre_ref, bf16[1024,512]{1,0:T(8,128)(2,1)} %get-tuple-element.134.act_ref, bf16[1024,1024]{1,0:T(8,128)(2,1)} %cot_ref.3, f32[6,1024]{1,0:T(8,128)} %reshape.132.mod_ref.refs_17_.refs_5_), custom_call_target="tpu_custom_call" | custom-call | flops 2147483648 | bytes 8388608 | tf_op jit(solution)/shard_map/pallas_call | solution.py:76
  113.1 1.5 collective-permute-start.23
  118.2 1.4 collective-permute-done.24.refs_3_
  119.6 1.3 shard_map.426
  122.5 4.7 %collective-permute-done.26.refs_2_ = bf16[128,1024]{1,0:T(8,128)(2,1)S(1)} collective-permute-done((bf16[128,1024]{1,0:T(8,128)(2,1)S(1)}, bf16[128,1024]{1,0:T(8,128)(2,1)S(1)}, u32[]{:S(2)}, u32[]{:S(2)}) %collective-permute-start.26) | collective-permute-done | bytes 262176 | tf_op jit(solution)/shard_map/ppermute | solution.py:394
  128.8 4.9 %collective-permute-done.30.refs_6_ = bf16[128,1024]{1,0:T(8,128)(2,1)S(1)} collective-permute-done((bf16[128,1024]{1,0:T(8,128)(2,1)S(1)}, bf16[128,1024]{1,0:T(8,128)(2,1)S(1)}, u32[]{:S(2)}, u32[]{:S(2)}) %collective-permute-start.30) | collective-permute-done | bytes 262176 | tf_op jit(solution)/shard_map/ppermute | solution.py:394
  133.8 1.4 collective-permute-done.31.refs_7_
  135.9 11.5 %shard_map.427 = (bf16[1024,384]{1,0:T(8,128)(2,1)}, f32[1,384]{1,0:T(1,128)}, f32[1,1024]{1,0:T(1,128)}, bf16[1024,128]{1,0:T(8,128)(2,1)}) custom-call(s32[2]{0:T(128)} %copy-done.14, bf16[128,1024]{1,0:T(8,128)(2,1)} %copy-done.17, bf16[128,1024]{1,0:T(8,128)(2,1)} %copy-done.48, bf16[128,1024]{1,0:T(8,128)(2,1)} %copy-done.42, ...), custom_call_target="tpu_custom_call" | custom-call | flops 5368709120 | bytes 6291456 | tf_op jit(solution)/shard_map/pallas_call | solution.py:84
  148.5 5.6 %shard_map.428 = (bf16[4,128,1024]{2,1,0:T(8,128)(2,1)}, bf16[4,128,1024]{2,1,0:T(8,128)(2,1)}, f32[2,1024]{1,0:T(2,128)S(1)}) custom-call(s32[2]{0:T(128)S(1)} %copy-done.15, bf16[1024,384]{1,0:T(8,128)(2,1)S(1)} %copy-done.1, bf16[1024,384]{1,0:T(8,128)(2,1)S(1)} %copy-done.7, bf16[1024,1024]{1,0:T(8,128)(2,1)} %x_ref.3), custom_call_target="tpu_custom_call" | custom-call | flops 805306368 | bytes 6291456 | tf_op jit(solution)/shard_map/pallas_call | solution.py:84
  155.4 3.6 %all-to-all-start = ((f32[8,1,768]{2,1,0:T(1,128)}), f32[8,1,768]{2,1,0:T(1,128)S(1)}, u32[]{:S(2)}, u32[]{:S(2)}) async-start(f32[8,1,768]{2,1,0:T(1,128)} %all_to_all.12), calls=%async_computation.1 | async-start | bytes 49152 | tf_op jit(solution)/shard_map/all_to_all | solution.py:615
  159.7 4.1 %all-to-all-done = f32[8,1,768]{2,1,0:T(1,128)S(1)} async-done(((f32[8,1,768]{2,1,0:T(1,128)}), f32[8,1,768]{2,1,0:T(1,128)S(1)}, u32[]{:S(2)}, u32[]{:S(2)}) %all-to-all-start) | async-done | bytes 24608 | tf_op jit(solution)/shard_map/all_to_all | solution.py:615
  163.9 4.5 %shard_map.433 = bf16[1024,512]{1,0:T(8,128)(2,1)} custom-call(bf16[1024,1024]{1,0:T(8,128)(2,1)} %get-tuple-element.182.in_ref, bf16[1024,384]{1,0:T(8,128)(2,1)S(1)} %copy-done.2, bf16[1024,128]{1,0:T(8,128)(2,1)S(1)} %copy-done.12), custom_call_target="tpu_custom_call" | custom-call | flops 805306368 | bytes 4194304 | tf_op jit(solution)/shard_map/pallas_call | solution.py:76
  168.7 2.2 collective-permute-start.33
  170.9 2.5 %collective-permute-start.34 = (f32[1,3584]{1,0:T(1,128)S(1)}, f32[1,3584]{1,0:T(1,128)S(1)}, u32[]{:S(2)}, u32[]{:S(2)}) collective-permute-start(f32[1,3584]{1,0:T(1,128)S(1)} %reshape.143), channel_id=1, source_target_pairs={{0,24},{8,0},{16,8},{24,16},{1,25},{9,1},{17,9},{25,17},{2,26},{10... | collective-permute-start | bytes 43016 | tf_op jit(solution)/shard_map/ppermute | solution.py:472
  176.9 1.2 copy-done.4
  179.3 2.9 %shard_map.429 = (f32[2,128,1024]{2,1,0:T(8,128)S(1)}, bf16[2,128,1024]{2,1,0:T(8,128)(2,1)}, f32[2,128,1024]{2,1,0:T(8,128)S(1)}, bf16[2,128,1024]{2,1,0:T(8,128)(2,1)}) custom-call(bf16[4,128,1024]{2,1,0:T(8,128)(2,1)} %get-tuple-element.160.refs_0_, bf16[4,128,1024]{2,1,0:T(8,128)(2,1)} %get-tuple-element.161.refs_1_, ...), custom_call_target="tpu_custom_call" | custom-call | bytes 10485760 | tf_op jit(solution)/shard_map/pallas_call | solution.py:76
  183.3 3.6 %shard_map.435 = (f32[256,512]{1,0:T(8,128)}, f32[256,512]{1,0:T(8,128)}, f32[256,512]{1,0:T(8,128)}, f32[512,256]{1,0:T(8,128)}, f32[512,256]{1,0:T(8,128)}, /*index=5*/f32[512,256]{1,0:T(8,128)}) custom-call(bf16[1024,256]{1,0:T(8,128)(2,1)} %reduce-scatter.3.cloned.1.call-done.gup_ref.gdown_ref, ...), custom_call_target="tpu_custom_call" | custom-call | bytes 6815744 | tf_op jit(solution)/shard_map/pallas_call | solution.py:76
  187.8 3.7 %all-to-all-start.1 = ((f32[8,1,128]{2,1,0:T(1,128)}), f32[8,1,128]{2,1,0:T(1,128)S(1)}, u32[]{:S(2)}, u32[]{:S(2)}) async-start(f32[8,1,128]{2,1,0:T(1,128)} %bitcast.14), calls=%async_computation.2 | async-start | bytes 8192 | tf_op jit(solution)/shard_map/all_to_all | solution.py:643
  192.2 3.9 %all-to-all-done.1 = f32[8,1,128]{2,1,0:T(1,128)S(1)} async-done(((f32[8,1,128]{2,1,0:T(1,128)}), f32[8,1,128]{2,1,0:T(1,128)S(1)}, u32[]{:S(2)}, u32[]{:S(2)}) %all-to-all-start.1) | async-done | bytes 4128 | tf_op jit(solution)/shard_map/all_to_all | solution.py:643
  196.8 1.3 shard_map.430
  198.1 4.5 %collective-permute-start.39 = (bf16[1,128,1024]{2,1,0:T(8,128)(2,1)S(1)}, bf16[1,128,1024]{2,1,0:T(8,128)(2,1)S(1)}, u32[]{:S(2)}, u32[]{:S(2)}) collective-permute-start(bf16[1,128,1024]{2,1,0:T(8,128)(2,1)S(1)} %get-tuple-element.169), channel_id=1, source_target_pairs={{0,4},{1,5},{2,6},{3,7},{4,0},{5,1},{6,2},{7,3},{8,12},{9,13},{10,... | collective-permute-start | bytes 786440 | tf_op jit(solution)/shard_map/ppermute | solution.py:394
  202.6 2.8 %collective-permute-start.40 = (bf16[1,128,1024]{2,1,0:T(8,128)(2,1)S(1)}, bf16[1,128,1024]{2,1,0:T(8,128)(2,1)S(1)}, u32[]{:S(2)}, u32[]{:S(2)}) collective-permute-start(bf16[1,128,1024]{2,1,0:T(8,128)(2,1)S(1)} %get-tuple-element.171), channel_id=1, source_target_pairs={{0,2},{1,3},{2,0},{3,1},{4,6},{5,7},{6,4},{7,5},{8,10},{9,11},{10,... | collective-permute-start | bytes 786440 | tf_op jit(solution)/shard_map/ppermute | solution.py:394
  206.7 4.3 %shard_map.432 = (f32[256,768]{1,0:T(8,128)}, f32[256,768]{1,0:T(8,128)}, f32[256,768]{1,0:T(8,128)}) custom-call(bf16[4,256]{1,0:T(4,128)(2,1)} %copy-done.13, bf16[4,768]{1,0:T(4,128)(2,1)} %slice.106.dmod_ref, f32[256,768]{1,0:T(8,128)} %refs_0_.3, f32[256,768]{1,0:T(8,128)} %refs_1_.3, f32[256,768]{1,0:T(8,128)} %refs_2_.3), custom_call_target="tpu_custom_call" | custom-call | bytes 4718592 | tf_op jit(solution)/shard_map/pallas_call | solution.py:76
  211.5 2.6 %shard_map.431 = (f32[128,1024]{1,0:T(8,128)}, f32[128,1024]{1,0:T(8,128)}) custom-call(f32[1,128,1024]{2,1,0:T(8,128)S(1)} %get-tuple-element.168.refs_0_, bf16[1,128,1024]{2,1,0:T(8,128)(2,1)S(1)} %collective-permute-done.39.refs_1_, f32[1,128,1024]{2,1,0:T(8,128)S(1)} %get-tuple-element.170.refs_2_, ...), custom_call_target="tpu_custom_call" | custom-call | bytes 3670016 | tf_op jit(solution)/shard_map/pallas_call | solution.py:76
  214.1 2.9 %shard_map.434 = (f32[256,384]{1,0:T(8,128)}, f32[256,384]{1,0:T(8,128)}, f32[256,384]{1,0:T(8,128)}, f32[128,256]{1,0:T(8,128)}, f32[128,256]{1,0:T(8,128)}, /*index=5*/f32[128,256]{1,0:T(8,128)}) custom-call(bf16[256,512]{1,0:T(8,128)(2,1)} %reduce-scatter.5.cloned.1.call-done.grad_ref, f32[256,384]{1,0:T(8,128)} %refs_0_.4, f32[256,384]{1,0:T(8,128)} %refs_1_.4, ...), custom_call_target="tpu_custom_call" | custom-call | bytes 4194304 | tf_op jit(solution)/shard_map/pallas_call | solution.py:76
  (241 shorter events, 38.6 us)
Async XLA Ops:
  7.2 35.3 %all-gather.4.cloned.1.call-start = ((), (), s32[]{:S(2)}) async-start(), calls=%async_computation.4 | async-start | bytes 1310720 | tf_op jit(solution)/shard_map/all_gather | solution.py:485
  9.2 79.6 %all-gather.6.cloned.1.call-start = ((), (), s32[]{:S(2)}) async-start(), calls=%async_computation.7 | async-start | bytes 2621440 | tf_op jit(solution)/shard_map/all_gather | solution.py:486
  11.3 143.4 %reduce-scatter.3.cloned.1.call-start = ((), (), s32[]{:S(2)}) async-start(), calls=%async_computation.5 | async-start | bytes 2621440 | tf_op jit(solution)/shard_map/reduce_scatter | solution.py:584
  11.5 7.2 %collective-permute-start = (f32[1,1920]{1,0:T(1,128)S(1)}, f32[1,1920]{1,0:T(1,128)S(1)}, u32[]{:S(2)}, u32[]{:S(2)}) collective-permute-start(f32[1,1920]{1,0:T(1,128)S(1)} %maximum_convert_fusion.refs_0_), channel_id=1, source_target_pairs={{0,8},{8,16},{16,24},{24,0},{1,9},{9,17},{17,25},{25,1},{2,10},{10... | collective-permute-start | bytes 23048 | tf_op jit(solution)/shard_map/ppermute | solution.py:472
  14.6 4.6 %collective-permute-start.1 = (f32[1,1920]{1,0:T(1,128)S(1)}, f32[1,1920]{1,0:T(1,128)S(1)}, u32[]{:S(2)}, u32[]{:S(2)}) collective-permute-start(f32[1,1920]{1,0:T(1,128)S(1)} %maximum_convert_fusion.refs_0_), channel_id=1, source_target_pairs={{0,16},{8,24},{16,0},{24,8},{1,17},{9,25},{17,1},{25,9},{2,18},{10... | collective-permute-start | bytes 23048 | tf_op jit(solution)/shard_map/ppermute | solution.py:472
  17.2 3.6 %collective-permute-start.2 = (f32[1,1920]{1,0:T(1,128)S(1)}, f32[1,1920]{1,0:T(1,128)S(1)}, u32[]{:S(2)}, u32[]{:S(2)}) collective-permute-start(f32[1,1920]{1,0:T(1,128)S(1)} %maximum_convert_fusion.refs_0_), channel_id=1, source_target_pairs={{0,24},{8,0},{16,8},{24,16},{1,25},{9,1},{17,9},{25,17},{2,26},{10... | collective-permute-start | bytes 23048 | tf_op jit(solution)/shard_map/ppermute | solution.py:472
  23.0 4.5 %collective-permute-start.3 = (f32[1,768]{1,0:T(1,128)S(1)}, f32[1,768]{1,0:T(1,128)S(1)}, u32[]{:S(2)}, u32[]{:S(2)}) collective-permute-start(f32[1,768]{1,0:T(1,128)S(1)} %get-tuple-element.210), channel_id=1, source_target_pairs={{0,24},{8,0},{16,8},{24,16},{1,25},{9,1},{17,9},{25,17},{2,26},{10... | collective-permute-start | bytes 9224 | tf_op jit(solution)/shard_map/ppermute | solution.py:472
  26.2 4.6 %collective-permute-start.4 = (f32[1,768]{1,0:T(1,128)S(1)}, f32[1,768]{1,0:T(1,128)S(1)}, u32[]{:S(2)}, u32[]{:S(2)}) collective-permute-start(f32[1,768]{1,0:T(1,128)S(1)} %get-tuple-element.212), channel_id=1, source_target_pairs={{0,16},{8,24},{16,0},{24,8},{1,17},{9,25},{17,1},{25,9},{2,18},{10... | collective-permute-start | bytes 9224 | tf_op jit(solution)/shard_map/ppermute | solution.py:472
  26.2 5.4 %collective-permute-start.5 = (f32[1,768]{1,0:T(1,128)S(1)}, f32[1,768]{1,0:T(1,128)S(1)}, u32[]{:S(2)}, u32[]{:S(2)}) collective-permute-start(f32[1,768]{1,0:T(1,128)S(1)} %get-tuple-element.211), channel_id=1, source_target_pairs={{0,8},{8,16},{16,24},{24,0},{1,9},{9,17},{17,25},{25,1},{2,10},{10... | collective-permute-start | bytes 9224 | tf_op jit(solution)/shard_map/ppermute | solution.py:472
  44.8 8.7 %collective-permute-start.6 = (bf16[128,1024]{1,0:T(8,128)(2,1)}, bf16[128,1024]{1,0:T(8,128)(2,1)S(1)}, u32[]{:S(2)}, u32[]{:S(2)}) collective-permute-start(bf16[128,1024]{1,0:T(8,128)(2,1)} %get-tuple-element.113.refs_8_), channel_id=1, source_target_pairs={{0,2},{1,3},{2,0},{3,1},{4,6},{5,7},{6,4},{7,5},{8,10},{9,11},{10,... | collective-permute-start | bytes 786440 | tf_op jit(solution)/shard_map/ppermute | solution.py:394
  46.3 8.5 %collective-permute-start.7 = (bf16[128,1024]{1,0:T(8,128)(2,1)}, bf16[128,1024]{1,0:T(8,128)(2,1)S(1)}, u32[]{:S(2)}, u32[]{:S(2)}) collective-permute-start(bf16[128,1024]{1,0:T(8,128)(2,1)} %get-tuple-element.113.refs_8_), channel_id=1, source_target_pairs={{0,4},{1,5},{2,6},{3,7},{4,0},{5,1},{6,2},{7,3},{8,12},{9,13},{10,... | collective-permute-start | bytes 786440 | tf_op jit(solution)/shard_map/ppermute | solution.py:394
  46.9 7.9 %collective-permute-start.8 = (bf16[128,1024]{1,0:T(8,128)(2,1)}, bf16[128,1024]{1,0:T(8,128)(2,1)S(1)}, u32[]{:S(2)}, u32[]{:S(2)}) collective-permute-start(bf16[128,1024]{1,0:T(8,128)(2,1)} %get-tuple-element.113.refs_8_), channel_id=1, source_target_pairs={{0,1},{1,0},{2,3},{3,2},{4,5},{5,4},{6,7},{7,6},{8,9},{9,8},{10,11... | collective-permute-start | bytes 786440 | tf_op jit(solution)/shard_map/ppermute | solution.py:394
  54.8 6.4 %collective-permute-start.10 = (bf16[128,1024]{1,0:T(8,128)(2,1)S(1)}, bf16[128,1024]{1,0:T(8,128)(2,1)S(1)}, u32[]{:S(2)}, u32[]{:S(2)}) collective-permute-start(bf16[128,1024]{1,0:T(8,128)(2,1)S(1)} %collective-permute-done.6.refs_10_), channel_id=1, source_target_pairs={{0,1},{1,0},{2,3},{3,2},{4,5},{5,4},{6,7},{7,6},{8,9},{9,8},{10,11... | collective-permute-start | bytes 786440 | tf_op jit(solution)/shard_map/ppermute | solution.py:394
  54.9 6.3 %collective-permute-start.11 = (bf16[128,1024]{1,0:T(8,128)(2,1)S(1)}, bf16[128,1024]{1,0:T(8,128)(2,1)S(1)}, u32[]{:S(2)}, u32[]{:S(2)}) collective-permute-start(bf16[128,1024]{1,0:T(8,128)(2,1)S(1)} %collective-permute-done.7.refs_12_), channel_id=1, source_target_pairs={{0,1},{1,0},{2,3},{3,2},{4,5},{5,4},{6,7},{7,6},{8,9},{9,8},{10,11... | collective-permute-start | bytes 786440 | tf_op jit(solution)/shard_map/ppermute | solution.py:394
  55.4 8.3 %collective-permute-start.9 = (bf16[128,1024]{1,0:T(8,128)(2,1)S(1)}, bf16[128,1024]{1,0:T(8,128)(2,1)S(1)}, u32[]{:S(2)}, u32[]{:S(2)}) collective-permute-start(bf16[128,1024]{1,0:T(8,128)(2,1)S(1)} %collective-permute-done.6.refs_10_), channel_id=1, source_target_pairs={{0,4},{1,5},{2,6},{3,7},{4,0},{5,1},{6,2},{7,3},{8,12},{9,13},{10,... | collective-permute-start | bytes 786440 | tf_op jit(solution)/shard_map/ppermute | solution.py:394
  63.7 7.6 %collective-permute-start.13 = (bf16[1024,128]{1,0:T(8,128)(2,1)S(1)}, bf16[1024,128]{1,0:T(8,128)(2,1)S(1)}, u32[]{:S(2)}, u32[]{:S(2)}) collective-permute-start(bf16[1024,128]{1,0:T(8,128)(2,1)S(1)} %get-tuple-element.120.refs_0_.refs_11_), channel_id=1, source_target_pairs={{0,2},{1,3},{2,0},{3,1},{4,6},{5,7},{6,4},{7,5},{8,10},{9,11},{10,... | collective-permute-start | bytes 786440 | tf_op jit(solution)/shard_map/ppermute | solution.py:394
  64.2 8.1 %collective-permute-start.15 = (bf16[1024,128]{1,0:T(8,128)(2,1)S(1)}, bf16[1024,128]{1,0:T(8,128)(2,1)S(1)}, u32[]{:S(2)}, u32[]{:S(2)}) collective-permute-start(bf16[1024,128]{1,0:T(8,128)(2,1)S(1)} %get-tuple-element.120.refs_0_.refs_11_), channel_id=1, source_target_pairs={{0,4},{1,5},{2,6},{3,7},{4,0},{5,1},{6,2},{7,3},{8,12},{9,13},{10,... | collective-permute-start | bytes 786440 | tf_op jit(solution)/shard_map/ppermute | solution.py:394
  71.2 6.7 %collective-permute-start.17 = (bf16[1024,128]{1,0:T(8,128)(2,1)S(1)}, bf16[1024,128]{1,0:T(8,128)(2,1)S(1)}, u32[]{:S(2)}, u32[]{:S(2)}) collective-permute-start(bf16[1024,128]{1,0:T(8,128)(2,1)S(1)} %collective-permute-done.13.refs_2_), channel_id=1, source_target_pairs={{0,4},{1,5},{2,6},{3,7},{4,0},{5,1},{6,2},{7,3},{8,12},{9,13},{10,... | collective-permute-start | bytes 786440 | tf_op jit(solution)/shard_map/ppermute | solution.py:394
  71.7 7.5 %collective-permute-start.12 = (bf16[1024,128]{1,0:T(8,128)(2,1)S(1)}, bf16[1024,128]{1,0:T(8,128)(2,1)S(1)}, u32[]{:S(2)}, u32[]{:S(2)}) collective-permute-start(bf16[1024,128]{1,0:T(8,128)(2,1)S(1)} %get-tuple-element.120.refs_0_.refs_11_), channel_id=1, source_target_pairs={{0,1},{1,0},{2,3},{3,2},{4,5},{5,4},{6,7},{7,6},{8,9},{9,8},{10,11... | collective-permute-start | bytes 786440 | tf_op jit(solution)/shard_map/ppermute | solution.py:394
  71.7 7.5 %collective-permute-start.19 = (bf16[128,1024]{1,0:T(8,128)(2,1)S(1)}, bf16[128,1024]{1,0:T(8,128)(2,1)S(1)}, u32[]{:S(2)}, u32[]{:S(2)}) collective-permute-start(bf16[128,1024]{1,0:T(8,128)(2,1)S(1)} %collective-permute-done.9.refs_14_), channel_id=1, source_target_pairs={{0,1},{1,0},{2,3},{3,2},{4,5},{5,4},{6,7},{7,6},{8,9},{9,8},{10,11... | collective-permute-start | bytes 786440 | tf_op jit(solution)/shard_map/ppermute | solution.py:394
  72.3 7.0 %collective-permute-start.14 = (bf16[1024,128]{1,0:T(8,128)(2,1)S(1)}, bf16[1024,128]{1,0:T(8,128)(2,1)S(1)}, u32[]{:S(2)}, u32[]{:S(2)}) collective-permute-start(bf16[1024,128]{1,0:T(8,128)(2,1)S(1)} %collective-permute-done.13.refs_2_), channel_id=1, source_target_pairs={{0,1},{1,0},{2,3},{3,2},{4,5},{5,4},{6,7},{7,6},{8,9},{9,8},{10,11... | collective-permute-start | bytes 786440 | tf_op jit(solution)/shard_map/ppermute | solution.py:394
  72.3 7.0 %collective-permute-start.16 = (bf16[1024,128]{1,0:T(8,128)(2,1)S(1)}, bf16[1024,128]{1,0:T(8,128)(2,1)S(1)}, u32[]{:S(2)}, u32[]{:S(2)}) collective-permute-start(bf16[1024,128]{1,0:T(8,128)(2,1)S(1)} %collective-permute-done.15.refs_4_), channel_id=1, source_target_pairs={{0,1},{1,0},{2,3},{3,2},{4,5},{5,4},{6,7},{7,6},{8,9},{9,8},{10,11... | collective-permute-start | bytes 786440 | tf_op jit(solution)/shard_map/ppermute | solution.py:394
  78.0 1.5 collective-permute-start.18
  99.0 3.1 %collective-permute-start.20 = (bf16[4,128,1024]{2,1,0:T(8,128)(2,1)}, bf16[4,128,1024]{2,1,0:T(8,128)(2,1)S(1)}, u32[]{:S(2)}, u32[]{:S(2)}) collective-permute-start(bf16[4,128,1024]{2,1,0:T(8,128)(2,1)} %get-tuple-element.127), channel_id=1, source_target_pairs={{0,1},{1,0},{2,3},{3,2},{4,5},{5,4},{6,7},{7,6},{8,9},{9,8},{10,11... | collective-permute-start | bytes 3145736 | tf_op jit(solution)/shard_map/ppermute | solution.py:394
  103.6 9.4 %collective-permute-start.21 = (bf16[2,128,512]{2,1,0:T(8,128)(2,1)S(1)}, bf16[2,128,512]{2,1,0:T(8,128)(2,1)S(1)}, u32[]{:S(2)}, u32[]{:S(2)}) collective-permute-start(bf16[2,128,512]{2,1,0:T(8,128)(2,1)S(1)} %get-tuple-element.129), channel_id=1, source_target_pairs={{0,2},{1,3},{2,0},{3,1},{4,6},{5,7},{6,4},{7,5},{8,10},{9,11},{10,... | collective-permute-start | bytes 786440 | tf_op jit(solution)/shard_map/ppermute | solution.py:394
  104.8 8.1 %collective-permute-start.22 = (bf16[2,128,512]{2,1,0:T(8,128)(2,1)S(1)}, bf16[2,128,512]{2,1,0:T(8,128)(2,1)S(1)}, u32[]{:S(2)}, u32[]{:S(2)}) collective-permute-start(bf16[2,128,512]{2,1,0:T(8,128)(2,1)S(1)} %get-tuple-element.131), channel_id=1, source_target_pairs={{0,4},{1,5},{2,6},{3,7},{4,0},{5,1},{6,2},{7,3},{8,12},{9,13},{10,... | collective-permute-start | bytes 786440 | tf_op jit(solution)/shard_map/ppermute | solution.py:394
  113.1 5.0 %collective-permute-start.23 = (bf16[1,128,512]{2,1,0:T(8,128)(2,1)S(1)}, bf16[1,128,512]{2,1,0:T(8,128)(2,1)S(1)}, u32[]{:S(2)}, u32[]{:S(2)}) collective-permute-start(bf16[1,128,512]{2,1,0:T(8,128)(2,1)S(1)} %get-tuple-element.140), channel_id=1, source_target_pairs={{0,4},{1,5},{2,6},{3,7},{4,0},{5,1},{6,2},{7,3},{8,12},{9,13},{10,... | collective-permute-start | bytes 393224 | tf_op jit(solution)/shard_map/ppermute | solution.py:394
  114.6 5.0 %collective-permute-start.24 = (bf16[1,128,512]{2,1,0:T(8,128)(2,1)S(1)}, bf16[1,128,512]{2,1,0:T(8,128)(2,1)S(1)}, u32[]{:S(2)}, u32[]{:S(2)}) collective-permute-start(bf16[1,128,512]{2,1,0:T(8,128)(2,1)S(1)} %get-tuple-element.142), channel_id=1, source_target_pairs={{0,2},{1,3},{2,0},{3,1},{4,6},{5,7},{6,4},{7,5},{8,10},{9,11},{10,... | collective-permute-start | bytes 393224 | tf_op jit(solution)/shard_map/ppermute | solution.py:394
  120.9 6.4 %collective-permute-start.26 = (bf16[128,1024]{1,0:T(8,128)(2,1)S(1)}, bf16[128,1024]{1,0:T(8,128)(2,1)S(1)}, u32[]{:S(2)}, u32[]{:S(2)}) collective-permute-start(bf16[128,1024]{1,0:T(8,128)(2,1)S(1)} %get-tuple-element.144.refs_0_), channel_id=1, source_target_pairs={{0,2},{1,3},{2,0},{3,1},{4,6},{5,7},{6,4},{7,5},{8,10},{9,11},{10,... | collective-permute-start | bytes 786440 | tf_op jit(solution)/shard_map/ppermute | solution.py:394
  121.4 7.3 %collective-permute-start.28 = (bf16[128,1024]{1,0:T(8,128)(2,1)S(1)}, bf16[128,1024]{1,0:T(8,128)(2,1)S(1)}, u32[]{:S(2)}, u32[]{:S(2)}) collective-permute-start(bf16[128,1024]{1,0:T(8,128)(2,1)S(1)} %get-tuple-element.144.refs_0_), channel_id=1, source_target_pairs={{0,4},{1,5},{2,6},{3,7},{4,0},{5,1},{6,2},{7,3},{8,12},{9,13},{10,... | collective-permute-start | bytes 786440 | tf_op jit(solution)/shard_map/ppermute | solution.py:394
  127.3 6.4 %collective-permute-start.30 = (bf16[128,1024]{1,0:T(8,128)(2,1)S(1)}, bf16[128,1024]{1,0:T(8,128)(2,1)S(1)}, u32[]{:S(2)}, u32[]{:S(2)}) collective-permute-start(bf16[128,1024]{1,0:T(8,128)(2,1)S(1)} %collective-permute-done.26.refs_2_), channel_id=1, source_target_pairs={{0,4},{1,5},{2,6},{3,7},{4,0},{5,1},{6,2},{7,3},{8,12},{9,13},{10,... | collective-permute-start | bytes 786440 | tf_op jit(solution)/shard_map/ppermute | solution.py:394
  128.2 5.5 %collective-permute-start.25 = (bf16[128,1024]{1,0:T(8,128)(2,1)S(1)}, bf16[128,1024]{1,0:T(8,128)(2,1)S(1)}, u32[]{:S(2)}, u32[]{:S(2)}) collective-permute-start(bf16[128,1024]{1,0:T(8,128)(2,1)S(1)} %get-tuple-element.144.refs_0_), channel_id=1, source_target_pairs={{0,1},{1,0},{2,3},{3,2},{4,5},{5,4},{6,7},{7,6},{8,9},{9,8},{10,11... | collective-permute-start | bytes 786440 | tf_op jit(solution)/shard_map/ppermute | solution.py:394
  128.2 5.5 %collective-permute-start.27 = (bf16[128,1024]{1,0:T(8,128)(2,1)S(1)}, bf16[128,1024]{1,0:T(8,128)(2,1)S(1)}, u32[]{:S(2)}, u32[]{:S(2)}) collective-permute-start(bf16[128,1024]{1,0:T(8,128)(2,1)S(1)} %collective-permute-done.26.refs_2_), channel_id=1, source_target_pairs={{0,1},{1,0},{2,3},{3,2},{4,5},{5,4},{6,7},{7,6},{8,9},{9,8},{10,11... | collective-permute-start | bytes 786440 | tf_op jit(solution)/shard_map/ppermute | solution.py:394
  128.7 5.0 %collective-permute-start.29 = (bf16[128,1024]{1,0:T(8,128)(2,1)S(1)}, bf16[128,1024]{1,0:T(8,128)(2,1)S(1)}, u32[]{:S(2)}, u32[]{:S(2)}) collective-permute-start(bf16[128,1024]{1,0:T(8,128)(2,1)S(1)} %collective-permute-done.28.refs_4_), channel_id=1, source_target_pairs={{0,1},{1,0},{2,3},{3,2},{4,5},{5,4},{6,7},{7,6},{8,9},{9,8},{10,11... | collective-permute-start | bytes 786440 | tf_op jit(solution)/shard_map/ppermute | solution.py:394
  133.6 1.5 collective-permute-start.31
  154.2 20.7 %collective-permute-start.35 = (bf16[4,128,1024]{2,1,0:T(8,128)(2,1)}, bf16[4,128,1024]{2,1,0:T(8,128)(2,1)S(1)}, u32[]{:S(2)}, u32[]{:S(2)}) collective-permute-start(bf16[4,128,1024]{2,1,0:T(8,128)(2,1)} %get-tuple-element.162), channel_id=1, source_target_pairs={{0,1},{1,0},{2,3},{3,2},{4,5},{5,4},{6,7},{7,6},{8,9},{9,8},{10,11... | collective-permute-start | bytes 3145736 | tf_op jit(solution)/shard_map/ppermute | solution.py:394
  155.4 8.4 %all-to-all-start = ((f32[8,1,768]{2,1,0:T(1,128)}), f32[8,1,768]{2,1,0:T(1,128)S(1)}, u32[]{:S(2)}, u32[]{:S(2)}) async-start(f32[8,1,768]{2,1,0:T(1,128)} %all_to_all.12), calls=%async_computation.1 | async-start | bytes 49152 | tf_op jit(solution)/shard_map/all_to_all | solution.py:615
  159.0 55.1 %reduce-scatter.5.cloned.1.call-start = ((), (), s32[]{:S(2)}) async-start(), calls=%async_computation.6 | async-start | bytes 1310720 | tf_op jit(solution)/shard_map/reduce_scatter | solution.py:623
  159.3 16.6 %collective-permute-start.36 = (bf16[4,128,1024]{2,1,0:T(8,128)(2,1)}, bf16[4,128,1024]{2,1,0:T(8,128)(2,1)S(1)}, u32[]{:S(2)}, u32[]{:S(2)}) collective-permute-start(bf16[4,128,1024]{2,1,0:T(8,128)(2,1)} %get-tuple-element.163), channel_id=1, source_target_pairs={{0,1},{1,0},{2,3},{3,2},{4,5},{5,4},{6,7},{7,6},{8,9},{9,8},{10,11... | collective-permute-start | bytes 3145736 | tf_op jit(solution)/shard_map/ppermute | solution.py:394
  168.6 5.6 %collective-permute-start.32 = (f32[1,3584]{1,0:T(1,128)S(1)}, f32[1,3584]{1,0:T(1,128)S(1)}, u32[]{:S(2)}, u32[]{:S(2)}) collective-permute-start(f32[1,3584]{1,0:T(1,128)S(1)} %reshape.143), channel_id=1, source_target_pairs={{0,8},{8,16},{16,24},{24,0},{1,9},{9,17},{17,25},{25,1},{2,10},{10... | collective-permute-start | bytes 43016 | tf_op jit(solution)/shard_map/ppermute | solution.py:472
  168.7 5.5 %collective-permute-start.33 = (f32[1,3584]{1,0:T(1,128)S(1)}, f32[1,3584]{1,0:T(1,128)S(1)}, u32[]{:S(2)}, u32[]{:S(2)}) collective-permute-start(f32[1,3584]{1,0:T(1,128)S(1)} %reshape.143), channel_id=1, source_target_pairs={{0,16},{8,24},{16,0},{24,8},{1,17},{9,25},{17,1},{25,9},{2,18},{10... | collective-permute-start | bytes 43016 | tf_op jit(solution)/shard_map/ppermute | solution.py:472
  170.9 4.0 %collective-permute-start.34 = (f32[1,3584]{1,0:T(1,128)S(1)}, f32[1,3584]{1,0:T(1,128)S(1)}, u32[]{:S(2)}, u32[]{:S(2)}) collective-permute-start(f32[1,3584]{1,0:T(1,128)S(1)} %reshape.143), channel_id=1, source_target_pairs={{0,24},{8,0},{16,8},{24,16},{1,25},{9,1},{17,9},{25,17},{2,26},{10... | collective-permute-start | bytes 43016 | tf_op jit(solution)/shard_map/ppermute | solution.py:472
  182.2 14.6 %collective-permute-start.37 = (bf16[2,128,1024]{2,1,0:T(8,128)(2,1)}, bf16[2,128,1024]{2,1,0:T(8,128)(2,1)S(1)}, u32[]{:S(2)}, u32[]{:S(2)}) collective-permute-start(bf16[2,128,1024]{2,1,0:T(8,128)(2,1)} %get-tuple-element.165), channel_id=1, source_target_pairs={{0,2},{1,3},{2,0},{3,1},{4,6},{5,7},{6,4},{7,5},{8,10},{9,11},{10,... | collective-permute-start | bytes 1572872 | tf_op jit(solution)/shard_map/ppermute | solution.py:394
  182.7 14.1 %collective-permute-start.38 = (bf16[2,128,1024]{2,1,0:T(8,128)(2,1)}, bf16[2,128,1024]{2,1,0:T(8,128)(2,1)}, u32[]{:S(2)}, u32[]{:S(2)}) collective-permute-start(bf16[2,128,1024]{2,1,0:T(8,128)(2,1)} %get-tuple-element.167), channel_id=1, source_target_pairs={{0,4},{1,5},{2,6},{3,7},{4,0},{5,1},{6,2},{7,3},{8,12},{9,13},{10,... | collective-permute-start | bytes 1572872 | tf_op jit(solution)/shard_map/ppermute | solution.py:394
  187.8 8.3 %all-to-all-start.1 = ((f32[8,1,128]{2,1,0:T(1,128)}), f32[8,1,128]{2,1,0:T(1,128)S(1)}, u32[]{:S(2)}, u32[]{:S(2)}) async-start(f32[8,1,128]{2,1,0:T(1,128)} %bitcast.14), calls=%async_computation.2 | async-start | bytes 8192 | tf_op jit(solution)/shard_map/all_to_all | solution.py:643
  196.1 14.8 %collective-permute-start.41 = (f32[1,128]{1,0:T(1,128)S(1)}, f32[1,128]{1,0:T(1,128)S(1)}, u32[]{:S(2)}, u32[]{:S(2)}) collective-permute-start(f32[1,128]{1,0:T(1,128)S(1)} %bitcast.45), channel_id=1, source_target_pairs={{0,0},{1,1},{2,24},{3,25},{4,16},{5,17},{6,8},{7,9},{8,10},{9,11},... | collective-permute-start | bytes 1544 | tf_op jit(solution)/shard_map/ppermute | solution.py:644
  198.1 13.4 %collective-permute-start.39 = (bf16[1,128,1024]{2,1,0:T(8,128)(2,1)S(1)}, bf16[1,128,1024]{2,1,0:T(8,128)(2,1)S(1)}, u32[]{:S(2)}, u32[]{:S(2)}) collective-permute-start(bf16[1,128,1024]{2,1,0:T(8,128)(2,1)S(1)} %get-tuple-element.169), channel_id=1, source_target_pairs={{0,4},{1,5},{2,6},{3,7},{4,0},{5,1},{6,2},{7,3},{8,12},{9,13},{10,... | collective-permute-start | bytes 786440 | tf_op jit(solution)/shard_map/ppermute | solution.py:394
  202.6 9.0 %collective-permute-start.40 = (bf16[1,128,1024]{2,1,0:T(8,128)(2,1)S(1)}, bf16[1,128,1024]{2,1,0:T(8,128)(2,1)S(1)}, u32[]{:S(2)}, u32[]{:S(2)}) collective-permute-start(bf16[1,128,1024]{2,1,0:T(8,128)(2,1)S(1)} %get-tuple-element.171), channel_id=1, source_target_pairs={{0,2},{1,3},{2,0},{3,1},{4,6},{5,7},{6,4},{7,5},{8,10},{9,11},{10,... | collective-permute-start | bytes 786440 | tf_op jit(solution)/shard_map/ppermute | solution.py:394
  (53 other events, 381.0 us)
Sparse Core Ops, SparseCore 0:
  10.2 30.8 all-gather.3
  43.2 45.3 all-gather.5
  113.1 41.5 reduce-scatter.2
  168.6 24.6 reduce-scatter.4

commit v4 on v3

--- a/solution.py
+++ b/solution.py
@@ -434,7 +434,7 @@
         outs = [shape(dims, F32), shape(dims, BF)] * 2
         specs = [full(dims)] * 4
         if left is None:
-            args, body, far = (*keeps, *gots), functools.partial(fold_first_body, len(keeps)), range(len(keeps))
+            args, body, far = (*keeps, *gots), functools.partial(fold_first_body, len(keeps)), range(len(keeps) ** 2)
         else:
             args, body, far = (left, lgot, right, rgot), fold_next_body, ()
         left, lsend, right, rsend = call(
@@ -607,13 +607,25 @@
         [rows_of(pair, 3 * hc), full((D, 3 * hc)), rows_of(pair, D)],
         [place_pair, place_pair, full((2, D))],
         [far_shape((T // 2, rows, D), BF)] * 2 + [shape((2, D), F32)],
-        (dqkv, w_qkv_all, inputs), scalar=scalar, flops=6 * S * D * hc, nbytes=6 * S * D, mib=32, far=(2,),
+        (dqkv, w_qkv_all, inputs), scalar=scalar, flops=6 * S * D * hc, nbytes=6 * S * D, mib=32, far=(1, 2),
     )
     sums_out = out_sum + bias_rows[1:2] * jnp.sum(cot_rows.astype(F32), 0, keepdims=True)
     dmod = jnp.concatenate([sums_in, sums_mid, sums_out], axis=0).reshape(T, ada)
     dmod, mlp_grad, keep2, send2 = lax.optimization_barrier((dmod, mlp_grad, keep2, send2))
     dmod = jnp.sum(lax.all_to_all(dmod, "tensor", 0, 0, tiled=True), 0)
-    dqkv_late, dmod = lax.optimization_barrier((dqkv, dmod))
+    wide = LR_SCALE * D ** (-0.5)
+    chunks = F // share
+    square = (share, share)
+    up_block = pl.BlockSpec(square, lambda i: (0, i))
+    down_block = pl.BlockSpec(square, lambda i: (i, 0))
+    mlp_out = call(
+        functools.partial(adam_mlp_body, wide, LR_SCALE * (F * T) ** (-0.5)), (chunks,),
+        [down_block, pl.BlockSpec(square, lambda i: (chunks + i, 0))] + [up_block] * 3 + [down_block] * 3,
+        [up_block] * 3 + [down_block] * 3,
+        [far_shape((share, F), F32)] * 3 + [far_shape((F, share), F32)] * 3,
+        (mlp_grad, mlp_grad, w_fc1, m_fc1, v_fc1, w_fc2, m_fc2, v_fc2), nbytes=52 * share * F,
+    )
+    dqkv_late, dmod, *mlp_out = lax.optimization_barrier((dqkv, dmod, *mlp_out))
     first_grad = call(
         first_grad_body, (G,),
         [pl.BlockSpec((S, share), lambda i: (0, i)), full((S, 3 * hc)), pl.BlockSpec((share, hc), lambda i: (i, 0))],
@@ -640,16 +652,6 @@
     row_sum = lax.dynamic_slice_in_dim(bias_sum[G * n_col :].reshape(2, D), z * share, share, 1)
     per = T // G
     grad_silu = dot(dmod_rel, ada_low, 1, 1).reshape(T, D // T)
-    grad_silu = jnp.sum(lax.all_to_all(grad_silu, "tensor", 0, 0, tiled=True), 0, keepdims=True)
-    grad_silu = lax.ppermute(
-        grad_silu, ("dp", "tensor"),
-        [(a * T + b, ((a - b // per) % G) * T + a * per + b % per) for a in range(G) for b in range(T)],
-    )
-    cond_here = lax.dynamic_slice_in_dim(cond, t * (D // T), D // T, 1)
-    sig_here = jax.nn.sigmoid(cond_here)
-    cond_grad = grad_silu * sig_here * (1.0 + cond_here * (1.0 - sig_here))
-
-    wide = LR_SCALE * D ** (-0.5)
     chunk = ada // 3
     by_chunk = pl.BlockSpec((share, chunk), lambda i: (0, i))
     ada_out = call(
@@ -658,23 +660,24 @@
         [by_chunk] * 3, [far_shape((share, ada), F32)] * 3,
         (silu_own, dmod_rel, w_ada, m_ada, v_ada), nbytes=24 * share * ada,
     )
+    grad_silu, *ada_out = lax.optimization_barrier(
+        (lax.all_to_all(grad_silu, "tensor", 0, 0, tiled=True), *ada_out)
+    )
+    grad_silu = jnp.sum(grad_silu, 0, keepdims=True)
+    grad_silu = lax.ppermute(
+        grad_silu, ("dp", "tensor"),
+        [(a * T + b, ((a - b // per) % G) * T + a * per + b % per) for a in range(G) for b in range(T)],
+    )
+    cond_here = lax.dynamic_slice_in_dim(cond, t * (D // T), D // T, 1)
+    sig_here = jax.nn.sigmoid(cond_here)
+    cond_grad = grad_silu * sig_here * (1.0 + cond_here * (1.0 - sig_here))
+
     wide_block, flat = full((share, 3 * hc)), full((hc, share))
     first_out = call(
         functools.partial(adam_first_body, wide, LR_SCALE * (D // 32) ** (-0.5)), (1,),
         [full((share, 4 * hc))] + [wide_block] * 3 + [flat] * 3, [wide_block] * 3 + [flat] * 3,
         [far_shape((share, 3 * hc), F32)] * 3 + [far_shape((hc, share), F32)] * 3,
         (first_grad, w_qkv, m_qkv, v_qkv, w_proj, m_proj, v_proj), nbytes=32 * share * 4 * hc,
-    )
-    chunks = F // share
-    square = (share, share)
-    up_block = pl.BlockSpec(square, lambda i: (0, i))
-    down_block = pl.BlockSpec(square, lambda i: (i, 0))
-    mlp_out = call(
-        functools.partial(adam_mlp_body, wide, LR_SCALE * (F * T) ** (-0.5)), (chunks,),
-        [down_block, pl.BlockSpec(square, lambda i: (chunks + i, 0))] + [up_block] * 3 + [down_block] * 3,
-        [up_block] * 3 + [down_block] * 3,
-        [far_shape((share, F), F32)] * 3 + [far_shape((F, share), F32)] * 3,
-        (mlp_grad, mlp_grad, w_fc1, m_fc1, v_fc1, w_fc2, m_fc2, v_fc2), nbytes=52 * share * F,
     )
     col_second, col_new = adam_step(col_bias, m_col, v_col, col_sum, LR_BIAS, 0.0)
     row_second, row_new = adam_step(row_bias, m_row, v_row, row_sum, LR_BIAS, 0.0)

time: 225 us -> 221 us (0.982)
  local copies, waits for them, and re-layouts: 16.8 us -> 11.6 us
  waiting for transfers between devices: 47.9 us -> 51.6 us
  starting transfers between devices: 47.8 us -> 45.1 us
    ppermute x32, waiting for transfers between devices: 31.2 us -> 38 us  [swap(): return lax.ppermute(value, 'tensor', [(i, i ^ mask) for i in range(size)])]
    unnamed x116 -> x98, local copies, waits for them, and re-layouts: 10.9 us -> 5.67 us
    all_to_all x1, waiting for transfers between devices: 4.1 us -> 0.47 us  [shards(): dmod = jnp.sum(lax.all_to_all(dmod, 'tensor', 0, 0, tiled=True), 0)]
    all_to_all x1, waiting for transfers between devices: 3.93 us -> 1.27 us  [shards(): lax.all_to_all(grad_silu, 'tensor', 0, 0, tiled=True)]
  transfers between devices with their start and end apart: 48 -> 48, of which waited for: 22 -> 24; matrix products, arithmetic and copies ran while one was open for 4% -> 4% of each run, Pallas kernels for 30% -> 31%
where the time goes in v4:
time: 221 us; the launch traced here: 220 us
  Pallas kernels  83.8 us (38%)
  waiting for transfers between devices  51.6 us (23%)
  starting transfers between devices  45.1 us (20%)
  between operations  14.5 us (7%)
  local copies, waits for them, and re-layouts  11.6 us (5%)
  blocking collectives  9.03 us (4%)
  other arithmetic  3.99 us (2%)
    pallas_call x16, Pallas kernels, call(): pl.pallas_call(body, grid=grid, in_specs=in_specs, out_specs=out_specs, o...  47 us
    ppermute x32, waiting for transfers between devices, swap(): return lax.ppermute(value, 'tensor', [(i, i ^ mask) for i in range(size)])  38 us
    pallas_call x5, Pallas kernels, call(): pl.pallas_call(body, grid_spec=spec, out_shape=out_shape, compiler_params...  36.8 us
    ppermute x32, starting transfers between devices, swap(): return lax.ppermute(value, 'tensor', [(i, i ^ mask) for i in range(size)])  22.6 us
    ppermute x9, starting transfers between devices, around(): return lax.ppermute(value, 'dp', [(i, (i + k) % G) for i in range(G)])  14.7 us
    ppermute x9, waiting for transfers between devices, around(): return lax.ppermute(value, 'dp', [(i, (i + k) % G) for i in range(G)])  9.04 us
    all_gather x1, blocking collectives, shards(): mod = lax.all_gather(mod_part, 'tensor', axis=1, tiled=True).reshape(6, D)  9.03 us
    unnamed x98, local copies, waits for them, and re-layouts  5.67 us
  transfers between devices with their start and end apart: 48, of which 24 were waited for; matrix products, arithmetic and copies ran while one was open for 4% of the time, Pallas kernels for 31%

profile of v4, /device:TPU:0, one launch (start us, length us, event | category | flops | bytes accessed | tf_op | source)
XLA Modules:
  0.0 219.8 jit_solution(16266407119980920314)
XLA Ops:
  7.3 1.9 shard_map.415
  9.3 2.0 shard_map.421
  11.5 3.1 %collective-permute-start = (f32[1,1920]{1,0:T(1,128)S(1)}, f32[1,1920]{1,0:T(1,128)S(1)}, u32[]{:S(2)}, u32[]{:S(2)}) collective-permute-start(f32[1,1920]{1,0:T(1,128)S(1)} %maximum_convert_fusion.refs_0_), channel_id=1, source_target_pairs={{0,8},{8,16},{16,24},{24,0},{1,9},{9,17},{17,25},{25,1},{2,10},{10... | collective-permute-start | bytes 23048 | tf_op jit(solution)/shard_map/ppermute | solution.py:472
  14.6 2.6 %collective-permute-start.1 = (f32[1,1920]{1,0:T(1,128)S(1)}, f32[1,1920]{1,0:T(1,128)S(1)}, u32[]{:S(2)}, u32[]{:S(2)}) collective-permute-start(f32[1,1920]{1,0:T(1,128)S(1)} %maximum_convert_fusion.refs_0_), channel_id=1, source_target_pairs={{0,16},{8,24},{16,0},{24,8},{1,17},{9,25},{17,1},{25,9},{2,18},{10... | collective-permute-start | bytes 23048 | tf_op jit(solution)/shard_map/ppermute | solution.py:472
  19.2 1.6 collective-permute-done.2.refs_3_
  22.3 3.6 %collective-permute-start.4 = (f32[1,768]{1,0:T(1,128)S(1)}, f32[1,768]{1,0:T(1,128)S(1)}, u32[]{:S(2)}, u32[]{:S(2)}) collective-permute-start(f32[1,768]{1,0:T(1,128)S(1)} %get-tuple-element.232), channel_id=1, source_target_pairs={{0,16},{8,24},{16,0},{24,8},{1,17},{9,25},{17,1},{25,9},{2,18},{10... | collective-permute-start | bytes 9224 | tf_op jit(solution)/shard_map/ppermute | solution.py:472
  27.7 1.9 collective-permute-done.3
  29.6 9.0 %all_gather.13 = f32[1,6144]{1,0:T(1,128)S(1)} all-gather(f32[1,768]{1,0:T(1,128)S(1)} %add_add_fusion), channel_id=1, replica_groups=mesh['dp'=4,'tensor'=8] {'tensor'}, dimensions={1}, use_global_device_ids=true | all-gather | bytes 27648 | tf_op jit(solution)/shard_map/all_gather | solution.py:514
  41.1 2.3 %shard_map.417 = (bf16[1024,384]{1,0:T(8,128)(2,1)}, bf16[128,1024]{1,0:T(8,128)(2,1)}) custom-call(bf16[1024,512]{1,0:T(8,128)(2,1)} %all-gather.4.cloned.1.call-done.first_ref), custom_call_target="tpu_custom_call" | custom-call | bytes 2621440 | tf_op jit(solution)/shard_map/pallas_call | solution.py:76
  43.4 1.5 collective-permute-start.6
  44.9 1.5 collective-permute-start.7
  47.1 5.4 %shard_map.418 = (bf16[1024,1024]{1,0:T(8,128)(2,1)}, bf16[1024,384]{1,0:T(8,128)(2,1)}) custom-call(bf16[1024,1024]{1,0:T(8,128)(2,1)} %x_ref.3, f32[6,1024]{1,0:T(8,128)} %reshape.132.mod_ref.refs_17_.refs_5_, f32[1,384]{1,0:T(1,128)} %reshape.133.bias_ref, bf16[1024,384]{1,0:T(8,128)(2,1)} %get-tuple-element.125.w_ref), custom_call_target="tpu_custom_call" | custom-call | flops 805306368 | bytes 6291456 | tf_op jit(solution)/shard_map/pallas_call | solution.py:76
  52.7 1.5 collective-permute-start.9
  55.9 3.5 %shard_map.419 = (bf16[1024,128]{1,0:T(8,128)(2,1)S(1)}, f32[2,1024]{1,0:T(2,128)S(1)}) custom-call(bf16[1024,384]{1,0:T(8,128)(2,1)S(1)} %copy-done.11, bf16[1024,384]{1,0:T(8,128)(2,1)S(1)} %copy-done.11), custom_call_target="tpu_custom_call" | custom-call | flops 2147483648 | bytes 524288 | tf_op jit(solution)/shard_map/pallas_call | solution.py:76
  59.4 1.9 collective-permute-done.9.refs_14_
  62.5 6.7 %collective-permute-done.13.refs_2_ = bf16[1024,128]{1,0:T(8,128)(2,1)S(1)} collective-permute-done((bf16[1024,128]{1,0:T(8,128)(2,1)S(1)}, bf16[1024,128]{1,0:T(8,128)(2,1)S(1)}, u32[]{:S(2)}, u32[]{:S(2)}) %collective-permute-start.13) | collective-permute-done | bytes 262176 | tf_op jit(solution)/shard_map/ppermute | solution.py:394
  70.2 6.0 %collective-permute-done.17.refs_6_ = bf16[1024,128]{1,0:T(8,128)(2,1)S(1)} collective-permute-done((bf16[1024,128]{1,0:T(8,128)(2,1)S(1)}, bf16[1024,128]{1,0:T(8,128)(2,1)S(1)}, u32[]{:S(2)}, u32[]{:S(2)}) %collective-permute-start.17) | collective-permute-done | bytes 262176 | tf_op jit(solution)/shard_map/ppermute | solution.py:394
  78.3 8.5 %shard_map.420 = (bf16[1024,1024]{1,0:T(8,128)(2,1)}, f32[128,1024]{1,0:T(8,128)}) custom-call(s32[2]{0:T(128)} %copy-done.7, bf16[1024,128]{1,0:T(8,128)(2,1)} %copy-done.9, bf16[1024,128]{1,0:T(8,128)(2,1)} %copy-done.35, bf16[1024,128]{1,0:T(8,128)(2,1)} %copy-done.32, bf16[1024,128]{1,0:T(8,128)(2,1)} %collective-permute-done.14.refs_3_, ...), custom_call_target="tpu_custom_call" | custom-call | flops 2147483648 | bytes 8388608 | tf_op jit(solution)/shard_map/pallas_call | solution.py:84
  86.9 1.9 all-gather.6.cloned.1.call-done
  88.7 10.1 %shard_map.422 = (bf16[1024,512]{1,0:T(8,128)(2,1)}, bf16[1024,512]{1,0:T(8,128)(2,1)}, bf16[4,128,1024]{2,1,0:T(8,128)(2,1)}, bf16[4,128,1024]{2,1,0:T(8,128)(2...) custom-call(s32[2]{0:T(128)} %copy-done.7, ...), custom_call_target="tpu_custom_call" | custom-call | flops 4294967296 | bytes 12582912 | tf_op jit(solution)/shard_map/pallas_call | solution.py:84
  98.9 2.9 %collective-permute-done.20.refs_1_ = bf16[4,128,1024]{2,1,0:T(8,128)(2,1)S(1)} collective-permute-done((bf16[4,128,1024]{2,1,0:T(8,128)(2,1)}, bf16[4,128,1024]{2,1,0:T(8,128)(2,1)S(1)}, u32[]{:S(2)}, u32[]{:S(2)}) %collective-permute-start.20) | collective-permute-done | bytes 1048608 | tf_op jit(solution)/shard_map/ppermute | solution.py:394
  101.8 1.5 shard_map.423
  103.3 1.5 collective-permute-start.21
  104.9 1.5 collective-permute-start.22
  106.3 6.6 %shard_map.424 = bf16[4,1024,256]{2,1,0:T(8,128)(2,1)} custom-call(bf16[1024,1024]{1,0:T(8,128)(2,1)} %get-tuple-element.135.in_ref, bf16[1024,512]{1,0:T(8,128)(2,1)} %get-tuple-element.143.dpre_ref, bf16[1024,512]{1,0:T(8,128)(2,1)} %get-tuple-element.144.act_ref, bf16[1024,1024]{1,0:T(8,128)(2,1)} %cot_ref.3, f32[6,1024]{1,0:T(8,128)} %reshape.132.mod_ref.refs_17_.refs_5_), custom_call_target="tpu_custom_call" | custom-call | flops 2147483648 | bytes 8388608 | tf_op jit(solution)/shard_map/pallas_call | solution.py:76
  113.1 1.5 collective-permute-start.23
  118.2 1.4 collective-permute-done.24.refs_3_
  122.1 5.2 %collective-permute-done.26.refs_2_ = bf16[128,1024]{1,0:T(8,128)(2,1)S(1)} collective-permute-done((bf16[128,1024]{1,0:T(8,128)(2,1)S(1)}, bf16[128,1024]{1,0:T(8,128)(2,1)S(1)}, u32[]{:S(2)}, u32[]{:S(2)}) %collective-permute-start.26) | collective-permute-done | bytes 262176 | tf_op jit(solution)/shard_map/ppermute | solution.py:394
  128.8 4.9 %collective-permute-done.30.refs_6_ = bf16[128,1024]{1,0:T(8,128)(2,1)S(1)} collective-permute-done((bf16[128,1024]{1,0:T(8,128)(2,1)S(1)}, bf16[128,1024]{1,0:T(8,128)(2,1)S(1)}, u32[]{:S(2)}, u32[]{:S(2)}) %collective-permute-start.30) | collective-permute-done | bytes 262176 | tf_op jit(solution)/shard_map/ppermute | solution.py:394
  133.8 1.4 collective-permute-done.31.refs_7_
  135.9 11.5 %shard_map.427 = (bf16[1024,384]{1,0:T(8,128)(2,1)}, f32[1,384]{1,0:T(1,128)}, f32[1,1024]{1,0:T(1,128)}, bf16[1024,128]{1,0:T(8,128)(2,1)}) custom-call(s32[2]{0:T(128)} %copy-done.7, bf16[128,1024]{1,0:T(8,128)(2,1)} %copy-done.10, bf16[128,1024]{1,0:T(8,128)(2,1)} %copy-done.40, bf16[128,1024]{1,0:T(8,128)(2,1)} %copy-done.36, ...), custom_call_target="tpu_custom_call" | custom-call | flops 5368709120 | bytes 6291456 | tf_op jit(solution)/shard_map/pallas_call | solution.py:84
  148.5 5.9 %shard_map.428 = (bf16[4,128,1024]{2,1,0:T(8,128)(2,1)}, bf16[4,128,1024]{2,1,0:T(8,128)(2,1)}, f32[2,1024]{1,0:T(2,128)S(1)}) custom-call(s32[2]{0:T(128)S(1)} %copy-done.8, bf16[1024,384]{1,0:T(8,128)(2,1)S(1)} %copy-done.1, bf16[1024,384]{1,0:T(8,128)(2,1)} %get-tuple-element.125.w_ref, bf16[1024,1024]{1,0:T(8,128)(2,1)} %x_ref.3), custom_call_target="tpu_custom_call" | custom-call | flops 805306368 | bytes 6291456 | tf_op jit(solution)/shard_map/pallas_call | solution.py:84
  155.4 3.6 %all-to-all-start = ((f32[8,1,768]{2,1,0:T(1,128)}), f32[8,1,768]{2,1,0:T(1,128)S(1)}, u32[]{:S(2)}, u32[]{:S(2)}) async-start(f32[8,1,768]{2,1,0:T(1,128)} %all_to_all.14), calls=%async_computation.1 | async-start | bytes 49152 | tf_op jit(solution)/shard_map/all_to_all | solution.py:615
  159.8 3.5 %shard_map.429 = (f32[256,512]{1,0:T(8,128)}, f32[256,512]{1,0:T(8,128)}, f32[256,512]{1,0:T(8,128)}, f32[512,256]{1,0:T(8,128)}, f32[512,256]{1,0:T(8,128)}, /*index=5*/f32[512,256]{1,0:T(8,128)}) custom-call(bf16[1024,256]{1,0:T(8,128)(2,1)} %reduce-scatter.3.cloned.1.call-done.gup_ref.gdown_ref, ...), custom_call_target="tpu_custom_call" | custom-call | bytes 6815744 | tf_op jit(solution)/shard_map/pallas_call | solution.py:76
  163.9 4.5 %shard_map.434 = bf16[1024,512]{1,0:T(8,128)(2,1)} custom-call(bf16[1024,1024]{1,0:T(8,128)(2,1)} %get-tuple-element.203.in_ref, bf16[1024,384]{1,0:T(8,128)(2,1)S(1)} %copy-done.2, bf16[1024,128]{1,0:T(8,128)(2,1)S(1)} %copy-done.5), custom_call_target="tpu_custom_call" | custom-call | flops 805306368 | bytes 4194304 | tf_op jit(solution)/shard_map/pallas_call | solution.py:76
  168.6 1.7 collective-permute-start.34
  170.4 1.9 collective-permute-start.32
  172.4 2.6 %collective-permute-done.33 = f32[1,3584]{1,0:T(1,128)S(1)} collective-permute-done((f32[1,3584]{1,0:T(1,128)S(1)}, f32[1,3584]{1,0:T(1,128)S(1)}, u32[]{:S(2)}, u32[]{:S(2)}) %collective-permute-start.33) | collective-permute-done | bytes 14368 | tf_op jit(solution)/shard_map/ppermute | solution.py:472
  177.0 3.3 %shard_map.430 = (f32[2,128,1024]{2,1,0:T(8,128)S(1)}, bf16[2,128,1024]{2,1,0:T(8,128)(2,1)}, f32[2,128,1024]{2,1,0:T(8,128)S(1)}, bf16[2,128,1024]{2,1,0:T(8,128)(2,1)}) custom-call(bf16[4,128,1024]{2,1,0:T(8,128)(2,1)} %get-tuple-element.177.refs_0_, bf16[4,128,1024]{2,1,0:T(8,128)(2,1)} %get-tuple-element.178.refs_1_, bf16[4,128,1024]{2,1,0:T(8,128)(2,1)} %copy-done.13, ...), custom_call_target="tpu_custom_call" | custom-call | bytes 10485760 | tf_op jit(solution)/shard_map/pallas_call | solution.py:76
  180.4 1.5 collective-permute-start.37
  181.9 1.5 collective-permute-start.38
  184.2 3.3 %all-to-all-start.1 = ((f32[8,1,128]{2,1,0:T(1,128)}), f32[8,1,128]{2,1,0:T(1,128)S(1)}, u32[]{:S(2)}, u32[]{:S(2)}) async-start(f32[8,1,128]{2,1,0:T(1,128)} %bitcast.14), calls=%async_computation.2 | async-start | bytes 8192 | tf_op jit(solution)/shard_map/all_to_all | solution.py:664
  188.9 4.3 %shard_map.433 = (f32[256,768]{1,0:T(8,128)}, f32[256,768]{1,0:T(8,128)}, f32[256,768]{1,0:T(8,128)}) custom-call(bf16[4,256]{1,0:T(4,128)(2,1)} %copy-done.6, bf16[4,768]{1,0:T(4,128)(2,1)} %slice.106.dmod_ref, f32[256,768]{1,0:T(8,128)} %refs_0_.4, f32[256,768]{1,0:T(8,128)} %refs_1_.4, f32[256,768]{1,0:T(8,128)} %refs_2_.4), custom_call_target="tpu_custom_call" | custom-call | bytes 4718592 | tf_op jit(solution)/shard_map/pallas_call | solution.py:76
  196.4 3.6 %collective-permute-start.39 = (bf16[1,128,1024]{2,1,0:T(8,128)(2,1)S(1)}, bf16[1,128,1024]{2,1,0:T(8,128)(2,1)S(1)}, u32[]{:S(2)}, u32[]{:S(2)}) collective-permute-start(bf16[1,128,1024]{2,1,0:T(8,128)(2,1)S(1)} %get-tuple-element.186), channel_id=1, source_target_pairs={{0,4},{1,5},{2,6},{3,7},{4,0},{5,1},{6,2},{7,3},{8,12},{9,13},{10,... | collective-permute-start | bytes 786440 | tf_op jit(solution)/shard_map/ppermute | solution.py:394
  201.7 4.6 %collective-permute-done.39.refs_1_ = bf16[1,128,1024]{2,1,0:T(8,128)(2,1)S(1)} collective-permute-done((bf16[1,128,1024]{2,1,0:T(8,128)(2,1)S(1)}, bf16[1,128,1024]{2,1,0:T(8,128)(2,1)S(1)}, u32[]{:S(2)}, u32[]{:S(2)}) %collective-permute-start.39) | collective-permute-done | bytes 262176 | tf_op jit(solution)/shard_map/ppermute | solution.py:394
  206.3 1.5 collective-permute-done.40.refs_3_
  207.8 2.6 %shard_map.432 = (f32[128,1024]{1,0:T(8,128)}, f32[128,1024]{1,0:T(8,128)}) custom-call(f32[1,128,1024]{2,1,0:T(8,128)S(1)} %get-tuple-element.185.refs_0_, bf16[1,128,1024]{2,1,0:T(8,128)(2,1)S(1)} %collective-permute-done.39.refs_1_, f32[1,128,1024]{2,1,0:T(8,128)S(1)} %get-tuple-element.187.refs_2_, ...), custom_call_target="tpu_custom_call" | custom-call | bytes 3670016 | tf_op jit(solution)/shard_map/pallas_call | solution.py:76
  210.4 2.9 %shard_map.435 = (f32[256,384]{1,0:T(8,128)}, f32[256,384]{1,0:T(8,128)}, f32[256,384]{1,0:T(8,128)}, f32[128,256]{1,0:T(8,128)}, f32[128,256]{1,0:T(8,128)}, /*index=5*/f32[128,256]{1,0:T(8,128)}) custom-call(bf16[256,512]{1,0:T(8,128)(2,1)} %reduce-scatter.5.cloned.1.call-done.grad_ref, f32[256,384]{1,0:T(8,128)} %refs_0_.5, f32[256,384]{1,0:T(8,128)} %refs_1_.5, ...), custom_call_target="tpu_custom_call" | custom-call | bytes 4194304 | tf_op jit(solution)/shard_map/pallas_call | solution.py:76
  (223 shorter events, 36.0 us)
Async XLA Ops:
  7.2 33.9 %all-gather.4.cloned.1.call-start = ((), (), s32[]{:S(2)}) async-start(), calls=%async_computation.4 | async-start | bytes 1310720 | tf_op jit(solution)/shard_map/all_gather | solution.py:485
  9.2 79.5 %all-gather.6.cloned.1.call-start = ((), (), s32[]{:S(2)}) async-start(), calls=%async_computation.7 | async-start | bytes 2621440 | tf_op jit(solution)/shard_map/all_gather | solution.py:486
  11.3 143.5 %reduce-scatter.3.cloned.1.call-start = ((), (), s32[]{:S(2)}) async-start(), calls=%async_computation.5 | async-start | bytes 2621440 | tf_op jit(solution)/shard_map/reduce_scatter | solution.py:584
  11.5 7.2 %collective-permute-start = (f32[1,1920]{1,0:T(1,128)S(1)}, f32[1,1920]{1,0:T(1,128)S(1)}, u32[]{:S(2)}, u32[]{:S(2)}) collective-permute-start(f32[1,1920]{1,0:T(1,128)S(1)} %maximum_convert_fusion.refs_0_), channel_id=1, source_target_pairs={{0,8},{8,16},{16,24},{24,0},{1,9},{9,17},{17,25},{25,1},{2,10},{10... | collective-permute-start | bytes 23048 | tf_op jit(solution)/shard_map/ppermute | solution.py:472
  14.6 4.6 %collective-permute-start.1 = (f32[1,1920]{1,0:T(1,128)S(1)}, f32[1,1920]{1,0:T(1,128)S(1)}, u32[]{:S(2)}, u32[]{:S(2)}) collective-permute-start(f32[1,1920]{1,0:T(1,128)S(1)} %maximum_convert_fusion.refs_0_), channel_id=1, source_target_pairs={{0,16},{8,24},{16,0},{24,8},{1,17},{9,25},{17,1},{25,9},{2,18},{10... | collective-permute-start | bytes 23048 | tf_op jit(solution)/shard_map/ppermute | solution.py:472
  17.2 3.6 %collective-permute-start.2 = (f32[1,1920]{1,0:T(1,128)S(1)}, f32[1,1920]{1,0:T(1,128)S(1)}, u32[]{:S(2)}, u32[]{:S(2)}) collective-permute-start(f32[1,1920]{1,0:T(1,128)S(1)} %maximum_convert_fusion.refs_0_), channel_id=1, source_target_pairs={{0,24},{8,0},{16,8},{24,16},{1,25},{9,1},{17,9},{25,17},{2,26},{10... | collective-permute-start | bytes 23048 | tf_op jit(solution)/shard_map/ppermute | solution.py:472
  22.1 5.5 %collective-permute-start.5 = (f32[1,768]{1,0:T(1,128)S(1)}, f32[1,768]{1,0:T(1,128)S(1)}, u32[]{:S(2)}, u32[]{:S(2)}) collective-permute-start(f32[1,768]{1,0:T(1,128)S(1)} %get-tuple-element.231), channel_id=1, source_target_pairs={{0,8},{8,16},{16,24},{24,0},{1,9},{9,17},{17,25},{25,1},{2,10},{10... | collective-permute-start | bytes 9224 | tf_op jit(solution)/shard_map/ppermute | solution.py:472
  22.3 5.4 %collective-permute-start.4 = (f32[1,768]{1,0:T(1,128)S(1)}, f32[1,768]{1,0:T(1,128)S(1)}, u32[]{:S(2)}, u32[]{:S(2)}) collective-permute-start(f32[1,768]{1,0:T(1,128)S(1)} %get-tuple-element.232), channel_id=1, source_target_pairs={{0,16},{8,24},{16,0},{24,8},{1,17},{9,25},{17,1},{25,9},{2,18},{10... | collective-permute-start | bytes 9224 | tf_op jit(solution)/shard_map/ppermute | solution.py:472
  25.9 3.7 %collective-permute-start.3 = (f32[1,768]{1,0:T(1,128)S(1)}, f32[1,768]{1,0:T(1,128)S(1)}, u32[]{:S(2)}, u32[]{:S(2)}) collective-permute-start(f32[1,768]{1,0:T(1,128)S(1)} %get-tuple-element.230), channel_id=1, source_target_pairs={{0,24},{8,0},{16,8},{24,16},{1,25},{9,1},{17,9},{25,17},{2,26},{10... | collective-permute-start | bytes 9224 | tf_op jit(solution)/shard_map/ppermute | solution.py:472
  43.4 9.0 %collective-permute-start.6 = (bf16[128,1024]{1,0:T(8,128)(2,1)}, bf16[128,1024]{1,0:T(8,128)(2,1)S(1)}, u32[]{:S(2)}, u32[]{:S(2)}) collective-permute-start(bf16[128,1024]{1,0:T(8,128)(2,1)} %get-tuple-element.123.refs_8_), channel_id=1, source_target_pairs={{0,2},{1,3},{2,0},{3,1},{4,6},{5,7},{6,4},{7,5},{8,10},{9,11},{10,... | collective-permute-start | bytes 786440 | tf_op jit(solution)/shard_map/ppermute | solution.py:394
  44.9 7.8 %collective-permute-start.7 = (bf16[128,1024]{1,0:T(8,128)(2,1)}, bf16[128,1024]{1,0:T(8,128)(2,1)S(1)}, u32[]{:S(2)}, u32[]{:S(2)}) collective-permute-start(bf16[128,1024]{1,0:T(8,128)(2,1)} %get-tuple-element.123.refs_8_), channel_id=1, source_target_pairs={{0,4},{1,5},{2,6},{3,7},{4,0},{5,1},{6,2},{7,3},{8,12},{9,13},{10,... | collective-permute-start | bytes 786440 | tf_op jit(solution)/shard_map/ppermute | solution.py:394
  46.4 6.4 %collective-permute-start.8 = (bf16[128,1024]{1,0:T(8,128)(2,1)}, bf16[128,1024]{1,0:T(8,128)(2,1)S(1)}, u32[]{:S(2)}, u32[]{:S(2)}) collective-permute-start(bf16[128,1024]{1,0:T(8,128)(2,1)} %get-tuple-element.123.refs_8_), channel_id=1, source_target_pairs={{0,1},{1,0},{2,3},{3,2},{4,5},{5,4},{6,7},{7,6},{8,9},{9,8},{10,11... | collective-permute-start | bytes 786440 | tf_op jit(solution)/shard_map/ppermute | solution.py:394
  52.7 8.6 %collective-permute-start.9 = (bf16[128,1024]{1,0:T(8,128)(2,1)S(1)}, bf16[128,1024]{1,0:T(8,128)(2,1)S(1)}, u32[]{:S(2)}, u32[]{:S(2)}) collective-permute-start(bf16[128,1024]{1,0:T(8,128)(2,1)S(1)} %collective-permute-done.6.refs_10_), channel_id=1, source_target_pairs={{0,4},{1,5},{2,6},{3,7},{4,0},{5,1},{6,2},{7,3},{8,12},{9,13},{10,... | collective-permute-start | bytes 786440 | tf_op jit(solution)/shard_map/ppermute | solution.py:394
  54.3 7.0 %collective-permute-start.10 = (bf16[128,1024]{1,0:T(8,128)(2,1)S(1)}, bf16[128,1024]{1,0:T(8,128)(2,1)S(1)}, u32[]{:S(2)}, u32[]{:S(2)}) collective-permute-start(bf16[128,1024]{1,0:T(8,128)(2,1)S(1)} %collective-permute-done.6.refs_10_), channel_id=1, source_target_pairs={{0,1},{1,0},{2,3},{3,2},{4,5},{5,4},{6,7},{7,6},{8,9},{9,8},{10,11... | collective-permute-start | bytes 786440 | tf_op jit(solution)/shard_map/ppermute | solution.py:394
  54.3 7.0 %collective-permute-start.11 = (bf16[128,1024]{1,0:T(8,128)(2,1)S(1)}, bf16[128,1024]{1,0:T(8,128)(2,1)S(1)}, u32[]{:S(2)}, u32[]{:S(2)}) collective-permute-start(bf16[128,1024]{1,0:T(8,128)(2,1)S(1)} %collective-permute-done.7.refs_12_), channel_id=1, source_target_pairs={{0,1},{1,0},{2,3},{3,2},{4,5},{5,4},{6,7},{7,6},{8,9},{9,8},{10,11... | collective-permute-start | bytes 786440 | tf_op jit(solution)/shard_map/ppermute | solution.py:394
  61.3 7.9 %collective-permute-start.13 = (bf16[1024,128]{1,0:T(8,128)(2,1)S(1)}, bf16[1024,128]{1,0:T(8,128)(2,1)S(1)}, u32[]{:S(2)}, u32[]{:S(2)}) collective-permute-start(bf16[1024,128]{1,0:T(8,128)(2,1)S(1)} %get-tuple-element.130.refs_0_.refs_11_), channel_id=1, source_target_pairs={{0,2},{1,3},{2,0},{3,1},{4,6},{5,7},{6,4},{7,5},{8,10},{9,11},{10,... | collective-permute-start | bytes 786440 | tf_op jit(solution)/shard_map/ppermute | solution.py:394
  62.0 7.8 %collective-permute-start.15 = (bf16[1024,128]{1,0:T(8,128)(2,1)S(1)}, bf16[1024,128]{1,0:T(8,128)(2,1)S(1)}, u32[]{:S(2)}, u32[]{:S(2)}) collective-permute-start(bf16[1024,128]{1,0:T(8,128)(2,1)S(1)} %get-tuple-element.130.refs_0_.refs_11_), channel_id=1, source_target_pairs={{0,4},{1,5},{2,6},{3,7},{4,0},{5,1},{6,2},{7,3},{8,12},{9,13},{10,... | collective-permute-start | bytes 786440 | tf_op jit(solution)/shard_map/ppermute | solution.py:394
  69.2 7.0 %collective-permute-start.17 = (bf16[1024,128]{1,0:T(8,128)(2,1)S(1)}, bf16[1024,128]{1,0:T(8,128)(2,1)S(1)}, u32[]{:S(2)}, u32[]{:S(2)}) collective-permute-start(bf16[1024,128]{1,0:T(8,128)(2,1)S(1)} %collective-permute-done.13.refs_2_), channel_id=1, source_target_pairs={{0,4},{1,5},{2,6},{3,7},{4,0},{5,1},{6,2},{7,3},{8,12},{9,13},{10,... | collective-permute-start | bytes 786440 | tf_op jit(solution)/shard_map/ppermute | solution.py:394
  69.2 8.3 %collective-permute-start.12 = (bf16[1024,128]{1,0:T(8,128)(2,1)S(1)}, bf16[1024,128]{1,0:T(8,128)(2,1)S(1)}, u32[]{:S(2)}, u32[]{:S(2)}) collective-permute-start(bf16[1024,128]{1,0:T(8,128)(2,1)S(1)} %get-tuple-element.130.refs_0_.refs_11_), channel_id=1, source_target_pairs={{0,1},{1,0},{2,3},{3,2},{4,5},{5,4},{6,7},{7,6},{8,9},{9,8},{10,11... | collective-permute-start | bytes 786440 | tf_op jit(solution)/shard_map/ppermute | solution.py:394
  69.2 8.3 %collective-permute-start.19 = (bf16[128,1024]{1,0:T(8,128)(2,1)S(1)}, bf16[128,1024]{1,0:T(8,128)(2,1)S(1)}, u32[]{:S(2)}, u32[]{:S(2)}) collective-permute-start(bf16[128,1024]{1,0:T(8,128)(2,1)S(1)} %collective-permute-done.9.refs_14_), channel_id=1, source_target_pairs={{0,1},{1,0},{2,3},{3,2},{4,5},{5,4},{6,7},{7,6},{8,9},{9,8},{10,11... | collective-permute-start | bytes 786440 | tf_op jit(solution)/shard_map/ppermute | solution.py:394
  69.7 7.8 %collective-permute-start.14 = (bf16[1024,128]{1,0:T(8,128)(2,1)S(1)}, bf16[1024,128]{1,0:T(8,128)(2,1)}, u32[]{:S(2)}, u32[]{:S(2)}) collective-permute-start(bf16[1024,128]{1,0:T(8,128)(2,1)S(1)} %collective-permute-done.13.refs_2_), channel_id=1, source_target_pairs={{0,1},{1,0},{2,3},{3,2},{4,5},{5,4},{6,7},{7,6},{8,9},{9,8},{10,11... | collective-permute-start | bytes 786440 | tf_op jit(solution)/shard_map/ppermute | solution.py:394
  69.8 7.7 %collective-permute-start.16 = (bf16[1024,128]{1,0:T(8,128)(2,1)S(1)}, bf16[1024,128]{1,0:T(8,128)(2,1)}, u32[]{:S(2)}, u32[]{:S(2)}) collective-permute-start(bf16[1024,128]{1,0:T(8,128)(2,1)S(1)} %collective-permute-done.15.refs_4_), channel_id=1, source_target_pairs={{0,1},{1,0},{2,3},{3,2},{4,5},{5,4},{6,7},{7,6},{8,9},{9,8},{10,11... | collective-permute-start | bytes 786440 | tf_op jit(solution)/shard_map/ppermute | solution.py:394
  76.2 1.7 collective-permute-start.18
  98.9 2.9 %collective-permute-start.20 = (bf16[4,128,1024]{2,1,0:T(8,128)(2,1)}, bf16[4,128,1024]{2,1,0:T(8,128)(2,1)S(1)}, u32[]{:S(2)}, u32[]{:S(2)}) collective-permute-start(bf16[4,128,1024]{2,1,0:T(8,128)(2,1)} %get-tuple-element.137), channel_id=1, source_target_pairs={{0,1},{1,0},{2,3},{3,2},{4,5},{5,4},{6,7},{7,6},{8,9},{9,8},{10,11... | collective-permute-start | bytes 3145736 | tf_op jit(solution)/shard_map/ppermute | solution.py:394
  103.3 9.6 %collective-permute-start.21 = (bf16[2,128,512]{2,1,0:T(8,128)(2,1)S(1)}, bf16[2,128,512]{2,1,0:T(8,128)(2,1)S(1)}, u32[]{:S(2)}, u32[]{:S(2)}) collective-permute-start(bf16[2,128,512]{2,1,0:T(8,128)(2,1)S(1)} %get-tuple-element.139), channel_id=1, source_target_pairs={{0,2},{1,3},{2,0},{3,1},{4,6},{5,7},{6,4},{7,5},{8,10},{9,11},{10,... | collective-permute-start | bytes 786440 | tf_op jit(solution)/shard_map/ppermute | solution.py:394
  104.9 8.1 %collective-permute-start.22 = (bf16[2,128,512]{2,1,0:T(8,128)(2,1)S(1)}, bf16[2,128,512]{2,1,0:T(8,128)(2,1)S(1)}, u32[]{:S(2)}, u32[]{:S(2)}) collective-permute-start(bf16[2,128,512]{2,1,0:T(8,128)(2,1)S(1)} %get-tuple-element.141), channel_id=1, source_target_pairs={{0,4},{1,5},{2,6},{3,7},{4,0},{5,1},{6,2},{7,3},{8,12},{9,13},{10,... | collective-permute-start | bytes 786440 | tf_op jit(solution)/shard_map/ppermute | solution.py:394
  113.1 5.0 %collective-permute-start.23 = (bf16[1,128,512]{2,1,0:T(8,128)(2,1)S(1)}, bf16[1,128,512]{2,1,0:T(8,128)(2,1)S(1)}, u32[]{:S(2)}, u32[]{:S(2)}) collective-permute-start(bf16[1,128,512]{2,1,0:T(8,128)(2,1)S(1)} %get-tuple-element.150), channel_id=1, source_target_pairs={{0,4},{1,5},{2,6},{3,7},{4,0},{5,1},{6,2},{7,3},{8,12},{9,13},{10,... | collective-permute-start | bytes 393224 | tf_op jit(solution)/shard_map/ppermute | solution.py:394
  114.6 5.0 %collective-permute-start.24 = (bf16[1,128,512]{2,1,0:T(8,128)(2,1)S(1)}, bf16[1,128,512]{2,1,0:T(8,128)(2,1)S(1)}, u32[]{:S(2)}, u32[]{:S(2)}) collective-permute-start(bf16[1,128,512]{2,1,0:T(8,128)(2,1)S(1)} %get-tuple-element.152), channel_id=1, source_target_pairs={{0,2},{1,3},{2,0},{3,1},{4,6},{5,7},{6,4},{7,5},{8,10},{9,11},{10,... | collective-permute-start | bytes 393224 | tf_op jit(solution)/shard_map/ppermute | solution.py:394
  120.9 6.4 %collective-permute-start.26 = (bf16[128,1024]{1,0:T(8,128)(2,1)S(1)}, bf16[128,1024]{1,0:T(8,128)(2,1)S(1)}, u32[]{:S(2)}, u32[]{:S(2)}) collective-permute-start(bf16[128,1024]{1,0:T(8,128)(2,1)S(1)} %get-tuple-element.154.refs_0_), channel_id=1, source_target_pairs={{0,2},{1,3},{2,0},{3,1},{4,6},{5,7},{6,4},{7,5},{8,10},{9,11},{10,... | collective-permute-start | bytes 786440 | tf_op jit(solution)/shard_map/ppermute | solution.py:394
  121.5 7.2 %collective-permute-start.28 = (bf16[128,1024]{1,0:T(8,128)(2,1)S(1)}, bf16[128,1024]{1,0:T(8,128)(2,1)S(1)}, u32[]{:S(2)}, u32[]{:S(2)}) collective-permute-start(bf16[128,1024]{1,0:T(8,128)(2,1)S(1)} %get-tuple-element.154.refs_0_), channel_id=1, source_target_pairs={{0,4},{1,5},{2,6},{3,7},{4,0},{5,1},{6,2},{7,3},{8,12},{9,13},{10,... | collective-permute-start | bytes 786440 | tf_op jit(solution)/shard_map/ppermute | solution.py:394
  127.3 6.4 %collective-permute-start.30 = (bf16[128,1024]{1,0:T(8,128)(2,1)S(1)}, bf16[128,1024]{1,0:T(8,128)(2,1)S(1)}, u32[]{:S(2)}, u32[]{:S(2)}) collective-permute-start(bf16[128,1024]{1,0:T(8,128)(2,1)S(1)} %collective-permute-done.26.refs_2_), channel_id=1, source_target_pairs={{0,4},{1,5},{2,6},{3,7},{4,0},{5,1},{6,2},{7,3},{8,12},{9,13},{10,... | collective-permute-start | bytes 786440 | tf_op jit(solution)/shard_map/ppermute | solution.py:394
  128.2 5.5 %collective-permute-start.25 = (bf16[128,1024]{1,0:T(8,128)(2,1)S(1)}, bf16[128,1024]{1,0:T(8,128)(2,1)S(1)}, u32[]{:S(2)}, u32[]{:S(2)}) collective-permute-start(bf16[128,1024]{1,0:T(8,128)(2,1)S(1)} %get-tuple-element.154.refs_0_), channel_id=1, source_target_pairs={{0,1},{1,0},{2,3},{3,2},{4,5},{5,4},{6,7},{7,6},{8,9},{9,8},{10,11... | collective-permute-start | bytes 786440 | tf_op jit(solution)/shard_map/ppermute | solution.py:394
  128.2 5.5 %collective-permute-start.27 = (bf16[128,1024]{1,0:T(8,128)(2,1)S(1)}, bf16[128,1024]{1,0:T(8,128)(2,1)S(1)}, u32[]{:S(2)}, u32[]{:S(2)}) collective-permute-start(bf16[128,1024]{1,0:T(8,128)(2,1)S(1)} %collective-permute-done.26.refs_2_), channel_id=1, source_target_pairs={{0,1},{1,0},{2,3},{3,2},{4,5},{5,4},{6,7},{7,6},{8,9},{9,8},{10,11... | collective-permute-start | bytes 786440 | tf_op jit(solution)/shard_map/ppermute | solution.py:394
  128.7 5.1 %collective-permute-start.29 = (bf16[128,1024]{1,0:T(8,128)(2,1)S(1)}, bf16[128,1024]{1,0:T(8,128)(2,1)S(1)}, u32[]{:S(2)}, u32[]{:S(2)}) collective-permute-start(bf16[128,1024]{1,0:T(8,128)(2,1)S(1)} %collective-permute-done.28.refs_4_), channel_id=1, source_target_pairs={{0,1},{1,0},{2,3},{3,2},{4,5},{5,4},{6,7},{7,6},{8,9},{9,8},{10,11... | collective-permute-start | bytes 786440 | tf_op jit(solution)/shard_map/ppermute | solution.py:394
  133.7 1.5 collective-permute-start.31
  155.4 8.4 %all-to-all-start = ((f32[8,1,768]{2,1,0:T(1,128)}), f32[8,1,768]{2,1,0:T(1,128)S(1)}, u32[]{:S(2)}, u32[]{:S(2)}) async-start(f32[8,1,768]{2,1,0:T(1,128)} %all_to_all.14), calls=%async_computation.1 | async-start | bytes 49152 | tf_op jit(solution)/shard_map/all_to_all | solution.py:615
  159.1 51.3 %reduce-scatter.5.cloned.1.call-start = ((), (), s32[]{:S(2)}) async-start(), calls=%async_computation.6 | async-start | bytes 1310720 | tf_op jit(solution)/shard_map/reduce_scatter | solution.py:635
  159.3 16.7 %collective-permute-start.35 = (bf16[4,128,1024]{2,1,0:T(8,128)(2,1)}, bf16[4,128,1024]{2,1,0:T(8,128)(2,1)S(1)}, u32[]{:S(2)}, u32[]{:S(2)}) collective-permute-start(bf16[4,128,1024]{2,1,0:T(8,128)(2,1)} %get-tuple-element.179), channel_id=1, source_target_pairs={{0,1},{1,0},{2,3},{3,2},{4,5},{5,4},{6,7},{7,6},{8,9},{9,8},{10,11... | collective-permute-start | bytes 3145736 | tf_op jit(solution)/shard_map/ppermute | solution.py:394
  159.8 17.3 %collective-permute-start.36 = (bf16[4,128,1024]{2,1,0:T(8,128)(2,1)}, bf16[4,128,1024]{2,1,0:T(8,128)(2,1)}, u32[]{:S(2)}, u32[]{:S(2)}) collective-permute-start(bf16[4,128,1024]{2,1,0:T(8,128)(2,1)} %get-tuple-element.180), channel_id=1, source_target_pairs={{0,1},{1,0},{2,3},{3,2},{4,5},{5,4},{6,7},{7,6},{8,9},{9,8},{10,11... | collective-permute-start | bytes 3145736 | tf_op jit(solution)/shard_map/ppermute | solution.py:394
  168.6 3.8 %collective-permute-start.34 = (f32[1,3584]{1,0:T(1,128)S(1)}, f32[1,3584]{1,0:T(1,128)S(1)}, u32[]{:S(2)}, u32[]{:S(2)}) collective-permute-start(f32[1,3584]{1,0:T(1,128)S(1)} %reshape.143), channel_id=1, source_target_pairs={{0,24},{8,0},{16,8},{24,16},{1,25},{9,1},{17,9},{25,17},{2,26},{10... | collective-permute-start | bytes 43016 | tf_op jit(solution)/shard_map/ppermute | solution.py:472
  170.3 4.7 %collective-permute-start.33 = (f32[1,3584]{1,0:T(1,128)S(1)}, f32[1,3584]{1,0:T(1,128)S(1)}, u32[]{:S(2)}, u32[]{:S(2)}) collective-permute-start(f32[1,3584]{1,0:T(1,128)S(1)} %reshape.143), channel_id=1, source_target_pairs={{0,16},{8,24},{16,0},{24,8},{1,17},{9,25},{17,1},{25,9},{2,18},{10... | collective-permute-start | bytes 43016 | tf_op jit(solution)/shard_map/ppermute | solution.py:472
  170.4 5.5 %collective-permute-start.32 = (f32[1,3584]{1,0:T(1,128)S(1)}, f32[1,3584]{1,0:T(1,128)S(1)}, u32[]{:S(2)}, u32[]{:S(2)}) collective-permute-start(f32[1,3584]{1,0:T(1,128)S(1)} %reshape.143), channel_id=1, source_target_pairs={{0,8},{8,16},{16,24},{24,0},{1,9},{9,17},{17,25},{25,1},{2,10},{10... | collective-permute-start | bytes 43016 | tf_op jit(solution)/shard_map/ppermute | solution.py:472
  180.4 14.8 %collective-permute-start.37 = (bf16[2,128,1024]{2,1,0:T(8,128)(2,1)}, bf16[2,128,1024]{2,1,0:T(8,128)(2,1)S(1)}, u32[]{:S(2)}, u32[]{:S(2)}) collective-permute-start(bf16[2,128,1024]{2,1,0:T(8,128)(2,1)} %get-tuple-element.182), channel_id=1, source_target_pairs={{0,2},{1,3},{2,0},{3,1},{4,6},{5,7},{6,4},{7,5},{8,10},{9,11},{10,... | collective-permute-start | bytes 1572872 | tf_op jit(solution)/shard_map/ppermute | solution.py:394
  181.9 13.3 %collective-permute-start.38 = (bf16[2,128,1024]{2,1,0:T(8,128)(2,1)}, bf16[2,128,1024]{2,1,0:T(8,128)(2,1)}, u32[]{:S(2)}, u32[]{:S(2)}) collective-permute-start(bf16[2,128,1024]{2,1,0:T(8,128)(2,1)} %get-tuple-element.184), channel_id=1, source_target_pairs={{0,4},{1,5},{2,6},{3,7},{4,0},{5,1},{6,2},{7,3},{8,12},{9,13},{10,... | collective-permute-start | bytes 1572872 | tf_op jit(solution)/shard_map/ppermute | solution.py:394
  184.2 10.3 %all-to-all-start.1 = ((f32[8,1,128]{2,1,0:T(1,128)}), f32[8,1,128]{2,1,0:T(1,128)S(1)}, u32[]{:S(2)}, u32[]{:S(2)}) async-start(f32[8,1,128]{2,1,0:T(1,128)} %bitcast.14), calls=%async_computation.2 | async-start | bytes 8192 | tf_op jit(solution)/shard_map/all_to_all | solution.py:664
  194.5 6.7 %collective-permute-start.41 = (f32[1,128]{1,0:T(1,128)S(1)}, f32[1,128]{1,0:T(1,128)S(1)}, u32[]{:S(2)}, u32[]{:S(2)}) collective-permute-start(f32[1,128]{1,0:T(1,128)S(1)} %bitcast.47), channel_id=1, source_target_pairs={{0,0},{1,1},{2,24},{3,25},{4,16},{5,17},{6,8},{7,9},{8,10},{9,11},... | collective-permute-start | bytes 1544 | tf_op jit(solution)/shard_map/ppermute | solution.py:667
  196.4 9.9 %collective-permute-start.39 = (bf16[1,128,1024]{2,1,0:T(8,128)(2,1)S(1)}, bf16[1,128,1024]{2,1,0:T(8,128)(2,1)S(1)}, u32[]{:S(2)}, u32[]{:S(2)}) collective-permute-start(bf16[1,128,1024]{2,1,0:T(8,128)(2,1)S(1)} %get-tuple-element.186), channel_id=1, source_target_pairs={{0,4},{1,5},{2,6},{3,7},{4,0},{5,1},{6,2},{7,3},{8,12},{9,13},{10,... | collective-permute-start | bytes 786440 | tf_op jit(solution)/shard_map/ppermute | solution.py:394
  200.1 7.7 %collective-permute-start.40 = (bf16[1,128,1024]{2,1,0:T(8,128)(2,1)S(1)}, bf16[1,128,1024]{2,1,0:T(8,128)(2,1)S(1)}, u32[]{:S(2)}, u32[]{:S(2)}) collective-permute-start(bf16[1,128,1024]{2,1,0:T(8,128)(2,1)S(1)} %get-tuple-element.188), channel_id=1, source_target_pairs={{0,2},{1,3},{2,0},{3,1},{4,6},{5,7},{6,4},{7,5},{8,10},{9,11},{10,... | collective-permute-start | bytes 786440 | tf_op jit(solution)/shard_map/ppermute | solution.py:394
  (44 other events, 348.5 us)
Sparse Core Ops, SparseCore 0:
  10.2 30.8 all-gather.3
  43.3 45.3 all-gather.5
  113.1 41.6 reduce-scatter.2
  168.6 26.4 reduce-scatter.4
